TPU v7x, 512 devices: a whole 4x4x16 slice. The times are simulated.
512 devices in a mesh: seq: 128 (over z, x, core), doc: 4 (over y).
Axes of the slice: x: 4, y: 4, z: 16, core: 2. Of those that a mesh axis runs over, the one named last changes fastest.
Arguments:
- block_input: bfloat16 [4, 16384, 2048], P('doc', 'seq'), may hold values from -6 to 6
- state_cotangent: bfloat16 [4, 16384, 2048], P('doc', 'seq'), may hold values from -24 to 24
- recur_weight: bfloat16 [2048, 256], P('seq'), may hold values from -0.375 to 0.375
- input_weight: bfloat16 [2048, 256], P('seq'), may hold values from -0.375 to 0.375
- gate_bias: float32 [2, 2048], replicated, may hold values from -4 to 4
- conv_taps: float32 [4, 2048], replicated, may hold values from -3 to 3
- conv_bias: float32 [2048], replicated, may hold values from -3 to 3
- decay_param: float32 [2048], replicated, may hold values from 2 to 20
Outputs:
- input_grad: bfloat16 [4, 16384, 2048], P('doc', 'seq')
- recur_weight_grad: float32 [2048, 256], P('seq')
- input_weight_grad: float32 [2048, 256], P('seq')
- channel_grads: float32 [8, 2048], replicated
All inputs are finite; a program needn't handle non-finite values.
Results may differ from a plain program's by a relative error of at most 0.008.
Values may be sent and summed in bfloat16 or wider, within the bound.
No kernel may reach another device: no remote copies, remote signals or barrier semaphores. Data moves between devices by JAX's collectives and lax.ppermute only.
A program may use at most 128 MiB of HBM per device.

v0:
```python
import math

import jax
import jax.numpy as jnp
from jax import lax
from jax.sharding import PartitionSpec as P

QFLOOR = 0.001


def passed_along(value, axis, steps):
    count = lax.axis_size(axis)
    leading, last = (max(0, -steps), min(count, count - steps))
    return lax.ppermute(value, axis, [(source, source + steps) for source in range(leading, last)])


def entering(shard, axis, combine, identity, reverse):
    peers, mine = (lax.axis_size(axis), lax.axis_index(axis))
    everything = jax.tree.map(lambda part: lax.all_gather(part, axis), shard)
    start = jax.tree.map(
        lambda part, zero: jnp.broadcast_to(jnp.asarray(zero, part.dtype), part.shape),
        shard,
        identity,
    )

    def turn(k, before):
        at = peers - 1 - k if reverse else k
        reached = at > mine if reverse else at < mine
        new = combine(before, jax.tree.map(lambda part: part[at], everything))
        return jax.tree.map(lambda a, b: jnp.where(reached, a, b), new, before)

    return lax.fori_loop(0, peers, turn, start)


def chain(earlier, later):
    return (earlier[0] * later[0], later[0] * earlier[1] + later[1])


def tap_sum(taps, padded, offset, steps):
    total = taps[0][None, :] * padded[offset : offset + steps]
    for k in range(1, 4):
        total = total + taps[k][None, :] * padded[offset - k : offset - k + steps]
    return total


def blocked_scan(mults, values, reverse):
    steps = mults.shape[0]
    width = mults.shape[1]
    length = math.gcd(steps, 16)
    count = steps // length
    mult_blocks = mults.reshape(count, length, width)
    value_blocks = values.reshape(count, length, width)
    order = range(length - 1, -1, -1) if reverse else range(length)
    running = jnp.ones((count, width), jnp.float32)
    summed = jnp.zeros((count, width), jnp.float32)
    prods = [None] * length
    sums = [None] * length
    for j in order:
        factor = mult_blocks[:, j]
        running = running * factor
        summed = factor * summed + value_blocks[:, j]
        prods[j] = running
        sums[j] = summed
    inner_p = jnp.stack(prods, axis=1)
    inner_h = jnp.stack(sums, axis=1)
    edge = 0 if reverse else length - 1
    block_p = inner_p[:, edge]
    block_h = inner_h[:, edge]

    def advance(carry, pair):
        new_carry = (pair[0] * carry[0], pair[0] * carry[1] + pair[1])
        return (new_carry, carry)

    start = (jnp.ones((width,), jnp.float32), jnp.zeros((width,), jnp.float32))
    _, (before_p, before_h) = lax.scan(advance, start, (block_p, block_h), reverse=reverse)
    cumulative = (inner_p * before_p[:, None, :]).reshape(steps, width)
    local = (inner_h + inner_p * before_h[:, None, :]).reshape(steps, width)
    return (cumulative, local)


def per_device(
    block_input,
    state_cotangent,
    recur_weight,
    input_weight,
    gate_bias,
    conv_taps,
    conv_bias,
    decay_param,
):
    xin = block_input[0]
    steps = xin.shape[0]
    width = xin.shape[1]
    block = recur_weight.shape[1]
    nblk = width // block
    prior = passed_along(xin[-3:], "seq", 1)
    padded = jnp.concatenate([prior, xin], axis=0).astype(jnp.float32)
    conv_out = (conv_bias[None, :] + tap_sum(conv_taps, padded, 3, steps)).astype(jnp.bfloat16)
    full_r, full_i = (
        lax.all_gather(recur_weight, "seq", axis=0, tiled=True),
        lax.all_gather(input_weight, "seq", axis=0, tiled=True),
    )
    w_recur = full_r.reshape(nblk, block, block)
    w_input = full_i.reshape(nblk, block, block)
    conv_blocks = conv_out.reshape(steps, nblk, block)
    pre_r = jnp.einsum(
        "tnk,nkj->tnj", conv_blocks, w_recur, preferred_element_type=jnp.float32
    ).reshape(steps, width)
    pre_i = jnp.einsum(
        "tnk,nkj->tnj", conv_blocks, w_input, preferred_element_type=jnp.float32
    ).reshape(steps, width)
    rgate = jax.nn.sigmoid(pre_r + gate_bias[0][None, :])
    igate = jax.nn.sigmoid(pre_i + gate_bias[1][None, :])
    rate = jax.nn.softplus(-decay_param)
    log_a = -8.0 * rgate * rate[None, :]
    decay = jnp.exp(log_a)
    qvalue = -jnp.expm1(2.0 * log_a)
    mult = jnp.sqrt(qvalue)
    conv_v = conv_out.astype(jnp.float32)
    normed = conv_v * igate * mult
    cum_a, local_h = blocked_scan(decay, normed, False)
    a_next = jnp.concatenate([decay[1:], jnp.ones((1, width), jnp.float32)], axis=0)
    dstate = state_cotangent[0].astype(jnp.float32)
    cum_m, local_g = blocked_scan(a_next, dstate, True)
    total = cum_a[-1]
    ending = local_h[-1]
    starting = decay[0] * local_g[0]
    ones = jnp.ones((width,), jnp.float32)
    zeros = jnp.zeros((width,), jnp.float32)
    incoming = entering((total, ending), "seq", chain, (ones, zeros), False)[1]
    carry = entering((total, starting), "seq", chain, (ones, zeros), True)[1]
    hstates = local_h + cum_a * incoming[None, :]
    h_prev = jnp.concatenate([incoming[None, :], hstates[:-1]], axis=0)
    gvals = local_g + cum_m * carry[None, :]
    grad_log_a = gvals * decay * h_prev - gvals * conv_v * igate * decay * decay / jnp.sqrt(
        jnp.maximum(qvalue, QFLOOR)
    )
    gpr = (grad_log_a * (-8.0 * rate[None, :]) * rgate * (1.0 - rgate)).astype(jnp.bfloat16)
    gpi = (gvals * conv_v * mult * igate * (1.0 - igate)).astype(jnp.bfloat16)
    gpr_blocks = gpr.reshape(steps, nblk, block)
    gpi_blocks = gpi.reshape(steps, nblk, block)
    grad_conv = gvals * igate * mult
    grad_conv = grad_conv + jnp.einsum(
        "tnj,nkj->tnk", gpr_blocks, w_recur, preferred_element_type=jnp.float32
    ).reshape(steps, width)
    grad_conv = grad_conv + jnp.einsum(
        "tnj,nkj->tnk", gpi_blocks, w_input, preferred_element_type=jnp.float32
    ).reshape(steps, width)
    following = passed_along(grad_conv[:3], "seq", -1)
    dpad = jnp.concatenate([grad_conv, following], axis=0)
    xgrad = conv_taps[0][None, :] * dpad[0:steps]
    for k in range(1, 4):
        xgrad = xgrad + conv_taps[k][None, :] * dpad[k : k + steps]
    input_grad = xgrad.astype(jnp.bfloat16)[None]
    local_r = jnp.einsum(
        "tnk,tnj->nkj", conv_blocks, gpr_blocks, preferred_element_type=jnp.float32
    ).reshape(width, block)
    local_i = jnp.einsum(
        "tnk,tnj->nkj", conv_blocks, gpi_blocks, preferred_element_type=jnp.float32
    ).reshape(width, block)
    rows = [jnp.sum(grad_conv * padded[3 - k : 3 - k + steps], axis=0) for k in range(4)]
    rows.append(jnp.sum(grad_conv, axis=0))
    rows.append(jnp.sum(gpr.astype(jnp.float32), axis=0))
    rows.append(jnp.sum(gpi.astype(jnp.float32), axis=0))
    rows.append(jnp.sum(grad_log_a * 8.0 * rgate, axis=0) * jax.nn.sigmoid(-decay_param))
    channel_grads = lax.psum(jnp.stack(rows, axis=0), ("seq", "doc"))
    share_r, share_i = (
        lax.psum_scatter(local_r, "seq", scatter_dimension=0, tiled=True),
        lax.psum_scatter(local_i, "seq", scatter_dimension=0, tiled=True),
    )
    recur_grad, input_grad_w = lax.psum((share_r, share_i), "doc")
    return (input_grad, recur_grad, input_grad_w, channel_grads)


def solution(mesh):
    in_specs = (
        P("doc", "seq", None),
        P("doc", "seq", None),
        P("seq", None),
        P("seq", None),
        P(),
        P(),
        P(),
        P(),
    )
    out_specs = (P("doc", "seq", None), P("seq", None), P("seq", None), P())
    return jax.shard_map(
        per_device, mesh=mesh, in_specs=in_specs, out_specs=out_specs, check_vma=False
    )
```

profile of v0, /device:TPU:1, one launch (start us, length us, event | category | flops | bytes accessed | tf_op | source)
XLA Modules:
  0.0 1876.2 jit_solution(11166447204905749308)
XLA Ops:
  9.5 4.5 collective-permute-start
  16.5 3.6 collective-permute-done
  20.6 2.5 add_convert_fusion
  23.1 124.4 %all-gather.9.cloned.1.call-done = bf16[2048,256]{1,0:T(8,128)(2,1)} async-done(((bf16[16,256]{1,0:T(8,128)(2,1)}), bf16[2048,256]{1,0:T(8,128)(2,1)}) %all-gather.9.cloned.1.call-update) | async-done | bytes 1048592 | tf_op jit(solution)/shard_map/all_gather | solution.py:100
  147.5 2.6 convolution_bitcast_fusion.3
  151.6 125.2 %all-gather.11.cloned.1.call-done = bf16[2048,256]{1,0:T(8,128)(2,1)} async-done(((bf16[16,256]{1,0:T(8,128)(2,1)}), bf16[2048,256]{1,0:T(8,128)(2,1)}) %all-gather.11.cloned.1.call-update) | async-done | bytes 1048592 | tf_op jit(solution)/shard_map/all_gather | solution.py:101
  276.8 2.7 convolution_bitcast_fusion.2
  279.5 2.6 copy.252
  282.2 6.0 multiply_exponential_fusion
  299.7 2.0 fusion.31
  304.3 46.8 %while.68 = (s32[]{:T(128)}, f32[2048]{0:T(1024)}, f32[2048]{0:T(1024)}, f32[8,2048]{1,0:T(8,128)}, f32[8,2048]{1,0:T(8,128)}, /*index=5*/f32[8,2048]{1,0:T(8,12...) while((s32[]{:T(128)}, f32[2048]{0:T(1024)}, f32[2048]{0:T(1024)}, f32[8,2048]{1,0:T(8,128)}, ...), condition=%wide.region_1.2_spmd.clone, body=%wide.region_0.1_spmd.clone.sunk | while | flops 10244 | bytes 131207 | solution.py:75
  351.2 1.7 constant_dynamic-update-slice_fusion.30
  373.3 2.7 broadcast_multiply_fusion.1
  377.6 2.6 copy.273
  380.2 2.5 fusion.12
  391.3 2.6 copy.253
  393.8 5.9 fusion.94
  410.7 31.2 %while.69 = (s32[]{:T(128)}, f32[2048]{0:T(1024)S(1)}, f32[2048]{0:T(1024)S(1)}, f32[8,2048]{1,0:T(8,128)}, f32[8,2048]{1,0:T(8,128)}, /*index=5*/f32[8,2048]{1,0:T(8,128)}, f32[8,2048]{1,0:T(8,128)}, s32[]{:T(128)}, s32[]{:T(128)}) while((s32[]{:T(128)}, f32[2048]{0:T(1024)S(1)}, f32[2048]{0:T(1024)S(1)}, f32[8,2048]{1,0:T(8,128)}, ...), condition=%wide.region_3.4_spmd.clone, body=%wide.region_2.3_spmd.clone.sunk | while | flops 10243 | bytes 131187 | solution.py:75
  444.6 2.4 broadcast_multiply_fusion
  449.3 1.8 copy.248
  452.5 2.8 copy.274
  455.3 2.5 copy.349
  457.8 2.6 copy.350
  461.9 47.3 %all-gather.15.cloned.1.call-done = f32[128,1,2048]{2,1,0:T(1,128)} async-done(((f32[1,1,2048]{2,1,0:T(1,128)}), f32[128,1,2048]{2,1,0:T(1,128)}) %all-gather.15.cloned.1.call-update) | async-done | bytes 1048592 | tf_op jit(solution)/shard_map/all_gather | solution.py:19
  509.2 2.5 copy.706
  511.7 127.2 %all-gather.13.cloned.1.call-done = f32[128,1,2048]{2,1,0:T(1,128)} async-done(((f32[1,1,2048]{2,1,0:T(1,128)}), f32[128,1,2048]{2,1,0:T(1,128)}) %all-gather.13.cloned.1.call-update) | async-done | bytes 1048592 | tf_op jit(solution)/shard_map/all_gather | solution.py:19
  640.5 116.2 %while.70 = (s32[]{:T(128)}, f32[2048]{0:T(1024)S(1)}, s32[]{:T(128)}, f32[128,2048]{1,0:T(8,128)S(1)}, f32[128,2048]{1,0:T(8,128)}, /*index=5*/s32[]{:T(128)}, s32[]{:T(128)}, s32[]{:T(128)}, s32[]{:T(128)}) while((s32[]{:T(128)}, f32[2048]{0:T(1024)S(1)}, s32[]{:T(128)}, f32[128,2048]{1,0:T(8,128)S(1)}, f32[128,2048]{1,0:T(8,128)}, ...), condition=%wide.region_5.6_spmd.clone, body=%wide.region_4.5_spmd.clone.sunk | while | flops 8200 | bytes 65699 | solution.py:32
  756.8 11.4 all-gather.17.cloned.1.call-done
  768.2 2.6 copy.705
  770.8 114.9 %while.71 = (s32[]{:T(128)}, f32[2048]{0:T(1024)S(1)}, s32[]{:T(128)}, f32[128,2048]{1,0:T(8,128)S(1)}, f32[128,2048]{1,0:T(8,128)}, /*index=5*/s32[]{:T(128)}, s32[]{:T(128)}) while((s32[]{:T(128)}, f32[2048]{0:T(1024)S(1)}, s32[]{:T(128)}, f32[128,2048]{1,0:T(8,128)S(1)}, f32[128,2048]{1,0:T(8,128)}, /*index=5*/s32[]{:T(128)}, ...), condition=%wide.region_7.8_spmd.clone, body=%wide.region_6.7_spmd.clone.sunk | while | flops 8196 | bytes 65637 | solution.py:32
  887.1 2.0 multiply_add_fusion.2
  889.6 6.8 multiply_reduce_fusion
  896.4 5.2 convert_reduce_fusion.1
  901.6 1.7 fusion.97
  903.4 3.0 fusion.98
  906.8 2.6 copy.351
  910.7 2.9 convolution_bitcast_fusion.1
  913.6 2.5 copy.279
  916.1 5.6 fusion.25
  921.8 2.6 copy.281
  924.3 5.2 multiply_reduce_fusion.1
  931.2 2.2 collective-permute-start.1
  934.1 2.3 collective-permute-done.1
  936.8 3.0 fusion.32
  940.9 208.1 %reduce-scatter.3.cloned.1.call-done = f32[16,256]{1,0:T(8,128)} async-done(((f32[2048,256]{1,0:T(8,128)}), f32[16,256]{1,0:T(8,128)}) %reduce-scatter.3.cloned.1.call-update) | async-done | bytes 16400 | tf_op jit(solution)/shard_map/reduce_scatter | solution.py:168
  1149.0 263.2 %reduce-scatter.5.cloned.1.call-done = f32[16,256]{1,0:T(8,128)} async-done(((f32[2048,256]{1,0:T(8,128)}), f32[16,256]{1,0:T(8,128)}) %reduce-scatter.5.cloned.1.call-update) | async-done | bytes 16400 | tf_op jit(solution)/shard_map/reduce_scatter | solution.py:169
  1412.2 15.2 all-reduce.1
  1427.4 440.5 %all-reduce.4.cloned.1.call-done = f32[8,2048]{1,0:T(8,128)} async-done(((f32[8,2048]{1,0:T(8,128)}), f32[8,2048]{1,0:T(8,128)}) %all-reduce.4.cloned.1.call-update) | async-done | bytes 65552 | tf_op jit(solution)/shard_map/psum | solution.py:166
  (838 shorter events, 379.7 us)
Async XLA Ops:
  7.2 6.9 copy-start.69
  7.2 7.0 copy-start.72
  7.2 7.7 copy-start.18
  7.2 140.3 %all-gather.9.cloned.1.call-start = ((), (), s32[]{:S(2)}) async-start(), calls=%async_computation.2 | async-start | bytes 1056768 | tf_op jit(solution)/shard_map/all_gather | solution.py:100
  7.9 8.5 copy-start.67
  7.9 268.9 %all-gather.11.cloned.1.call-start = ((), (), s32[]{:S(2)}) async-start(), calls=%async_computation.3 | async-start | bytes 1056768 | tf_op jit(solution)/shard_map/all_gather | solution.py:101
  9.5 10.6 collective-permute-start
  14.1 495.1 %all-gather.15.cloned.1.call-start = ((), (), s32[]{:S(2)}) async-start(), calls=%async_computation.8 | async-start | bytes 1056768 | tf_op jit(solution)/shard_map/all_gather | solution.py:19
  14.2 268.0 %copy-start.49 = (f32[1,2048]{1,0:T(1,128)}, f32[1,2048]{1,0:T(1,128)S(1)}, u32[]{:S(2)}) copy-start(f32[1,2048]{1,0:T(1,128)S(1)} %get-tuple-element.711) | copy-start | bytes 24580
  14.2 268.0 %copy-start.51 = (f32[1,2048]{1,0:T(1,128)}, f32[1,2048]{1,0:T(1,128)S(1)}, u32[]{:S(2)}) copy-start(f32[1,2048]{1,0:T(1,128)S(1)} %get-tuple-element.712) | copy-start | bytes 24580
  14.2 268.0 %copy-start.53 = (f32[1,2048]{1,0:T(1,128)}, f32[1,2048]{1,0:T(1,128)S(1)}, u32[]{:S(2)}) copy-start(f32[1,2048]{1,0:T(1,128)S(1)} %get-tuple-element.713) | copy-start | bytes 24580
  14.2 268.0 %copy-start.55 = (f32[1,2048]{1,0:T(1,128)}, f32[1,2048]{1,0:T(1,128)S(1)}, u32[]{:S(2)}) copy-start(f32[1,2048]{1,0:T(1,128)S(1)} %get-tuple-element.714) | copy-start | bytes 24580
  14.8 267.3 %copy-start.63 = (f32[1,2048]{1,0:T(1,128)}, f32[1,2048]{1,0:T(1,128)S(1)}, u32[]{:S(2)}) copy-start(f32[1,2048]{1,0:T(1,128)S(1)} %get-tuple-element.715) | copy-start | bytes 24580
  14.9 284.9 %copy-start.57 = (f32[1,2048]{1,0:T(1,128)}, f32[1,2048]{1,0:T(1,128)S(1)}, u32[]{:S(2)}) copy-start(f32[1,2048]{1,0:T(1,128)S(1)} %get-tuple-element.716) | copy-start | bytes 24580
  16.5 283.2 %copy-start.47 = (f32[2048]{0:T(1024)}, f32[2048]{0:T(1024)S(1)}, u32[]{:S(2)}) copy-start(f32[2048]{0:T(1024)S(1)} %fusion.89) | copy-start | bytes 24580
  23.1 124.4 %copy-start.3 = (bf16[128,2048]{0,1:T(8,128)(2,1)}, bf16[128,2048]{0,1:T(8,128)(2,1)S(1)}, u32[]{:S(2)}) copy-start(bf16[128,2048]{0,1:T(8,128)(2,1)S(1)} %add_convert_fusion) | copy-start | bytes 1572868
  151.6 130.6 %copy-start = (f32[128,8,256]{0,2,1:T(8,128)}, f32[128,8,256]{0,2,1:T(8,128)S(1)}, u32[]{:S(2)}) copy-start(f32[128,8,256]{0,2,1:T(8,128)S(1)} %copy.211) | copy-start | bytes 3145732
  351.2 14.2 copy-start.44
  351.2 14.8 copy-start.46
  351.2 15.4 copy-start.27
  351.2 15.4 copy-start.42
  351.2 15.4 copy-start.45
  351.2 17.4 copy-start.25
  351.2 17.4 copy-start.41
  351.2 17.4 copy-start.43
  351.2 19.4 %copy-start.21 = (f32[8,1,2048]{2,1,0:T(1,128)S(1)}, f32[8,1,2048]{2,1,0:T(1,128)}, u32[]{:S(2)}) copy-start(f32[8,1,2048]{2,1,0:T(1,128)} %get-tuple-element.681) | copy-start | bytes 196612
  351.2 19.4 %copy-start.40 = (f32[8,1,2048]{2,0,1:T(8,128)S(1)}, f32[8,1,2048]{2,0,1:T(8,128)}, u32[]{:S(2)}) copy-start(f32[8,1,2048]{2,0,1:T(8,128)} %get-tuple-element.624) | copy-start | bytes 196612
  354.5 18.1 copy-start.23
  354.5 18.8 %copy-start.59 = (f32[8,2048]{1,0:T(8,128)S(1)}, f32[8,2048]{1,0:T(8,128)}, u32[]{:S(2)}) copy-start(f32[8,2048]{1,0:T(8,128)} %get-tuple-element.411) | copy-start | bytes 196612
  354.5 18.8 %copy-start.60 = (f32[8,2048]{1,0:T(8,128)S(1)}, f32[8,2048]{1,0:T(8,128)}, u32[]{:S(2)}) copy-start(f32[8,2048]{1,0:T(8,128)} %get-tuple-element.410) | copy-start | bytes 196612
  382.7 256.2 %all-gather.13.cloned.1.call-start = ((), (), s32[]{:S(2)}) async-start(), calls=%async_computation.7 | async-start | bytes 1056768 | tf_op jit(solution)/shard_map/all_gather | solution.py:19
  405.1 5.6 copy-start.61
  405.1 5.6 copy-start.62
  449.2 318.9 %all-gather.17.cloned.1.call-start = ((), (), s32[]{:S(2)}) async-start(), calls=%async_computation.9 | async-start | bytes 1056768 | tf_op jit(solution)/shard_map/all_gather | solution.py:19
  461.8 687.2 %reduce-scatter.3.cloned.1.call-start = ((), (), s32[]{:S(2)}) async-start(), calls=%async_computation.4 | async-start | bytes 2113536 | tf_op jit(solution)/shard_map/reduce_scatter | solution.py:168
  768.1 121.0 %copy-start.52 = (f32[1,2048]{1,0:T(1,128)S(1)}, f32[1,2048]{1,0:T(1,128)}, u32[]{:S(2)}) copy-start(f32[1,2048]{1,0:T(1,128)} %copy-done.51) | copy-start | bytes 24580
  768.1 121.0 %copy-start.54 = (f32[1,2048]{1,0:T(1,128)S(1)}, f32[1,2048]{1,0:T(1,128)}, u32[]{:S(2)}) copy-start(f32[1,2048]{1,0:T(1,128)} %copy-done.53) | copy-start | bytes 24580
  768.2 121.0 %copy-start.56 = (f32[1,2048]{1,0:T(1,128)S(1)}, f32[1,2048]{1,0:T(1,128)}, u32[]{:S(2)}) copy-start(f32[1,2048]{1,0:T(1,128)} %copy-done.55) | copy-start | bytes 24580
  768.2 121.0 %copy-start.58 = (f32[1,2048]{1,0:T(1,128)S(1)}, f32[1,2048]{1,0:T(1,128)}, u32[]{:S(2)}) copy-start(f32[1,2048]{1,0:T(1,128)} %copy-done.57) | copy-start | bytes 24580
  768.2 121.0 %copy-start.64 = (f32[1,2048]{1,0:T(1,128)S(1)}, f32[1,2048]{1,0:T(1,128)}, u32[]{:S(2)}) copy-start(f32[1,2048]{1,0:T(1,128)} %copy-done.63) | copy-start | bytes 24580
  768.2 121.0 %copy-start.66 = (f32[2048]{0:T(1024)S(1)}, f32[2048]{0:T(1024)}, u32[]{:S(2)}) copy-start(f32[2048]{0:T(1024)} %param.22) | copy-start | bytes 24580
  896.4 5.2 copy-start.5
  896.4 5.2 copy-start.4
  903.4 508.8 %reduce-scatter.5.cloned.1.call-start = ((), (), s32[]{:S(2)}) async-start(), calls=%async_computation.5 | async-start | bytes 2113536 | tf_op jit(solution)/shard_map/reduce_scatter | solution.py:169
  906.4 961.5 %all-reduce.4.cloned.1.call-start = ((), (), s32[]{:S(2)}) async-start(), calls=%async_computation.6 | async-start | bytes 131072 | tf_op jit(solution)/shard_map/psum | solution.py:166
  924.3 9.0 copy-start.68
  929.5 7.3 copy-start.10
  931.2 5.2 collective-permute-start.1
  (35 other events, 84.1 us)
Sparse Core Ops, SparseCore 0:
  11.0 136.4 all-gather.8
  150.5 126.3 all-gather.10
  382.8 126.3 all-gather.14
  512.6 126.3 all-gather.12
  641.8 126.3 all-gather.16
  903.5 245.4 reduce-scatter.2
  1153.6 258.5 reduce-scatter.4
  1418.2 449.6 all-reduce.3
where the time goes:
time: 1890 us; the launch traced here: 1880 us
  waiting for transfers between devices  1350 us (71%)
  local copies, waits for them, and re-layouts  366 us (19%)
  other arithmetic  90.2 us (5%)
    psum x1, waiting for transfers between devices, per_device(): channel_grads = lax.psum(jnp.stack(rows, axis=0), ('seq', 'doc'))  441 us
    reduce_scatter x1, waiting for transfers between devices, per_device(): lax.psum_scatter(local_i, 'seq', scatter_dimension=0, tiled=True)  263 us
    dynamic_slice x256, local copies, waits for them, and re-layouts, turn(): new = combine(before, jax.tree.map(lambda part: part[at], everything))  220 us
    reduce_scatter x1, waiting for transfers between devices, per_device(): lax.psum_scatter(local_r, 'seq', scatter_dimension=0, tiled=True)  208 us
    all_gather x3, waiting for transfers between devices, entering(): everything = jax.tree.map(lambda part: lax.all_gather(part, axis), shard)  186 us
    all_gather x1, waiting for transfers between devices, per_device(): lax.all_gather(input_weight, 'seq', axis=0, tiled=True)  125 us
    all_gather x1, waiting for transfers between devices, per_device(): lax.all_gather(recur_weight, 'seq', axis=0, tiled=True)  124 us
    dynamic_update_slice x32, local copies, waits for them, and re-layouts, blocked_scan(): lax.scan(advance, start, (block_p, block_h), reverse=reverse)  48 us
  transfers between devices with their start and end apart: 10, of which 10 were waited for; matrix products, arithmetic and copies ran while one was open for 13% of the time, Pallas kernels for 0%

commit v1 on v0

v1 whole, which is shorter than its diff:
```python
import functools

import jax
import jax.numpy as jnp
from jax import lax
from jax.experimental import pallas as pl
from jax.experimental.pallas import tpu as pltpu
from jax.sharding import Mesh
from jax.sharding import PartitionSpec as P

QFLOOR = 0.001
SEGS = 8
SPAN = 16
ROWS = SEGS * SPAN
F32 = jnp.float32
BF16 = jnp.bfloat16


def dot(a, b, contract=((1,), (0,))):
    return lax.dot_general(a, b, (contract, ((), ())), preferred_element_type=F32)


def shuffle_matrix():
    row = lax.broadcasted_iota(jnp.int32, (ROWS, ROWS), 0)
    col = lax.broadcasted_iota(jnp.int32, (ROWS, ROWS), 1)
    return jnp.where(col == (row % SEGS) * SPAN + row // SEGS, 1.0, 0.0).astype(BF16)


def by_step(buf_ref, shuffle, first):
    tiles = [buf_ref[s, pl.ds(first, SPAN), :] for s in range(SEGS)]
    return dot(shuffle, jnp.concatenate(tiles, axis=0))


def load_weights(buf_ref, w_ref, steps):
    block = w_ref.shape[0]
    share = block // 2 // SEGS
    for p in range(2):
        for s in range(SEGS):
            row = p * (block // 2) + s * share
            for w in range(2):
                at = 2 * steps + (p * 2 + w) * share
                w_ref[row : row + share, w * block : (w + 1) * block] = buf_ref[s, at : at + share, :]


def one_minus_exp(x):
    series = x * (1.0 - x * (1 / 2) * (1.0 - x * (1 / 3) * (1.0 - x * (1 / 4) * (1.0 - x * (1 / 5) * (1.0 - x * (1 / 6))))))
    return jnp.where(x < 0.25, series, 1.0 - jnp.exp(-x))


def block_params(at_ref, bias_ref, taps_ref, cbias_ref, decay_ref, block):
    lanes = pl.ds(pl.multiple_of(at_ref[1] * block, block), block)
    rate = jax.nn.softplus(-decay_ref[:, lanes])
    return bias_ref[:, lanes], taps_ref[:, lanes], cbias_ref[:, lanes], rate


def forward_kernel(
    steps, at_ref, buf_ref, halo_ref, bias_ref, taps_ref, cbias_ref, decay_ref,
    conv_ref, r_ref, i_ref, a_ref, m_ref, xpad_ref, seg_ref, sum_ref, w_ref,
):
    block = w_ref.shape[0]
    shuffle = shuffle_matrix()
    load_weights(buf_ref, w_ref, steps)
    bias, taps, cbias, rate = block_params(at_ref, bias_ref, taps_ref, cbias_ref, decay_ref, block)
    last = by_step(buf_ref, shuffle, steps - SPAN)[ROWS - 3 * SEGS :]
    halo = jnp.where(at_ref[0] > 0, halo_ref[...].astype(F32), 0.0)
    for k in range(3):
        rows = last[k * SEGS : (k + 1) * SEGS]
        xpad_ref[k * SEGS : (k + 1) * SEGS, :] = jnp.concatenate(
            [halo[SPAN - 3 + k : SPAN - 2 + k], rows[: SEGS - 1]], axis=0
        )

    def chunk(c, carry):
        prod, state, start = carry
        base = pl.multiple_of(c * ROWS, ROWS)
        first = pl.multiple_of(c * SPAN, SPAN)
        x = by_step(buf_ref, shuffle, first)
        d = by_step(buf_ref, shuffle, steps + first)
        xpad_ref[pl.ds(base + 3 * SEGS, ROWS), :] = x
        conv = cbias + taps[0:1] * x
        for k in range(1, 4):
            conv = conv + taps[k : k + 1] * xpad_ref[pl.ds(base + (3 - k) * SEGS, ROWS), :]
        conv_b = conv.astype(BF16)
        conv_ref[pl.ds(base, ROWS), :] = conv_b
        conv_v = conv_b.astype(F32)
        pre = dot(conv_b, w_ref[...])
        r = jax.nn.sigmoid(pre[:, :block] + bias[0:1])
        i = jax.nn.sigmoid(pre[:, block:] + bias[1:2])
        decay = 8.0 * r * rate
        a = jnp.exp(-decay)
        m = jnp.sqrt(one_minus_exp(2.0 * decay))
        r_ref[pl.ds(base, ROWS), :] = r
        i_ref[pl.ds(base, ROWS), :] = i
        a_ref[pl.ds(base, ROWS), :] = a
        m_ref[pl.ds(base, ROWS), :] = m
        normed = conv_v * i * m
        for s in range(SPAN):
            rows = slice(s * SEGS, (s + 1) * SEGS)
            prod = prod * a[rows]
            state = a[rows] * state + normed[rows]
            start = start + prod * d[rows]
        return prod, state, start

    zero = jnp.zeros((SEGS, block), F32)
    prod, state, start = lax.fori_loop(0, steps // SPAN, chunk, (zero + 1.0, zero, zero))
    seg_ref[0:SEGS, :] = prod
    seg_ref[SEGS : 2 * SEGS, :] = state
    seg_ref[2 * SEGS : 3 * SEGS, :] = start
    whole, end, begin = prod[0:1], state[0:1], start[SEGS - 1 : SEGS]
    for s in range(1, SEGS):
        whole = whole * prod[s : s + 1]
        end = prod[s : s + 1] * end + state[s : s + 1]
        back = SEGS - 1 - s
        begin = start[back : back + 1] + prod[back : back + 1] * begin
    sum_ref[...] = jnp.concatenate([whole, end, begin, begin], axis=0)


def backward_kernel(
    steps, shards, at_ref, buf_ref, conv_ref, r_ref, i_ref, a_ref, m_ref, xpad_ref, seg_ref, all_ref, w_ref,
    bias_ref, taps_ref, cbias_ref, decay_ref,
    ig_ref, wg_ref, rows_ref, edge_ref,
    prev_ref, gates_ref,
):
    block = w_ref.shape[0]
    shuffle = shuffle_matrix()
    _, taps, _, rate = block_params(at_ref, bias_ref, taps_ref, cbias_ref, decay_ref, block)
    mine = at_ref[0]
    entering = jnp.zeros((1, block), F32)
    carry_in = jnp.zeros((1, block), F32)
    for k in range(shards):
        part = all_ref[k]
        entering = jnp.where(k < mine, part[0:1] * entering + part[1:2], entering)
        back = shards - 1 - k
        part = all_ref[back]
        carry_in = jnp.where(back > mine, part[0:1] * carry_in + part[2:3], carry_in)
    heads, tails = [entering], [carry_in]
    for s in range(SEGS - 1):
        heads.append(seg_ref[s : s + 1] * heads[-1] + seg_ref[SEGS + s : SEGS + s + 1])
        back = SEGS - 1 - s
        tails.append(seg_ref[2 * SEGS + back : 2 * SEGS + back + 1] + seg_ref[back : back + 1] * tails[-1])
    state = jnp.concatenate(heads, axis=0)
    carry = jnp.concatenate(tails[::-1], axis=0)

    def ahead(c, state):
        base = pl.multiple_of(c * ROWS, ROWS)
        rows = pl.ds(base, ROWS)
        a = a_ref[rows, :]
        normed = conv_ref[rows, :].astype(F32) * i_ref[rows, :] * m_ref[rows, :]
        before = []
        for s in range(SPAN):
            at = slice(s * SEGS, (s + 1) * SEGS)
            before.append(state)
            state = a[at] * state + normed[at]
        prev_ref[rows, :] = jnp.concatenate(before, axis=0)
        return state

    lax.fori_loop(0, steps // SPAN, ahead, state)

    def put(first, xgrad):
        tiles = dot(shuffle, xgrad.astype(BF16), ((0,), (0,))).astype(BF16)
        for s in range(SEGS):
            ig_ref[s, pl.ds(first, SPAN), :] = tiles[s * SPAN : (s + 1) * SPAN]

    def folded(v):
        return jnp.sum(v.reshape(SPAN, SEGS, block), axis=0)

    def chunk(c, carry, after, totals):
        base = pl.multiple_of(c * ROWS, ROWS)
        first = pl.multiple_of(c * SPAN, SPAN)
        rows = pl.ds(base, ROWS)
        d = by_step(buf_ref, shuffle, steps + first)
        a = a_ref[rows, :]
        held = [None] * SPAN
        for s in range(SPAN - 1, -1, -1):
            at = slice(s * SEGS, (s + 1) * SEGS)
            held[s] = d[at] + carry
            carry = a[at] * held[s]
        g = jnp.concatenate(held, axis=0)
        r, i, m = r_ref[rows, :], i_ref[rows, :], m_ref[rows, :]
        conv_v = conv_ref[rows, :].astype(F32)
        gi = g * i
        ga = g * a
        gla = ga * prev_ref[rows, :] - gi * conv_v * a * a * lax.rsqrt(jnp.maximum(m * m, QFLOOR))
        glr = gla * 8.0 * r
        gpr = (glr * (r - 1.0) * rate).astype(BF16)
        gim = gi * m
        gpi = (gim * conv_v * (1.0 - i)).astype(BF16)
        both = jnp.concatenate([gpr, gpi], axis=1)
        gates_ref[rows, :] = both
        gc = gim + dot(both, w_ref[...], ((1,), (1,)))
        padded = jnp.concatenate([gc, after], axis=0)
        xgrad = taps[0:1] * gc
        for k in range(1, 4):
            xgrad = xgrad + taps[k : k + 1] * padded[k * SEGS : k * SEGS + ROWS]
        new = [folded(gc * xpad_ref[pl.ds(base + (3 - k) * SEGS, ROWS), :]) for k in range(4)]
        new += [folded(gc), folded(gpr.astype(F32)), folded(gpi.astype(F32)), folded(glr)]
        totals = tuple(t + n for t, n in zip(totals, new, strict=True))
        return carry, gc[: 3 * SEGS], totals, xgrad

    final = steps // SPAN - 1
    zero = jnp.zeros((SEGS, block), F32)
    carry, after, totals, ending = chunk(final, carry, jnp.zeros((3 * SEGS, block), F32), (zero,) * 8)

    def turn(k, held):
        c = final - 1 - k
        carry, after, totals = held
        carry, after, totals, xgrad = chunk(c, carry, after, totals)
        put(pl.multiple_of(c * SPAN, SPAN), xgrad)
        return carry, after, totals

    carry, after, totals = lax.fori_loop(0, final, turn, (carry, after, totals))
    none = jnp.zeros((1, block), F32)
    follow = [jnp.concatenate([after[k * SEGS + 1 : (k + 1) * SEGS], none], axis=0) for k in range(3)]
    cut = ROWS - 3 * SEGS
    late = [ending[cut + k * SEGS : cut + (k + 1) * SEGS] for k in range(3)]
    for k in range(3):
        for n in range(k + 1):
            late[k] = late[k] + taps[3 - k + n : 4 - k + n] * follow[n]
    put(final * SPAN, jnp.concatenate([ending[:cut]] + late, axis=0))
    edge_ref[...] = jnp.concatenate(
        [after[k * SEGS : k * SEGS + 1] for k in range(3)] + [none] + [v[SEGS - 1 :] for v in late] + [none], axis=0
    )
    scale = jax.nn.sigmoid(-decay_ref[:, pl.ds(pl.multiple_of(at_ref[1] * block, block), block)])
    sums = [jnp.sum(t, axis=0, keepdims=True) for t in totals]
    sums[7] = sums[7] * scale
    rows_ref[...] = jnp.concatenate(sums, axis=0)
    wg = dot(conv_ref[...], gates_ref[...], ((0,), (0,)))
    half = block // 2
    for s in range(SEGS):
        for w in range(2):
            for h in range(2):
                at = [p * half + s * 16 + h * 8 for p in range(2)]
                lanes = slice(w * block, (w + 1) * block)
                pair = jnp.concatenate([wg[k : k + 8, lanes] for k in at], axis=0)
                wg_ref[s * 4 + w * 2 + h] = pair.astype(BF16)


def split(v):
    high = v.astype(BF16)
    return high, (v - high.astype(F32)).astype(BF16)


def joined(high, low):
    return high.astype(F32) + low.astype(F32)


def per_device(
    shards, docs, block_input, state_cotangent, recur_weight, input_weight, gate_bias, conv_taps, conv_bias, decay_param
):
    steps, width = block_input.shape[1:]
    block = recur_weight.shape[1]
    share = recur_weight.shape[0]
    z, j = lax.axis_index("z"), lax.axis_index("j")
    at = jnp.stack([z, j]).astype(jnp.int32)
    params = (gate_bias, conv_taps, conv_bias[None], decay_param[None])

    weights = jnp.concatenate([recur_weight, input_weight], axis=0)
    weights = jnp.broadcast_to(weights[None], (shards, 2 * share, block))
    weights = lax.all_to_all(weights, "z", 0, 0).reshape(SEGS, 4 * share, block)
    by_block = [v[0].reshape(steps, SEGS, block).transpose(1, 0, 2) for v in (block_input, state_cotangent)]
    buf = lax.all_to_all(jnp.concatenate(by_block + [weights], axis=1), "j", 0, 0)
    halo = lax.ppermute(
        buf[SEGS - 1, steps - SPAN : steps], "z", [(k, k + 1) for k in range(shards - 1)]
    )

    total = SEGS * steps
    smem = pl.BlockSpec(memory_space=pltpu.SMEM)
    vmem = pl.BlockSpec(memory_space=pltpu.VMEM)
    shape = jax.ShapeDtypeStruct
    limit = pltpu.CompilerParams(vmem_limit_bytes=48 * 1024 * 1024)
    full = shape((total, block), F32)
    conv, r, i, a, m, xpad, seg, summary, w = pl.pallas_call(
        functools.partial(forward_kernel, steps),
        out_shape=(
            shape((total, block), BF16), full, full, full, full,
            shape((total + 3 * SEGS, block), F32), shape((3 * SEGS, block), F32),
            shape((4, block), F32), shape((block, 2 * block), BF16),
        ),
        in_specs=[smem] + [vmem] * 6,
        out_specs=(vmem,) * 9,
        compiler_params=limit,
        name="forward",
    )(at, buf, halo, *params)

    everyone = lax.all_to_all(jnp.broadcast_to(summary[None], (shards, 4, block)), "z", 0, 0)

    ig, wg, rows, edge = pl.pallas_call(
        functools.partial(backward_kernel, steps, shards),
        out_shape=(
            shape((SEGS, steps, block), BF16), shape((4 * SEGS, 16, block), BF16),
            shape((8, block), F32), shape((8, block), F32),
        ),
        in_specs=[smem] + [vmem] * 14,
        out_specs=(vmem,) * 4,
        scratch_shapes=[pltpu.VMEM((total, block), F32), pltpu.VMEM((total, 2 * block), BF16)],
        compiler_params=limit,
        name="backward",
    )(at, buf, conv, r, i, a, m, xpad, seg, everyone, w, *params)

    head = lax.ppermute(edge[0:3], "z", [(k + 1, k) for k in range(shards - 1)])
    taps = lax.dynamic_slice_in_dim(conv_taps, j * block, block, axis=1)
    late = []
    for k in range(3):
        row = edge[4 + k]
        for n in range(k + 1):
            row = row + taps[3 - k + n] * head[n]
        late.append(row)
    ig = ig.at[SEGS - 1, steps - 3 :].set(jnp.stack(late).astype(BF16))
    ig = lax.all_to_all(ig, "j", 0, 0)
    input_grad = ig.transpose(1, 0, 2).reshape(1, steps, width)

    quarter = block // docs
    pieces = split(rows.reshape(SEGS, docs, quarter).reshape(SEGS * docs, 1, quarter))
    packed = jnp.pad(jnp.concatenate(pieces, axis=2), ((0, 0), (0, 7), (0, block - 2 * quarter)))
    got = lax.all_to_all(jnp.concatenate([wg, packed], axis=1), ("j", "doc"), 0, 0)
    got = got.reshape(SEGS, docs, 24, block)
    wsum = jnp.sum(got[:, :, :16].astype(F32), axis=1).reshape(shards, 8, block)
    csum = jnp.sum(joined(got[:, :, 16, :quarter], got[:, :, 16, quarter : 2 * quarter]), axis=1)
    csum = jnp.broadcast_to(csum.reshape(1, 2, block), (shards, 2, block))
    got = lax.all_to_all(jnp.concatenate((wsum.astype(BF16),) + split(csum), axis=1), "z", 0, 0)
    wsum = jnp.sum(got[:, :8].astype(F32), axis=0)
    csum = jnp.sum(joined(got[:, 8:10], got[:, 10:12]), axis=0)
    send = jnp.broadcast_to(jnp.concatenate([wsum, csum], axis=0)[None], (SEGS * docs, 10, block))
    got = lax.all_to_all(send, ("j", "doc"), 0, 0).reshape(SEGS, docs, 10, block)
    wgrads = lax.dynamic_index_in_dim(got[:, :, :8], j, 0, keepdims=False).reshape(2, 2 * 8, block)
    channel_grads = got[:, :, 8:].reshape(SEGS, docs, SEGS, quarter).transpose(0, 2, 1, 3).reshape(8, width)
    return input_grad, wgrads[0], wgrads[1], channel_grads


def solution(mesh):
    seq, docs = mesh.shape["seq"], mesh.shape["doc"]
    shards = seq // SEGS
    fine = Mesh(mesh.devices.reshape(shards, SEGS, docs), ("z", "j", "doc"))
    tokens, rows = P("doc", ("z", "j"), None), P(("z", "j"), None)
    return jax.shard_map(
        functools.partial(per_device, shards, docs),
        mesh=fine,
        in_specs=(tokens, tokens, rows, rows, P(), P(), P(), P()),
        out_specs=(tokens, rows, rows, P()),
        check_vma=False,
    )
```

time: 1890 us -> 168 us (0.09)
  waiting for transfers between devices: 1350 us -> 58.1 us
  local copies, waits for them, and re-layouts: 366 us -> 9 us
  other arithmetic: 90.2 us -> 3.1 us
  starting transfers between devices: 7.39 us -> 45.6 us
  blocking collectives: 15.2 us -> 37.3 us
    reduce_scatter x2 -> x0, waiting for transfers between devices: 471 us -> none  [the longest x1 263 us: per_device(): lax.psum_scatter(local_i, 'seq', scatter_dimension=0, tiled=True)]
    psum x1 -> x0, waiting for transfers between devices: 441 us -> none  [per_device(): channel_grads = lax.psum(jnp.stack(rows, axis=0), ('seq', 'doc'))]
    all_gather x5 -> x0, waiting for transfers between devices: 435 us -> none  [the longest x3 186 us: entering(): everything = jax.tree.map(lambda part: lax.all_gather(part, axis), shard)]
    dynamic_slice x272 -> x0, local copies, waits for them, and re-layouts: 239 us -> none  [the longest x256 220 us: turn(): new = combine(before, jax.tree.map(lambda part: part[at], everything))]
    all_to_all x0 -> x5, waiting for transfers between devices: none -> 54.2 us  [the longest x1 17.9 us: per_device(): lax.all_to_all(jnp.concatenate(by_block + [weights], axis=1), 'j', 0, 0)]
    dynamic_update_slice x32 -> x0, local copies, waits for them, and re-layouts: 48 us -> none  [blocked_scan(): lax.scan(advance, start, (block_p, block_h), reverse=reverse)]
    all_to_all x0 -> x5, starting transfers between devices: none -> 41.2 us  [the longest x1 15.9 us: per_device(): weights = lax.all_to_all(weights, 'z', 0, 0).reshape(SEGS, 4 * share, block)]
    all_to_all x0 -> x2, blocking collectives: none -> 37.3 us  [the longest x1 18.6 us: per_device(): lax.all_to_all(jnp.concatenate([wg, packed], axis=1), ('j', 'doc'), 0, 0)]
  transfers between devices with their start and end apart: 10 -> 7, of which waited for: 10 -> 7; matrix products, arithmetic and copies ran while one was open for 13% -> 3% of each run, Pallas kernels for 0% -> 0%
where the time goes in v1:
time: 168 us
  waiting for transfers between devices  58.1 us (35%)
  starting transfers between devices  45.6 us (27%)
  blocking collectives  37.3 us (22%)
  Pallas kernels  13.7 us (8%)
  local copies, waits for them, and re-layouts  9 us (5%)
  other arithmetic  3.1 us (2%)
    all_to_all x1, blocking collectives, per_device(): lax.all_to_all(jnp.concatenate([wg, packed], axis=1), ('j', 'doc'), 0, 0)  18.6 us
    all_to_all x1, blocking collectives, per_device(): lax.all_to_all(jnp.broadcast_to(summary[None], (shards, 4, block)), 'z',...  18.6 us
    all_to_all x1, waiting for transfers between devices, per_device(): lax.all_to_all(jnp.concatenate(by_block + [weights], axis=1), 'j', 0, 0)  17.9 us
    all_to_all x1, starting transfers between devices, per_device(): weights = lax.all_to_all(weights, 'z', 0, 0).reshape(SEGS, 4 * share, block)  15.9 us
    all_to_all x1, waiting for transfers between devices, per_device(): weights = lax.all_to_all(weights, 'z', 0, 0).reshape(SEGS, 4 * share, block)  11.1 us
    all_to_all x1, starting transfers between devices, per_device(): lax.all_to_all(jnp.concatenate(by_block + [weights], axis=1), 'j', 0, 0)  10.6 us
    all_to_all x1, waiting for transfers between devices, per_device(): lax.all_to_all(send, ('j', 'doc'), 0, 0).reshape(SEGS, docs, 10, block)  9.83 us
    all_to_all x1, waiting for transfers between devices, per_device(): ig = lax.all_to_all(ig, 'j', 0, 0)  9.41 us
  transfers between devices with their start and end apart: 7, of which 7 were waited for; matrix products, arithmetic and copies ran while one was open for 3% of the time, Pallas kernels for 0%

profile of v1, /device:TPU:1, one launch (start us, length us, event | category | flops | bytes accessed | tf_op | source)
XLA Modules:
  0.0 167.6 jit_solution(16388283153127164698)
XLA Ops:
  0.6 0.7 pad_maximum_fusion.3
  1.3 0.7 broadcast_in_dim.16
  2.1 0.0 copy-start.6
  2.1 15.9 %all-to-all-start = ((bf16[16,32,256]{2,1,0:T(8,128)(2,1)}), bf16[16,32,256]{2,1,0:T(8,128)(2,1)S(1)}, u32[]{:S(2)}, u32[]{:S(2)}) async-start(bf16[16,32,256]{2,1,0:T(8,128)(2,1)} %broadcast_in_dim.16), calls=%async_computation | async-start | bytes 524288 | tf_op jit(solution)/shard_map/all_to_all | solution.py:258
  18.0 1.3 copy.62
  19.3 0.2 copy.63
  19.5 0.0 copy-done.6
  19.5 0.3 copy.64
  19.8 0.2 copy.65
  20.0 11.1 %all-to-all-done = bf16[16,32,256]{2,1,0:T(8,128)(2,1)S(1)} async-done(((bf16[16,32,256]{2,1,0:T(8,128)(2,1)}), bf16[16,32,256]{2,1,0:T(8,128)(2,1)S(1)}, u32[]{:S(2)}, u32[]{:S(2)}) %all-to-all-start) | async-done | bytes 262176 | tf_op jit(solution)/shard_map/all_to_all | solution.py:258
  31.1 1.2 pad_maximum_fusion
  32.3 10.6 %all-to-all-start.1 = ((bf16[8,320,256]{2,1,0:T(8,128)(2,1)}), bf16[8,320,256]{2,1,0:T(8,128)(2,1)S(1)}, u32[]{:S(2)}, u32[]{:S(2)}) async-start(bf16[8,320,256]{2,1,0:T(8,128)(2,1)} %pad_maximum_fusion), calls=%async_computation.1 | async-start | bytes 2621440 | tf_op jit(solution)/shard_map/all_to_all | solution.py:260
  42.9 17.9 %all-to-all-done.1.buf_ref = bf16[8,320,256]{2,1,0:T(8,128)(2,1)S(1)} async-done(((bf16[8,320,256]{2,1,0:T(8,128)(2,1)}), bf16[8,320,256]{2,1,0:T(8,128)(2,1)S(1)}, u32[]{:S(2)}, u32[]{:S(2)}) %all-to-all-start.1) | async-done | bytes 1310752 | tf_op jit(solution)/shard_map/all_to_all | solution.py:260
  60.8 3.1 %collective-permute-start = (bf16[16,256]{1,0:T(8,128)(2,1)S(1)}, bf16[16,256]{1,0:T(8,128)(2,1)S(1)}, u32[]{:S(2)}, u32[]{:S(2)}) collective-permute-start(bf16[16,256]{1,0:T(8,128)(2,1)S(1)} %slice_bitcast_fusion), channel_id=1, source_target_pairs={{0,32},{32,64},{64,96},{96,128},{128,160},{160,192},{192,224},{224... | collective-permute-start | bytes 24584 | tf_op jit(solution)/shard_map/ppermute | solution.py:261
  63.9 0.1 pad_add_fusion.at_ref
  64.0 0.7 collective-permute-done.halo_ref
  64.7 0.0 copy-done.5
  64.7 0.0 copy-done.1
  64.7 0.0 copy-done.2
  64.7 0.0 copy-done.3
  64.7 0.0 copy-done.4
  64.7 5.9 %forward.1 = (bf16[1024,256]{1,0:T(8,128)(2,1)S(1)}, f32[1024,256]{1,0:T(8,128)S(1)}, f32[1024,256]{1,0:T(8,128)S(1)}, f32[1024,256]{1,0:T(8,128)S(1)}, f32[1024...) custom-call(s32[2]{0:T(128)S(1)} %pad_add_fusion.at_ref, ...), custom_call_target="tpu_custom_call" | custom-call | tf_op jit(solution)/shard_map/forward/pallas_call | solution.py:271
  70.6 0.0 copy-start
  70.7 1.0 copy-done
  71.6 18.6 %all_to_all.35.all_ref = f32[16,4,256]{2,1,0:T(4,128)S(1)} all-to-all(f32[16,4,256]{2,1,0:T(4,128)S(1)} %broadcast_in_dim.36), channel_id=1, replica_groups=mesh['z'=16,'j'=8,'doc'=4] {'z'}, dimensions={0} | all-to-all | bytes 131072 | tf_op jit(solution)/shard_map/all_to_all | solution.py:284
  90.2 7.8 %backward.1 = (bf16[8,128,256]{2,1,0:T(8,128)(2,1)}, bf16[32,16,256]{2,1,0:T(8,128)(2,1)S(1)}, f32[8,256]{1,0:T(8,128)S(1)}, f32[8,256]{1,0:T(8,128)S(1)}) custom-call(s32[2]{0:T(128)S(1)} %pad_add_fusion.at_ref, bf16[8,320,256]{2,1,0:T(8,128)(2,1)} %copy-done.5, bf16[1024,256]{1,0:T(8,128)(2,1)S(1)} %get-tuple-element.29.conv_ref, ...), custom_call_target="tpu_custom_call" | custom-call | tf_op jit(solution)/shard_map/backward/pallas_call | solution.py:286
  98.0 0.1 reshape_reshape.3
  98.1 0.1 fusion.5
  98.3 18.6 %all_to_all.36 = bf16[32,24,256]{2,1,0:T(8,128)(2,1)S(1)} all-to-all(bf16[32,24,256]{2,1,0:T(8,128)(2,1)S(1)} %pad_maximum_fusion.1), channel_id=1, replica_groups=mesh['z'=16,'j'=8,'doc'=4] {'j','doc'}, dimensions={0} | all-to-all | bytes 786432 | tf_op jit(solution)/shard_map/all_to_all | solution.py:314
  116.9 0.1 fusion.7
  117.0 0.1 broadcast_in_dim.37
  117.2 0.7 pad_maximum_fusion.2
  117.9 3.5 %all-to-all-start.5 = ((bf16[16,12,256]{2,1,0:T(8,128)(2,1)}), bf16[16,12,256]{2,1,0:T(8,128)(2,1)S(1)}, u32[]{:S(2)}, u32[]{:S(2)}) async-start(bf16[16,12,256]{2,1,0:T(8,128)(2,1)} %pad_maximum_fusion.2), calls=%async_computation.5 | async-start | bytes 262144 | tf_op jit(solution)/shard_map/all_to_all | solution.py:319
  121.4 1.3 collective-permute-start.1
  122.7 3.2 %collective-permute-done.1 = f32[3,256]{1,0:T(4,128)S(1)} collective-permute-done((f32[3,256]{1,0:T(4,128)S(1)}, f32[3,256]{1,0:T(4,128)S(1)}, u32[]{:S(2)}, u32[]{:S(2)}) %collective-permute-start.1) | collective-permute-done | bytes 3104 | tf_op jit(solution)/shard_map/ppermute | solution.py:299
  125.9 0.1 convert_bitcast_fusion.2
  126.0 1.3 scatter.4
  127.3 6.0 %all-to-all-done.5 = bf16[16,12,256]{2,1,0:T(8,128)(2,1)S(1)} async-done(((bf16[16,12,256]{2,1,0:T(8,128)(2,1)}), bf16[16,12,256]{2,1,0:T(8,128)(2,1)S(1)}, u32[]{:S(2)}, u32[]{:S(2)}) %all-to-all-start.5) | async-done | bytes 98336 | tf_op jit(solution)/shard_map/all_to_all | solution.py:319
  133.3 6.8 %all-to-all-start.3 = ((bf16[8,128,256]{2,1,0:T(8,128)(2,1)}), bf16[8,128,256]{2,1,0:T(8,128)(2,1)S(1)}, u32[]{:S(2)}, u32[]{:S(2)}) async-start(bf16[8,128,256]{2,1,0:T(8,128)(2,1)} %scatter.4), calls=%async_computation.3 | async-start | bytes 1048576 | tf_op jit(solution)/shard_map/all_to_all | solution.py:308
  140.2 9.4 %all-to-all-done.3 = bf16[8,128,256]{2,1,0:T(8,128)(2,1)S(1)} async-done(((bf16[8,128,256]{2,1,0:T(8,128)(2,1)}), bf16[8,128,256]{2,1,0:T(8,128)(2,1)S(1)}, u32[]{:S(2)}, u32[]{:S(2)}) %all-to-all-start.3) | async-done | bytes 524320 | tf_op jit(solution)/shard_map/all_to_all | solution.py:308
  149.6 0.9 broadcast_in_dim.40
  150.5 4.4 %all-to-all-start.6 = ((f32[32,10,256]{2,1,0:T(8,128)}), f32[32,10,256]{2,1,0:T(8,128)S(1)}, u32[]{:S(2)}, u32[]{:S(2)}) async-start(f32[32,10,256]{2,1,0:T(8,128)} %broadcast_in_dim.40), calls=%async_computation.6 | async-start | bytes 1048576 | tf_op jit(solution)/shard_map/all_to_all | solution.py:323
  154.9 0.3 copy.66
  155.2 1.0 copy.72
  156.2 9.8 %all-to-all-done.6 = f32[32,10,256]{2,1,0:T(8,128)S(1)} async-done(((f32[32,10,256]{2,1,0:T(8,128)}), f32[32,10,256]{2,1,0:T(8,128)S(1)}, u32[]{:S(2)}, u32[]{:S(2)}) %all-to-all-start.6) | async-done | bytes 327712 | tf_op jit(solution)/shard_map/all_to_all | solution.py:323
  166.1 0.1 reshape.151
  166.2 0.8 reshape.152
  167.0 0.6 dynamic-slice_bitcast_fusion
  (23 shorter events, 0.3 us)
Async XLA Ops:
  2.1 17.4 %copy-start.6 = (bf16[1,128,2048]{2,1,0:T(8,128)(2,1)S(1)}, bf16[1,128,2048]{2,1,0:T(8,128)(2,1)}, u32[]{:S(2)}) copy-start(bf16[1,128,2048]{2,1,0:T(8,128)(2,1)} %param.11) | copy-start | bytes 1572868
  2.1 29.0 %all-to-all-start = ((bf16[16,32,256]{2,1,0:T(8,128)(2,1)}), bf16[16,32,256]{2,1,0:T(8,128)(2,1)S(1)}, u32[]{:S(2)}, u32[]{:S(2)}) async-start(bf16[16,32,256]{2,1,0:T(8,128)(2,1)} %broadcast_in_dim.16), calls=%async_computation | async-start | bytes 524288 | tf_op jit(solution)/shard_map/all_to_all | solution.py:258
  32.3 32.4 %copy-start.1 = (f32[4,2048]{1,0:T(4,128)S(1)}, f32[4,2048]{1,0:T(4,128)}, u32[]{:S(2)}) copy-start(f32[4,2048]{1,0:T(4,128)} %taps_ref.3) | copy-start | bytes 98308
  32.3 32.4 %copy-start.2 = (f32[2,2048]{1,0:T(2,128)S(1)}, f32[2,2048]{1,0:T(2,128)}, u32[]{:S(2)}) copy-start(f32[2,2048]{1,0:T(2,128)} %bias_ref.3) | copy-start | bytes 49156
  32.3 32.4 %copy-start.3 = (f32[2048]{0:T(1024)S(1)}, f32[2048]{0:T(1024)}, u32[]{:S(2)}) copy-start(f32[2048]{0:T(1024)} %param.16) | copy-start | bytes 24580
  32.3 32.4 %copy-start.4 = (f32[2048]{0:T(1024)S(1)}, f32[2048]{0:T(1024)}, u32[]{:S(2)}) copy-start(f32[2048]{0:T(1024)} %param.17) | copy-start | bytes 24580
  32.3 28.5 %all-to-all-start.1 = ((bf16[8,320,256]{2,1,0:T(8,128)(2,1)}), bf16[8,320,256]{2,1,0:T(8,128)(2,1)S(1)}, u32[]{:S(2)}, u32[]{:S(2)}) async-start(bf16[8,320,256]{2,1,0:T(8,128)(2,1)} %pad_maximum_fusion), calls=%async_computation.1 | async-start | bytes 2621440 | tf_op jit(solution)/shard_map/all_to_all | solution.py:260
  60.8 3.9 %copy-start.5 = (bf16[8,320,256]{2,1,0:T(8,128)(2,1)}, bf16[8,320,256]{2,1,0:T(8,128)(2,1)S(1)}, u32[]{:S(2)}) copy-start(bf16[8,320,256]{2,1,0:T(8,128)(2,1)S(1)} %all-to-all-done.1.buf_ref) | copy-start | bytes 3932164
  60.8 3.9 %collective-permute-start = (bf16[16,256]{1,0:T(8,128)(2,1)S(1)}, bf16[16,256]{1,0:T(8,128)(2,1)S(1)}, u32[]{:S(2)}, u32[]{:S(2)}) collective-permute-start(bf16[16,256]{1,0:T(8,128)(2,1)S(1)} %slice_bitcast_fusion), channel_id=1, source_target_pairs={{0,32},{32,64},{64,96},{96,128},{128,160},{160,192},{192,224},{224... | collective-permute-start | bytes 24584 | tf_op jit(solution)/shard_map/ppermute | solution.py:261
  70.6 1.0 copy-start
  117.9 15.5 %all-to-all-start.5 = ((bf16[16,12,256]{2,1,0:T(8,128)(2,1)}), bf16[16,12,256]{2,1,0:T(8,128)(2,1)S(1)}, u32[]{:S(2)}, u32[]{:S(2)}) async-start(bf16[16,12,256]{2,1,0:T(8,128)(2,1)} %pad_maximum_fusion.2), calls=%async_computation.5 | async-start | bytes 262144 | tf_op jit(solution)/shard_map/all_to_all | solution.py:319
  121.4 4.5 %collective-permute-start.1 = (f32[3,256]{1,0:T(4,128)S(1)}, f32[3,256]{1,0:T(4,128)S(1)}, u32[]{:S(2)}, u32[]{:S(2)}) collective-permute-start(f32[3,256]{1,0:T(4,128)S(1)} %slice.100), channel_id=1, source_target_pairs={{32,0},{64,32},{96,64},{128,96},{160,128},{192,160},{224,192},{256... | collective-permute-start | bytes 9224 | tf_op jit(solution)/shard_map/ppermute | solution.py:299
  133.3 16.3 %all-to-all-start.3 = ((bf16[8,128,256]{2,1,0:T(8,128)(2,1)}), bf16[8,128,256]{2,1,0:T(8,128)(2,1)S(1)}, u32[]{:S(2)}, u32[]{:S(2)}) async-start(bf16[8,128,256]{2,1,0:T(8,128)(2,1)} %scatter.4), calls=%async_computation.3 | async-start | bytes 1048576 | tf_op jit(solution)/shard_map/all_to_all | solution.py:308
  150.5 15.6 %all-to-all-start.6 = ((f32[32,10,256]{2,1,0:T(8,128)}), f32[32,10,256]{2,1,0:T(8,128)S(1)}, u32[]{:S(2)}, u32[]{:S(2)}) async-start(f32[32,10,256]{2,1,0:T(8,128)} %broadcast_in_dim.40), calls=%async_computation.6 | async-start | bytes 1048576 | tf_op jit(solution)/shard_map/all_to_all | solution.py:323

commit v2 on v1

--- a/solution.py
+++ b/solution.py
@@ -31,15 +31,13 @@
     return dot(shuffle, jnp.concatenate(tiles, axis=0))
 
 
-def load_weights(buf_ref, w_ref, steps):
+def load_weights(buf_ref, w_ref, first):
     block = w_ref.shape[0]
-    share = block // 2 // SEGS
-    for p in range(2):
-        for s in range(SEGS):
-            row = p * (block // 2) + s * share
+    for s in range(SEGS):
+        for p in range(2):
             for w in range(2):
-                at = 2 * steps + (p * 2 + w) * share
-                w_ref[row : row + share, w * block : (w + 1) * block] = buf_ref[s, at : at + share, :]
+                row, at = p * (block // 2) + s * 16, first + (p * 2 + w) * 16
+                w_ref[row : row + 16, w * block : (w + 1) * block] = buf_ref[s, at : at + 16, :]
 
 
 def one_minus_exp(x):
@@ -54,15 +52,15 @@
 
 
 def forward_kernel(
-    steps, at_ref, buf_ref, halo_ref, bias_ref, taps_ref, cbias_ref, decay_ref,
+    steps, at_ref, buf_ref, bias_ref, taps_ref, cbias_ref, decay_ref,
     conv_ref, r_ref, i_ref, a_ref, m_ref, xpad_ref, seg_ref, sum_ref, w_ref,
 ):
     block = w_ref.shape[0]
     shuffle = shuffle_matrix()
-    load_weights(buf_ref, w_ref, steps)
+    load_weights(buf_ref, w_ref, 2 * steps)
     bias, taps, cbias, rate = block_params(at_ref, bias_ref, taps_ref, cbias_ref, decay_ref, block)
     last = by_step(buf_ref, shuffle, steps - SPAN)[ROWS - 3 * SEGS :]
-    halo = jnp.where(at_ref[0] > 0, halo_ref[...].astype(F32), 0.0)
+    halo = jnp.where(at_ref[0] > 0, buf_ref[SEGS - 1, 2 * steps + 64 : 2 * steps + 80, :].astype(F32), 0.0)
     for k in range(3):
         rows = last[k * SEGS : (k + 1) * SEGS]
         xpad_ref[k * SEGS : (k + 1) * SEGS, :] = jnp.concatenate(
@@ -224,14 +222,22 @@
     sums[7] = sums[7] * scale
     rows_ref[...] = jnp.concatenate(sums, axis=0)
     wg = dot(conv_ref[...], gates_ref[...], ((0,), (0,)))
-    half = block // 2
     for s in range(SEGS):
-        for w in range(2):
-            for h in range(2):
-                at = [p * half + s * 16 + h * 8 for p in range(2)]
-                lanes = slice(w * block, (w + 1) * block)
-                pair = jnp.concatenate([wg[k : k + 8, lanes] for k in at], axis=0)
-                wg_ref[s * 4 + w * 2 + h] = pair.astype(BF16)
+        for q in range(4):
+            for p in range(2):
+                row = p * (block // 2) + s * 16
+                tile = wg[row : row + 16, q * 128 : (q + 1) * 128]
+                wg_ref[s * 4 + q, p * 16 : (p + 1) * 16, :] = tile.astype(BF16)
+
+
+def unpack_kernel(steps, got_ref, ig_ref, rows_ref):
+    block = got_ref.shape[2]
+    for b in range(SEGS):
+        ig_ref[0, :, b * block : (b + 1) * block] = got_ref[b, :steps, :]
+        pair = got_ref[b, steps : steps + 2 * SEGS, :].astype(F32)
+        row = pair[:SEGS] + pair[SEGS:]
+        for k in range(SEGS):
+            rows_ref[b : b + 1, k * block : (k + 1) * block] = row[k : k + 1]
 
 
 def split(v):
@@ -256,17 +262,17 @@
     weights = jnp.concatenate([recur_weight, input_weight], axis=0)
     weights = jnp.broadcast_to(weights[None], (shards, 2 * share, block))
     weights = lax.all_to_all(weights, "z", 0, 0).reshape(SEGS, 4 * share, block)
-    by_block = [v[0].reshape(steps, SEGS, block).transpose(1, 0, 2) for v in (block_input, state_cotangent)]
-    buf = lax.all_to_all(jnp.concatenate(by_block + [weights], axis=1), "j", 0, 0)
-    halo = lax.ppermute(
-        buf[SEGS - 1, steps - SPAN : steps], "z", [(k, k + 1) for k in range(shards - 1)]
-    )
+    forth = [(k, k + 1) for k in range(shards - 1)]
+    halo = lax.ppermute(block_input[0, steps - 16 :], "z", forth)
+    tokens = (block_input[0], state_cotangent[0], halo)
+    xs, ds, halo = (v.reshape(-1, SEGS, block).transpose(1, 0, 2) for v in tokens)
+    buf = lax.all_to_all(jnp.concatenate([xs, ds, weights, halo], axis=1), "j", 0, 0)
 
     total = SEGS * steps
     smem = pl.BlockSpec(memory_space=pltpu.SMEM)
     vmem = pl.BlockSpec(memory_space=pltpu.VMEM)
     shape = jax.ShapeDtypeStruct
-    limit = pltpu.CompilerParams(vmem_limit_bytes=48 * 1024 * 1024)
+    limit = pltpu.CompilerParams(vmem_limit_bytes=24 * 1024 * 1024)
     full = shape((total, block), F32)
     conv, r, i, a, m, xpad, seg, summary, w = pl.pallas_call(
         functools.partial(forward_kernel, steps),
@@ -275,18 +281,18 @@
             shape((total + 3 * SEGS, block), F32), shape((3 * SEGS, block), F32),
             shape((4, block), F32), shape((block, 2 * block), BF16),
         ),
-        in_specs=[smem] + [vmem] * 6,
+        in_specs=[smem] + [vmem] * 5,
         out_specs=(vmem,) * 9,
         compiler_params=limit,
         name="forward",
-    )(at, buf, halo, *params)
+    )(at, buf, *params)
 
     everyone = lax.all_to_all(jnp.broadcast_to(summary[None], (shards, 4, block)), "z", 0, 0)
 
     ig, wg, rows, edge = pl.pallas_call(
         functools.partial(backward_kernel, steps, shards),
         out_shape=(
-            shape((SEGS, steps, block), BF16), shape((4 * SEGS, 16, block), BF16),
+            shape((SEGS, steps, block), BF16), shape((4 * SEGS, 32, 128), BF16),
             shape((8, block), F32), shape((8, block), F32),
         ),
         in_specs=[smem] + [vmem] * 14,
@@ -305,24 +311,30 @@
             row = row + taps[3 - k + n] * head[n]
         late.append(row)
     ig = ig.at[SEGS - 1, steps - 3 :].set(jnp.stack(late).astype(BF16))
-    ig = lax.all_to_all(ig, "j", 0, 0)
-    input_grad = ig.transpose(1, 0, 2).reshape(1, steps, width)
-
     quarter = block // docs
-    pieces = split(rows.reshape(SEGS, docs, quarter).reshape(SEGS * docs, 1, quarter))
-    packed = jnp.pad(jnp.concatenate(pieces, axis=2), ((0, 0), (0, 7), (0, block - 2 * quarter)))
+    packed = jnp.concatenate(split(rows.reshape(SEGS * docs, 1, quarter)), axis=2)
     got = lax.all_to_all(jnp.concatenate([wg, packed], axis=1), ("j", "doc"), 0, 0)
-    got = got.reshape(SEGS, docs, 24, block)
-    wsum = jnp.sum(got[:, :, :16].astype(F32), axis=1).reshape(shards, 8, block)
-    csum = jnp.sum(joined(got[:, :, 16, :quarter], got[:, :, 16, quarter : 2 * quarter]), axis=1)
-    csum = jnp.broadcast_to(csum.reshape(1, 2, block), (shards, 2, block))
+    got = got.reshape(SEGS, docs, 33, 128)
+    wsum = jnp.sum(got[:, :, :32].astype(F32), axis=1).reshape(shards, 16, 128)
+    csum = jnp.sum(joined(got[:, :, 32, :quarter], got[:, :, 32, quarter:]), axis=1)
+    csum = jnp.broadcast_to(csum.reshape(1, 4, 128), (shards, 4, 128))
     got = lax.all_to_all(jnp.concatenate((wsum.astype(BF16),) + split(csum), axis=1), "z", 0, 0)
-    wsum = jnp.sum(got[:, :8].astype(F32), axis=0)
-    csum = jnp.sum(joined(got[:, 8:10], got[:, 10:12]), axis=0)
-    send = jnp.broadcast_to(jnp.concatenate([wsum, csum], axis=0)[None], (SEGS * docs, 10, block))
-    got = lax.all_to_all(send, ("j", "doc"), 0, 0).reshape(SEGS, docs, 10, block)
-    wgrads = lax.dynamic_index_in_dim(got[:, :, :8], j, 0, keepdims=False).reshape(2, 2 * 8, block)
-    channel_grads = got[:, :, 8:].reshape(SEGS, docs, SEGS, quarter).transpose(0, 2, 1, 3).reshape(8, width)
+    wsum = jnp.sum(got[:, :16].astype(F32), axis=0)
+    csum = jnp.sum(joined(got[:, 16:20], got[:, 20:]), axis=0)
+    send = jnp.concatenate([wsum, csum], axis=0)
+    got = lax.all_to_all(jnp.broadcast_to(send[None], (docs, 20, 128)), "doc", 0, 0)
+    wgrads = got[:, :16].reshape(2, 2, 16, 128).transpose(0, 2, 1, 3).reshape(2, 16, block)
+    csum = got[:, 16:].reshape(docs, SEGS, quarter).transpose(1, 0, 2).reshape(SEGS, block)
+    csum = jnp.broadcast_to(jnp.concatenate(split(csum), axis=0)[None], (SEGS, 2 * SEGS, block))
+    got = lax.all_to_all(jnp.concatenate([ig, csum], axis=1), "j", 0, 0)
+    input_grad, channel_grads = pl.pallas_call(
+        functools.partial(unpack_kernel, steps),
+        out_shape=(shape((1, steps, width), BF16), shape((SEGS, width), F32)),
+        in_specs=[vmem],
+        out_specs=(vmem,) * 2,
+        compiler_params=limit,
+        name="unpack",
+    )(got)
     return input_grad, wgrads[0], wgrads[1], channel_grads
 
 

time: 168 us -> 153 us (0.911)
  waiting for transfers between devices: 58.1 us -> 49.6 us
  blocking collectives: 37.3 us -> 33.2 us
  local copies, waits for them, and re-layouts: 9 us -> 5.38 us
    all_to_all x1, waiting for transfers between devices: 11.1 us -> 3.77 us  [per_device(): weights = lax.all_to_all(weights, 'z', 0, 0).reshape(SEGS, 4 * share, block)]
    all_to_all x3, waiting for transfers between devices: 37.2 us -> 32.3 us  [the longest x1 18.5 us: per_device(): lax.all_to_all(jnp.concatenate([xs, ds, weights, halo], axis=1), 'j', 0, 0)]
    ppermute x1, waiting for transfers between devices: 0.7 us -> 3.2 us  [per_device(): halo = lax.ppermute(block_input[0, steps - 16:], 'z', forth)]
    all_to_all x1, blocking collectives: 18.6 us -> 16.4 us  [per_device(): lax.all_to_all(jnp.broadcast_to(summary[None], (shards, 4, block)), 'z',...]
    unnamed x17 -> x12, local copies, waits for them, and re-layouts: 3.58 us -> 1.6 us
    all_to_all x1, blocking collectives: 18.6 us -> 16.8 us  [per_device(): lax.all_to_all(jnp.concatenate([wg, packed], axis=1), ('j', 'doc'), 0, 0)]
where the time goes in v2:
time: 153 us; the launch traced here: 152 us
  waiting for transfers between devices  49.6 us (32%)
  starting transfers between devices  47.1 us (31%)
  blocking collectives  33.2 us (22%)
  Pallas kernels  12.1 us (8%)
  local copies, waits for them, and re-layouts  5.38 us (4%)
  other arithmetic  3.93 us (3%)
    all_to_all x1, waiting for transfers between devices, per_device(): lax.all_to_all(jnp.concatenate([xs, ds, weights, halo], axis=1), 'j', 0, 0)  18.5 us
    all_to_all x1, blocking collectives, per_device(): lax.all_to_all(jnp.concatenate([wg, packed], axis=1), ('j', 'doc'), 0, 0)  16.8 us
    all_to_all x1, blocking collectives, per_device(): lax.all_to_all(jnp.broadcast_to(summary[None], (shards, 4, block)), 'z',...  16.4 us
    all_to_all x1, starting transfers between devices, per_device(): weights = lax.all_to_all(weights, 'z', 0, 0).reshape(SEGS, 4 * share, block)  15.9 us
    all_to_all x1, starting transfers between devices, per_device(): lax.all_to_all(jnp.concatenate([xs, ds, weights, halo], axis=1), 'j', 0, 0)  12.5 us
    all_to_all x1, waiting for transfers between devices, per_device(): got = lax.all_to_all(jnp.concatenate([ig, csum], axis=1), 'j', 0, 0)  9.54 us
    all_to_all x1, starting transfers between devices, per_device(): got = lax.all_to_all(jnp.concatenate([ig, csum], axis=1), 'j', 0, 0)  7.38 us
    all_to_all x1, waiting for transfers between devices, per_device(): lax.all_to_all(jnp.concatenate((wsum.astype(BF16),) + split(csum), axis=1...  6.9 us
  transfers between devices with their start and end apart: 7, of which 7 were waited for; matrix products, arithmetic and copies ran while one was open for 3% of the time, Pallas kernels for 0%

profile of v2, /device:TPU:1, one launch (start us, length us, event | category | flops | bytes accessed | tf_op | source)
XLA Modules:
  0.0 152.1 jit_solution(6289746475283039508)
XLA Ops:
  0.6 0.7 pad_maximum_fusion.3
  1.3 0.7 broadcast_in_dim.18
  2.1 0.0 copy-start.4
  2.1 15.9 %all-to-all-start = ((bf16[16,32,256]{2,1,0:T(8,128)(2,1)}), bf16[16,32,256]{2,1,0:T(8,128)(2,1)S(1)}, u32[]{:S(2)}, u32[]{:S(2)}) async-start(bf16[16,32,256]{2,1,0:T(8,128)(2,1)} %broadcast_in_dim.18), calls=%async_computation | async-start | bytes 524288 | tf_op jit(solution)/shard_map/all_to_all | solution.py:264
  18.0 0.8 slice_bitcast_fusion
  18.8 3.3 %collective-permute-start = (bf16[16,2048]{1,0:T(8,128)(2,1)S(1)}, bf16[16,2048]{1,0:T(8,128)(2,1)S(1)}, u32[]{:S(2)}, u32[]{:S(2)}) collective-permute-start(bf16[16,2048]{1,0:T(8,128)(2,1)S(1)} %slice_bitcast_fusion), channel_id=1, source_target_pairs={{0,32},{32,64},{64,96},{96,128},{128,160},{160,192},{192,224},{224... | collective-permute-start | bytes 196616 | tf_op jit(solution)/shard_map/ppermute | solution.py:266
  22.1 1.3 copy.42
  23.4 0.2 copy.43
  23.6 0.0 copy-done.4
  23.6 0.3 copy.44
  23.9 0.2 copy.45
  24.1 3.2 %collective-permute-done = bf16[16,2048]{1,0:T(8,128)(2,1)S(1)} collective-permute-done((bf16[16,2048]{1,0:T(8,128)(2,1)S(1)}, bf16[16,2048]{1,0:T(8,128)(2,1)S(1)}, u32[]{:S(2)}, u32[]{:S(2)}) %collective-permute-start) | collective-permute-done | bytes 65568 | tf_op jit(solution)/shard_map/ppermute | solution.py:266
  27.3 3.8 %all-to-all-done = bf16[16,32,256]{2,1,0:T(8,128)(2,1)S(1)} async-done(((bf16[16,32,256]{2,1,0:T(8,128)(2,1)}), bf16[16,32,256]{2,1,0:T(8,128)(2,1)S(1)}, u32[]{:S(2)}, u32[]{:S(2)}) %all-to-all-start) | async-done | bytes 262176 | tf_op jit(solution)/shard_map/all_to_all | solution.py:264
  31.1 1.2 pad_maximum_fusion
  32.3 0.0 copy-start
  32.3 0.0 copy-start.1
  32.3 12.5 %all-to-all-start.1 = ((bf16[8,336,256]{2,1,0:T(8,128)(2,1)}), bf16[8,336,256]{2,1,0:T(8,128)(2,1)S(1)}, u32[]{:S(2)}, u32[]{:S(2)}) async-start(bf16[8,336,256]{2,1,0:T(8,128)(2,1)} %pad_maximum_fusion), calls=%async_computation.1 | async-start | bytes 2752512 | tf_op jit(solution)/shard_map/all_to_all | solution.py:269
  44.8 0.1 pad_add_fusion.at_ref
  44.9 18.5 %all-to-all-done.1.buf_ref = bf16[8,336,256]{2,1,0:T(8,128)(2,1)S(1)} async-done(((bf16[8,336,256]{2,1,0:T(8,128)(2,1)}), bf16[8,336,256]{2,1,0:T(8,128)(2,1)S(1)}, u32[]{:S(2)}, u32[]{:S(2)}) %all-to-all-start.1) | async-done | bytes 1376288 | tf_op jit(solution)/shard_map/all_to_all | solution.py:269
  63.4 0.0 copy-done
  63.4 0.0 copy-done.1
  63.4 0.0 copy-done.2
  63.5 0.0 copy-done.3
  63.5 5.1 %forward.1 = (bf16[1024,256]{1,0:T(8,128)(2,1)S(1)}, f32[1024,256]{1,0:T(8,128)S(1)}, f32[1024,256]{1,0:T(8,128)S(1)}, f32[1024,256]{1,0:T(8,128)S(1)}, f32[1024...) custom-call(s32[2]{0:T(128)S(1)} %pad_add_fusion.at_ref, ...), custom_call_target="tpu_custom_call" | custom-call | tf_op jit(solution)/shard_map/forward/pallas_call | solution.py:277
  68.6 16.4 %all_to_all.35.all_ref = f32[16,4,256]{2,1,0:T(4,128)S(1)} all-to-all(f32[16,4,256]{2,1,0:T(4,128)S(1)} %broadcast_in_dim.42), channel_id=1, replica_groups=mesh['z'=16,'j'=8,'doc'=4] {'z'}, dimensions={0} | all-to-all | bytes 131072 | tf_op jit(solution)/shard_map/all_to_all | solution.py:290
  85.0 6.1 %backward.1 = (bf16[8,128,256]{2,1,0:T(8,128)(2,1)S(1)}, bf16[32,32,128]{2,1,0:T(8,128)(2,1)S(1)}, f32[8,256]{1,0:T(8,128)S(1)}, f32[8,256]{1,0:T(8,128)S(1)}) custom-call(s32[2]{0:T(128)S(1)} %pad_add_fusion.at_ref, bf16[8,336,256]{2,1,0:T(8,128)(2,1)S(1)} %all-to-all-done.1.buf_ref, bf16[1024,256]{1,0:T(8,128)(2,1)S(1)} %get-tuple-element.31.conv_ref, ...), custom_call_target="tpu_custom_call" | custom-call | tf_op jit(solution)/shard_map/backward/pallas_call | solution.py:292
  91.1 0.1 reshape.152
  91.2 0.1 maximum_maximum_fusion
  91.3 16.8 %all_to_all.36 = bf16[32,33,128]{2,1,0:T(8,128)(2,1)S(1)} all-to-all(bf16[32,33,128]{2,1,0:T(8,128)(2,1)S(1)} %maximum_maximum_fusion), channel_id=1, replica_groups=mesh['z'=16,'j'=8,'doc'=4] {'j','doc'}, dimensions={0} | all-to-all | bytes 540672 | tf_op jit(solution)/shard_map/all_to_all | solution.py:316
  108.2 0.1 fusion.1
  108.3 0.1 broadcast_in_dim.43
  108.4 0.7 pad_maximum_fusion.2
  109.0 3.5 %all-to-all-start.4 = ((bf16[16,24,128]{2,1,0:T(8,128)(2,1)}), bf16[16,24,128]{2,1,0:T(8,128)(2,1)S(1)}, u32[]{:S(2)}, u32[]{:S(2)}) async-start(bf16[16,24,128]{2,1,0:T(8,128)(2,1)} %pad_maximum_fusion.2), calls=%async_computation.4 | async-start | bytes 196608 | tf_op jit(solution)/shard_map/all_to_all | solution.py:321
  112.6 1.3 collective-permute-start.1
  113.9 3.5 %collective-permute-done.1 = f32[3,256]{1,0:T(4,128)S(1)} collective-permute-done((f32[3,256]{1,0:T(4,128)S(1)}, f32[3,256]{1,0:T(4,128)S(1)}, u32[]{:S(2)}, u32[]{:S(2)}) %collective-permute-start.1) | collective-permute-done | bytes 3104 | tf_op jit(solution)/shard_map/ppermute | solution.py:305
  117.3 0.1 convert_bitcast_fusion.2
  117.4 6.9 %all-to-all-done.4 = bf16[16,24,128]{2,1,0:T(8,128)(2,1)S(1)} async-done(((bf16[16,24,128]{2,1,0:T(8,128)(2,1)}), bf16[16,24,128]{2,1,0:T(8,128)(2,1)S(1)}, u32[]{:S(2)}, u32[]{:S(2)}) %all-to-all-start.4) | async-done | bytes 98336 | tf_op jit(solution)/shard_map/all_to_all | solution.py:321
  124.4 0.6 broadcast_in_dim.46
  125.0 3.3 %all-to-all-start.5 = ((f32[4,20,128]{2,1,0:T(8,128)}), f32[4,20,128]{2,1,0:T(8,128)S(1)}, u32[]{:S(2)}, u32[]{:S(2)}) async-start(f32[4,20,128]{2,1,0:T(8,128)} %broadcast_in_dim.46), calls=%async_computation.5 | async-start | bytes 98304 | tf_op jit(solution)/shard_map/all_to_all | solution.py:325
  128.3 0.1 scatter.4
  128.4 4.2 %all-to-all-done.5 = f32[4,20,128]{2,1,0:T(8,128)S(1)} async-done(((f32[4,20,128]{2,1,0:T(8,128)}), f32[4,20,128]{2,1,0:T(8,128)S(1)}, u32[]{:S(2)}, u32[]{:S(2)}) %all-to-all-start.5) | async-done | bytes 40992 | tf_op jit(solution)/shard_map/all_to_all | solution.py:325
  132.6 0.1 reshape.154
  132.7 0.1 reshape.155
  132.8 0.9 pad_maximum_fusion.1
  133.7 7.4 %all-to-all-start.6 = ((bf16[8,144,256]{2,1,0:T(8,128)(2,1)}), bf16[8,144,256]{2,1,0:T(8,128)(2,1)S(1)}, u32[]{:S(2)}, u32[]{:S(2)}) async-start(bf16[8,144,256]{2,1,0:T(8,128)(2,1)} %pad_maximum_fusion.1), calls=%async_computation.6 | async-start | bytes 1179648 | tf_op jit(solution)/shard_map/all_to_all | solution.py:329
  141.1 0.6 copy_bitcast_fusion
  141.7 9.5 %all-to-all-done.6.got_ref = bf16[8,144,256]{2,1,0:T(8,128)(2,1)S(1)} async-done(((bf16[8,144,256]{2,1,0:T(8,128)(2,1)}), bf16[8,144,256]{2,1,0:T(8,128)(2,1)S(1)}, u32[]{:S(2)}, u32[]{:S(2)}) %all-to-all-start.6) | async-done | bytes 589856 | tf_op jit(solution)/shard_map/all_to_all | solution.py:329
  151.3 0.9 unpack.1
  (24 shorter events, 0.2 us)
Async XLA Ops:
  2.1 21.5 %copy-start.4 = (bf16[1,128,2048]{2,1,0:T(8,128)(2,1)S(1)}, bf16[1,128,2048]{2,1,0:T(8,128)(2,1)}, u32[]{:S(2)}) copy-start(bf16[1,128,2048]{2,1,0:T(8,128)(2,1)} %param.11) | copy-start | bytes 1572868
  2.1 29.0 %all-to-all-start = ((bf16[16,32,256]{2,1,0:T(8,128)(2,1)}), bf16[16,32,256]{2,1,0:T(8,128)(2,1)S(1)}, u32[]{:S(2)}, u32[]{:S(2)}) async-start(bf16[16,32,256]{2,1,0:T(8,128)(2,1)} %broadcast_in_dim.18), calls=%async_computation | async-start | bytes 524288 | tf_op jit(solution)/shard_map/all_to_all | solution.py:264
  18.8 8.5 %collective-permute-start = (bf16[16,2048]{1,0:T(8,128)(2,1)S(1)}, bf16[16,2048]{1,0:T(8,128)(2,1)S(1)}, u32[]{:S(2)}, u32[]{:S(2)}) collective-permute-start(bf16[16,2048]{1,0:T(8,128)(2,1)S(1)} %slice_bitcast_fusion), channel_id=1, source_target_pairs={{0,32},{32,64},{64,96},{96,128},{128,160},{160,192},{192,224},{224... | collective-permute-start | bytes 196616 | tf_op jit(solution)/shard_map/ppermute | solution.py:266
  32.3 31.2 %copy-start = (f32[4,2048]{1,0:T(4,128)S(1)}, f32[4,2048]{1,0:T(4,128)}, u32[]{:S(2)}) copy-start(f32[4,2048]{1,0:T(4,128)} %taps_ref.3) | copy-start | bytes 98308
  32.3 31.2 %copy-start.1 = (f32[2,2048]{1,0:T(2,128)S(1)}, f32[2,2048]{1,0:T(2,128)}, u32[]{:S(2)}) copy-start(f32[2,2048]{1,0:T(2,128)} %bias_ref.3) | copy-start | bytes 49156
  32.3 31.2 %copy-start.2 = (f32[2048]{0:T(1024)S(1)}, f32[2048]{0:T(1024)}, u32[]{:S(2)}) copy-start(f32[2048]{0:T(1024)} %param.16) | copy-start | bytes 24580
  32.3 31.2 %copy-start.3 = (f32[2048]{0:T(1024)S(1)}, f32[2048]{0:T(1024)}, u32[]{:S(2)}) copy-start(f32[2048]{0:T(1024)} %param.17) | copy-start | bytes 24580
  32.3 31.1 %all-to-all-start.1 = ((bf16[8,336,256]{2,1,0:T(8,128)(2,1)}), bf16[8,336,256]{2,1,0:T(8,128)(2,1)S(1)}, u32[]{:S(2)}, u32[]{:S(2)}) async-start(bf16[8,336,256]{2,1,0:T(8,128)(2,1)} %pad_maximum_fusion), calls=%async_computation.1 | async-start | bytes 2752512 | tf_op jit(solution)/shard_map/all_to_all | solution.py:269
  109.0 15.3 %all-to-all-start.4 = ((bf16[16,24,128]{2,1,0:T(8,128)(2,1)}), bf16[16,24,128]{2,1,0:T(8,128)(2,1)S(1)}, u32[]{:S(2)}, u32[]{:S(2)}) async-start(bf16[16,24,128]{2,1,0:T(8,128)(2,1)} %pad_maximum_fusion.2), calls=%async_computation.4 | async-start | bytes 196608 | tf_op jit(solution)/shard_map/all_to_all | solution.py:321
  112.6 4.8 %collective-permute-start.1 = (f32[3,256]{1,0:T(4,128)S(1)}, f32[3,256]{1,0:T(4,128)S(1)}, u32[]{:S(2)}, u32[]{:S(2)}) collective-permute-start(f32[3,256]{1,0:T(4,128)S(1)} %slice.100), channel_id=1, source_target_pairs={{32,0},{64,32},{96,64},{128,96},{160,128},{192,160},{224,192},{256... | collective-permute-start | bytes 9224 | tf_op jit(solution)/shard_map/ppermute | solution.py:305
  125.0 7.6 %all-to-all-start.5 = ((f32[4,20,128]{2,1,0:T(8,128)}), f32[4,20,128]{2,1,0:T(8,128)S(1)}, u32[]{:S(2)}, u32[]{:S(2)}) async-start(f32[4,20,128]{2,1,0:T(8,128)} %broadcast_in_dim.46), calls=%async_computation.5 | async-start | bytes 98304 | tf_op jit(solution)/shard_map/all_to_all | solution.py:325
  133.7 17.6 %all-to-all-start.6 = ((bf16[8,144,256]{2,1,0:T(8,128)(2,1)}), bf16[8,144,256]{2,1,0:T(8,128)(2,1)S(1)}, u32[]{:S(2)}, u32[]{:S(2)}) async-start(bf16[8,144,256]{2,1,0:T(8,128)(2,1)} %pad_maximum_fusion.1), calls=%async_computation.6 | async-start | bytes 1179648 | tf_op jit(solution)/shard_map/all_to_all | solution.py:329

commit v3 on v2

v3 whole, which is shorter than its diff:
```python
import functools

import jax
import jax.numpy as jnp
from jax import lax
from jax.experimental import pallas as pl
from jax.experimental.pallas import tpu as pltpu
from jax.sharding import Mesh
from jax.sharding import PartitionSpec as P

QFLOOR = 0.001
SEGS = 8
SPAN = 16
ROWS = SEGS * SPAN
UNROLL = (True, True, True, True)
F32 = jnp.float32
BF16 = jnp.bfloat16


def dot(a, b, contract=((1,), (0,))):
    return lax.dot_general(a, b, (contract, ((), ())), preferred_element_type=F32)


def shuffle_matrix():
    row = lax.broadcasted_iota(jnp.int32, (ROWS, ROWS), 0)
    col = lax.broadcasted_iota(jnp.int32, (ROWS, ROWS), 1)
    return jnp.where(col == (row % SEGS) * SPAN + row // SEGS, 1.0, 0.0).astype(BF16)


def by_step(buf_ref, shuffle, first):
    tiles = [buf_ref[s, pl.ds(first, SPAN), :] for s in range(SEGS)]
    return dot(shuffle, jnp.concatenate(tiles, axis=0))


def load_weights(buf_ref, w_ref, first):
    block = w_ref.shape[0]
    for s in range(SEGS):
        for p in range(2):
            for w in range(2):
                row, at = p * (block // 2) + s * 16, first + (p * 2 + w) * 16
                w_ref[row : row + 16, w * block : (w + 1) * block] = buf_ref[s, at : at + 16, :]


def one_minus_square(a, decay):
    x = 2.0 * decay
    series = x * (1.0 - x * (1 / 2) * (1.0 - x * (1 / 3) * (1.0 - x * (1 / 4))))
    return jnp.where(x < 0.0625, series, 1.0 - a * a)


def sigmoid(x):
    below = 1.0 + jnp.exp(-jnp.maximum(x, -80.0))
    guess = pl.reciprocal(below, approx=True)
    return guess * (2.0 - below * guess)


def block_params(at_ref, bias_ref, taps_ref, cbias_ref, decay_ref, block):
    lanes = pl.ds(pl.multiple_of(at_ref[1] * block, block), block)
    rate = jax.nn.softplus(-decay_ref[:, lanes])
    return bias_ref[:, lanes], taps_ref[:, lanes], cbias_ref[:, lanes], rate


def forward_kernel(
    steps, at_ref, buf_ref, bias_ref, taps_ref, cbias_ref, decay_ref,
    conv_ref, r_ref, i_ref, a_ref, m_ref, xpad_ref, seg_ref, sum_ref, w_ref,
):
    block = w_ref.shape[0]
    shuffle = shuffle_matrix()
    load_weights(buf_ref, w_ref, 2 * steps)
    bias, taps, cbias, rate = block_params(at_ref, bias_ref, taps_ref, cbias_ref, decay_ref, block)
    rate8 = 8.0 * rate
    last = by_step(buf_ref, shuffle, steps - SPAN)[ROWS - 3 * SEGS :]
    halo = jnp.where(at_ref[0] > 0, buf_ref[SEGS - 1, 2 * steps + 64 : 2 * steps + 80, :].astype(F32), 0.0)
    for k in range(3):
        rows = last[k * SEGS : (k + 1) * SEGS]
        xpad_ref[k * SEGS : (k + 1) * SEGS, :] = jnp.concatenate(
            [halo[k : k + 1], rows[: SEGS - 1]], axis=0
        )

    def chunk(c, carry):
        prod, state, start = carry
        base = pl.multiple_of(c * ROWS, ROWS)
        first = pl.multiple_of(c * SPAN, SPAN)
        x = by_step(buf_ref, shuffle, first)
        d = by_step(buf_ref, shuffle, steps + first)
        xpad_ref[pl.ds(base + 3 * SEGS, ROWS), :] = x
        conv = cbias + taps[0:1] * x
        for k in range(1, 4):
            conv = conv + taps[k : k + 1] * xpad_ref[pl.ds(base + (3 - k) * SEGS, ROWS), :]
        conv_b = conv.astype(BF16)
        conv_ref[pl.ds(base, ROWS), :] = conv_b
        conv_v = conv_b.astype(F32)
        pre = dot(conv_b, w_ref[...])
        r = sigmoid(pre[:, :block] + bias[0:1])
        i = sigmoid(pre[:, block:] + bias[1:2])
        decay = r * rate8
        a = jnp.exp(-decay)
        q = one_minus_square(a, decay)
        m = q * lax.rsqrt(jnp.maximum(q, 1e-37))
        r_ref[pl.ds(base, ROWS), :] = r
        i_ref[pl.ds(base, ROWS), :] = i
        a_ref[pl.ds(base, ROWS), :] = a
        m_ref[pl.ds(base, ROWS), :] = m
        normed = conv_v * i * m
        for s in range(SPAN):
            rows = slice(s * SEGS, (s + 1) * SEGS)
            prod = prod * a[rows]
            state = a[rows] * state + normed[rows]
            start = start + prod * d[rows]
        return prod, state, start

    zero = jnp.zeros((SEGS, block), F32)
    prod, state, start = lax.fori_loop(0, steps // SPAN, chunk, (zero + 1.0, zero, zero), unroll=UNROLL[0])
    seg_ref[0:SEGS, :] = prod
    seg_ref[SEGS : 2 * SEGS, :] = state
    seg_ref[2 * SEGS : 3 * SEGS, :] = start
    whole, end, begin = prod[0:1], state[0:1], start[SEGS - 1 : SEGS]
    for s in range(1, SEGS):
        whole = whole * prod[s : s + 1]
        end = prod[s : s + 1] * end + state[s : s + 1]
        back = SEGS - 1 - s
        begin = start[back : back + 1] + prod[back : back + 1] * begin
    summary = jnp.concatenate([whole, end, begin, begin], axis=0)
    for k in range(sum_ref.shape[0]):
        sum_ref[k] = summary


def backward_kernel(
    steps, shards, at_ref, buf_ref, all_ref, seg_ref, conv_ref, r_ref, i_ref, a_ref, m_ref, xpad_ref, w_ref, decay_ref,
    gc_ref, wg_ref, rows_ref,
    prev_ref, gates_ref,
):
    block = w_ref.shape[0]
    shuffle = shuffle_matrix()
    mine = at_ref[0]
    decay = decay_ref[:, pl.ds(pl.multiple_of(at_ref[1] * block, block), block)]
    rate = jax.nn.softplus(-decay)
    entering = jnp.zeros((1, block), F32)
    carry_in = jnp.zeros((1, block), F32)
    for k in range(shards):
        part = all_ref[k]
        entering = jnp.where(k < mine, part[0:1] * entering + part[1:2], entering)
        back = shards - 1 - k
        part = all_ref[back]
        carry_in = jnp.where(back > mine, part[0:1] * carry_in + part[2:3], carry_in)
    heads, tails = [entering], [carry_in]
    for s in range(SEGS - 1):
        heads.append(seg_ref[s : s + 1] * heads[-1] + seg_ref[SEGS + s : SEGS + s + 1])
        back = SEGS - 1 - s
        tails.append(seg_ref[2 * SEGS + back : 2 * SEGS + back + 1] + seg_ref[back : back + 1] * tails[-1])
    state = jnp.concatenate(heads, axis=0)
    carry = jnp.concatenate(tails[::-1], axis=0)

    def ahead(c, state):
        rows = pl.ds(pl.multiple_of(c * ROWS, ROWS), ROWS)
        a, m = a_ref[rows, :], m_ref[rows, :]
        ci = conv_ref[rows, :].astype(F32) * i_ref[rows, :]
        normed = ci * m
        before = []
        for s in range(SPAN):
            at = slice(s * SEGS, (s + 1) * SEGS)
            before.append(state)
            state = a[at] * state + normed[at]
        direct = ci * a * lax.rsqrt(jnp.maximum(m * m, QFLOOR))
        prev_ref[rows, :] = a * (jnp.concatenate(before, axis=0) - direct)
        return state

    lax.fori_loop(0, steps // SPAN, ahead, state, unroll=UNROLL[1])

    def folded(v):
        return jnp.sum(v.reshape(SPAN, SEGS, block), axis=0)

    def back(k, held):
        carry, totals = held
        c = steps // SPAN - 1 - k
        base = pl.multiple_of(c * ROWS, ROWS)
        rows = pl.ds(base, ROWS)
        d = by_step(buf_ref, shuffle, steps + pl.multiple_of(c * SPAN, SPAN))
        a = a_ref[rows, :]
        grads = [None] * SPAN
        for s in range(SPAN - 1, -1, -1):
            at = slice(s * SEGS, (s + 1) * SEGS)
            grads[s] = d[at] + carry
            carry = a[at] * grads[s]
        g = jnp.concatenate(grads, axis=0)
        r, i = r_ref[rows, :], i_ref[rows, :]
        glr = g * prev_ref[rows, :] * (8.0 * r)
        gpr = (glr * ((r - 1.0) * rate)).astype(BF16)
        gim = g * (i * m_ref[rows, :])
        gpi = (gim * (conv_ref[rows, :].astype(F32) * (1.0 - i))).astype(BF16)
        both = jnp.concatenate([gpr, gpi], axis=1)
        gates_ref[rows, :] = both
        gc = gim + dot(both, w_ref[...], ((1,), (1,)))
        gc_ref[rows, :] = gc
        new = [folded(gc * xpad_ref[pl.ds(base + (3 - k) * SEGS, ROWS), :]) for k in range(4)]
        new += [folded(gc), folded(gpr.astype(F32)), folded(gpi.astype(F32)), folded(glr)]
        return carry, tuple(t + n for t, n in zip(totals, new, strict=True))

    zero = jnp.zeros((SEGS, block), F32)
    _, totals = lax.fori_loop(0, steps // SPAN, back, (carry, (zero,) * 8), unroll=UNROLL[2])
    sums = [jnp.sum(t, axis=0, keepdims=True) for t in totals]
    sums[7] = sums[7] * jax.nn.sigmoid(-decay)
    rows_ref[...] = jnp.concatenate(sums, axis=0)
    wg = dot(conv_ref[...], gates_ref[...], ((0,), (0,)))
    for s in range(SEGS):
        for q in range(4):
            for p in range(2):
                row = p * (block // 2) + s * 16
                tile = wg[row : row + 16, q * 128 : (q + 1) * 128]
                wg_ref[s * 4 + q, p * 16 : (p + 1) * 16, :] = tile.astype(BF16)


def taps_kernel(steps, at_ref, gc_ref, head_ref, taps_ref, ig_ref, tail_ref):
    block = gc_ref.shape[1]
    shuffle = shuffle_matrix()
    taps = taps_ref[:, pl.ds(pl.multiple_of(at_ref[1] * block, block), block)]
    final = steps // SPAN - 1
    tail_ref[:ROWS, :] = gc_ref[final * ROWS :, :]
    for k in range(3):
        rows = gc_ref[k * SEGS + 1 : (k + 1) * SEGS, :]
        tail_ref[ROWS + k * SEGS : ROWS + (k + 1) * SEGS, :] = jnp.concatenate([rows, head_ref[k : k + 1, :]], axis=0)

    def put(ref, base, first):
        xgrad = taps[0:1] * ref[pl.ds(base, ROWS), :]
        for k in range(1, 4):
            xgrad = xgrad + taps[k : k + 1] * ref[pl.ds(base + k * SEGS, ROWS), :]
        tiles = dot(shuffle, xgrad.astype(BF16), ((0,), (0,))).astype(BF16)
        for s in range(SEGS):
            ig_ref[s, pl.ds(first, SPAN), :] = tiles[s * SPAN : (s + 1) * SPAN]

    def turn(c, _):
        put(gc_ref, pl.multiple_of(c * ROWS, ROWS), pl.multiple_of(c * SPAN, SPAN))
        return 0

    lax.fori_loop(0, final, turn, 0, unroll=UNROLL[3])
    put(tail_ref, 0, final * SPAN)


def unpack_kernel(steps, got_ref, ig_ref, rows_ref):
    block = got_ref.shape[2]
    for b in range(SEGS):
        ig_ref[0, :, b * block : (b + 1) * block] = got_ref[b, :steps, :]
        pair = got_ref[b, steps : steps + 2 * SEGS, :].astype(F32)
        row = pair[:SEGS] + pair[SEGS:]
        for k in range(SEGS):
            rows_ref[b : b + 1, k * block : (k + 1) * block] = row[k : k + 1]


def split(v):
    high = lax.reduce_precision(v, 8, 7)
    return high.astype(BF16), (v - high).astype(BF16)


def joined(high, low):
    return high.astype(F32) + low.astype(F32)


def per_device(
    shards, docs, block_input, state_cotangent, recur_weight, input_weight, gate_bias, conv_taps, conv_bias, decay_param
):
    steps, width = block_input.shape[1:]
    block = recur_weight.shape[1]
    share = recur_weight.shape[0]
    z, j = lax.axis_index("z"), lax.axis_index("j")
    at = jnp.stack([z, j]).astype(jnp.int32)
    params = (gate_bias, conv_taps, conv_bias[None], decay_param[None])

    weights = jnp.concatenate([recur_weight, input_weight], axis=0)
    weights = jnp.broadcast_to(weights[None], (shards, 2 * share, block))
    weights = lax.all_to_all(weights, "z", 0, 0).reshape(SEGS, 4 * share, block)
    halo = lax.ppermute(block_input[0, steps - 3 :], "z", [(k, k + 1) for k in range(shards - 1)])
    halo = jnp.pad(halo, ((0, 13), (0, 0)))
    tokens = (block_input[0], state_cotangent[0], halo)
    xs, ds, halo = (v.reshape(-1, SEGS, block).transpose(1, 0, 2) for v in tokens)
    buf = lax.all_to_all(jnp.concatenate([xs, ds, weights, halo], axis=1), "j", 0, 0)

    total = SEGS * steps
    smem = pl.BlockSpec(memory_space=pltpu.SMEM)
    vmem = pl.BlockSpec(memory_space=pltpu.VMEM)
    shape = jax.ShapeDtypeStruct
    limit = pltpu.CompilerParams(vmem_limit_bytes=12 * 1024 * 1024)
    cost = pl.CostEstimate(flops=200 * total * block, bytes_accessed=12 * total * block, transcendentals=0)
    full, half = pltpu.VMEM((total, block), F32), pltpu.VMEM((total, block), BF16)

    def call(kernel, name, out_shape, operands, scratch=()):
        return pl.pallas_call(
            kernel,
            out_shape=out_shape,
            in_specs=[smem] + [vmem] * (len(operands) - 1),
            out_specs=(vmem,) * len(out_shape),
            scratch_shapes=scratch,
            compiler_params=limit,
            cost_estimate=cost,
            name=name,
        )(*operands)

    conv, r, i, a, m, xpad, seg, summary, w = call(
        functools.partial(forward_kernel, steps),
        "forward",
        (half, full, full, full, full, pltpu.VMEM((total + 3 * SEGS, block), F32), shape((3 * SEGS, block), F32))
        + (shape((shards, 4, block), F32), shape((block, 2 * block), BF16)),
        (at, buf, *params),
    )
    everyone = lax.all_to_all(summary, "z", 0, 0)
    gc, wg, rows = call(
        functools.partial(backward_kernel, steps, shards),
        "backward",
        (full, shape((4 * SEGS, 32, 128), BF16), shape((8, block), F32)),
        (at, buf, everyone, seg, conv, r, i, a, m, xpad, w, params[3]),
        [pltpu.VMEM((total, block), F32), pltpu.VMEM((total, 2 * block), BF16)],
    )
    head = gc[: 3 * SEGS].reshape(3, SEGS, block)[:, 0]
    head = lax.ppermute(head, "z", [(k + 1, k) for k in range(shards - 1)])
    (ig,) = call(
        functools.partial(taps_kernel, steps),
        "taps",
        (shape((SEGS, steps, block), BF16),),
        (at, gc, head, conv_taps),
        [pltpu.VMEM((ROWS + 3 * SEGS, block), F32)],
    )

    quarter = block // docs
    packed = jnp.concatenate(split(rows.reshape(SEGS * docs, 1, quarter)), axis=2)
    got = lax.all_to_all(jnp.concatenate([wg, packed], axis=1), ("j", "doc"), 0, 0)
    got = got.reshape(SEGS, docs, 33, 128)
    wsum = jnp.sum(got[:, :, :32].astype(F32), axis=1).reshape(shards, 16, 128)
    csum = jnp.sum(joined(got[:, :, 32, :quarter], got[:, :, 32, quarter:]), axis=1)
    csum = jnp.broadcast_to(csum.reshape(1, 4, 128), (shards, 4, 128))
    got = lax.all_to_all(jnp.concatenate((wsum.astype(BF16),) + split(csum), axis=1), "z", 0, 0)
    wsum = jnp.sum(got[:, :16].astype(F32), axis=0)
    csum = jnp.sum(joined(got[:, 16:20], got[:, 20:]), axis=0)
    send, ig = lax.optimization_barrier((jnp.concatenate([wsum, csum], axis=0), ig))
    got = lax.all_to_all(jnp.broadcast_to(send[None], (docs, 20, 128)), "doc", 0, 0)
    wgrads = got[:, :16].reshape(2, 2, 16, 128).transpose(0, 2, 1, 3).reshape(2, 16, block)
    csum = got[:, 16:].reshape(docs, SEGS, quarter).transpose(1, 0, 2).reshape(SEGS, block)
    csum = jnp.broadcast_to(jnp.concatenate(split(csum), axis=0)[None], (SEGS, 2 * SEGS, block))
    got = lax.all_to_all(jnp.concatenate([ig, csum], axis=1), "j", 0, 0)
    input_grad, channel_grads = pl.pallas_call(
        functools.partial(unpack_kernel, steps),
        out_shape=(shape((1, steps, width), BF16), shape((SEGS, width), F32)),
        in_specs=[vmem],
        out_specs=(vmem,) * 2,
        compiler_params=limit,
        name="unpack",
    )(got)
    return input_grad, wgrads[0], wgrads[1], channel_grads


def solution(mesh):
    seq, docs = mesh.shape["seq"], mesh.shape["doc"]
    shards = seq // SEGS
    fine = Mesh(mesh.devices.reshape(shards, SEGS, docs), ("z", "j", "doc"))
    tokens, rows = P("doc", ("z", "j"), None), P(("z", "j"), None)
    return jax.shard_map(
        functools.partial(per_device, shards, docs),
        mesh=fine,
        in_specs=(tokens, tokens, rows, rows, P(), P(), P(), P()),
        out_specs=(tokens, rows, rows, P()),
        check_vma=False,
    )
```

time: 153 us -> 146 us (0.954)
  blocking collectives: 33.2 us -> 40.1 us
  waiting for transfers between devices: 49.6 us -> 44.5 us
  starting transfers between devices: 47.1 us -> 42.5 us
  Pallas kernels: 12.1 us -> 8.4 us
    all_to_all x1 -> x2, blocking collectives: 16.4 us -> 23.4 us  [the longest x1 16.6 us: per_device(): everyone = lax.all_to_all(summary, 'z', 0, 0)]
    all_to_all x1 -> x0, waiting for transfers between devices: 4.2 us -> none  [per_device(): lax.all_to_all(jnp.broadcast_to(send[None], (docs, 20, 128)), 'doc', 0, 0)]
    pallas_call x2 -> x3, Pallas kernels: 11.2 us -> 7.52 us  [call(): pl.pallas_call(kernel, out_shape=out_shape, in_specs=[smem] + [vmem] * (l...]
    all_to_all x1 -> x0, starting transfers between devices: 3.27 us -> none  [per_device(): lax.all_to_all(jnp.broadcast_to(send[None], (docs, 20, 128)), 'doc', 0, 0)]
    all_to_all x1, waiting for transfers between devices: 3.77 us -> 6.99 us  [per_device(): weights = lax.all_to_all(weights, 'z', 0, 0).reshape(SEGS, 4 * share, block)]
    ppermute x2, waiting for transfers between devices: 6.65 us -> 3.44 us  [the longest x1 3.43 us: per_device(): head = lax.ppermute(head, 'z', [(k + 1, k) for k in range(shards - 1)])]
  transfers between devices with their start and end apart: 7 -> 6, of which waited for: 7 -> 5; matrix products, arithmetic and copies ran while one was open for 3% -> 2% of each run, Pallas kernels for 0% -> 1%
where the time goes in v3:
time: 146 us; the launch traced here: 145 us
  waiting for transfers between devices  44.5 us (30%)
  starting transfers between devices  42.5 us (29%)
  blocking collectives  40.1 us (27%)
  Pallas kernels  8.4 us (6%)
  local copies, waits for them, and re-layouts  4.58 us (3%)
  other arithmetic  3.88 us (3%)
    all_to_all x1, waiting for transfers between devices, per_device(): lax.all_to_all(jnp.concatenate([xs, ds, weights, halo], axis=1), 'j', 0, 0)  18.5 us
    all_to_all x1, blocking collectives, per_device(): lax.all_to_all(jnp.concatenate([wg, packed], axis=1), ('j', 'doc'), 0, 0)  16.8 us
    all_to_all x1, blocking collectives, per_device(): everyone = lax.all_to_all(summary, 'z', 0, 0)  16.6 us
    all_to_all x1, starting transfers between devices, per_device(): weights = lax.all_to_all(weights, 'z', 0, 0).reshape(SEGS, 4 * share, block)  15.7 us
    all_to_all x1, starting transfers between devices, per_device(): lax.all_to_all(jnp.concatenate([xs, ds, weights, halo], axis=1), 'j', 0, 0)  11.3 us
    all_to_all x1, waiting for transfers between devices, per_device(): got = lax.all_to_all(jnp.concatenate([ig, csum], axis=1), 'j', 0, 0)  9.54 us
    pallas_call x3, Pallas kernels, call(): pl.pallas_call(kernel, out_shape=out_shape, in_specs=[smem] + [vmem] * (l...  7.52 us
    all_to_all x1, starting transfers between devices, per_device(): got = lax.all_to_all(jnp.concatenate([ig, csum], axis=1), 'j', 0, 0)  7.38 us
  transfers between devices with their start and end apart: 6, of which 5 were waited for; matrix products, arithmetic and copies ran while one was open for 2% of the time, Pallas kernels for 1%

profile of v3, /device:TPU:1, one launch (start us, length us, event | category | flops | bytes accessed | tf_op | source)
XLA Modules:
  0.0 144.8 jit_solution(14766301219028479833)
XLA Ops:
  0.6 0.0 copy-start.4
  0.6 0.8 pad_maximum_fusion.3
  1.4 0.7 broadcast_in_dim.16
  2.1 15.7 %all-to-all-start = ((bf16[16,32,256]{2,1,0:T(8,128)(2,1)}), bf16[16,32,256]{2,1,0:T(8,128)(2,1)S(1)}, u32[]{:S(2)}, u32[]{:S(2)}) async-start(bf16[16,32,256]{2,1,0:T(8,128)(2,1)} %broadcast_in_dim.16), calls=%async_computation | async-start | bytes 524288 | tf_op jit(solution)/shard_map/all_to_all | solution.py:269
  17.9 0.8 slice_bitcast_fusion.1
  18.7 3.3 %collective-permute-start = (bf16[3,2048]{1,0:T(4,128)(2,1)S(1)}, bf16[3,2048]{1,0:T(4,128)(2,1)S(1)}, u32[]{:S(2)}, u32[]{:S(2)}) collective-permute-start(bf16[3,2048]{1,0:T(4,128)(2,1)S(1)} %slice_bitcast_fusion.1), channel_id=1, source_target_pairs={{0,32},{32,64},{64,96},{96,128},{128,160},{160,192},{192,224},{224... | collective-permute-start | bytes 36872 | tf_op jit(solution)/shard_map/ppermute | solution.py:270
  21.9 1.3 copy.57
  23.3 0.0 copy-done.4
  23.3 0.3 copy.59
  23.6 0.2 copy.60
  23.8 0.2 copy.58
  24.0 0.0 collective-permute-done
  24.0 7.0 %all-to-all-done = bf16[16,32,256]{2,1,0:T(8,128)(2,1)S(1)} async-done(((bf16[16,32,256]{2,1,0:T(8,128)(2,1)}), bf16[16,32,256]{2,1,0:T(8,128)(2,1)S(1)}, u32[]{:S(2)}, u32[]{:S(2)}) %all-to-all-start) | async-done | bytes 262176 | tf_op jit(solution)/shard_map/all_to_all | solution.py:269
  31.0 1.2 pad_maximum_fusion
  32.2 0.0 copy-start
  32.2 0.0 copy-start.1
  32.2 0.0 copy-start.2
  32.2 0.0 copy-start.3
  32.2 11.3 %all-to-all-start.1 = ((bf16[8,336,256]{2,1,0:T(8,128)(2,1)}), bf16[8,336,256]{2,1,0:T(8,128)(2,1)S(1)}, u32[]{:S(2)}, u32[]{:S(2)}) async-start(bf16[8,336,256]{2,1,0:T(8,128)(2,1)} %pad_maximum_fusion), calls=%async_computation.1 | async-start | bytes 2752512 | tf_op jit(solution)/shard_map/all_to_all | solution.py:274
  43.5 0.1 pad_add_fusion.at_ref
  43.6 18.5 %all-to-all-done.1.buf_ref = bf16[8,336,256]{2,1,0:T(8,128)(2,1)S(1)} async-done(((bf16[8,336,256]{2,1,0:T(8,128)(2,1)}), bf16[8,336,256]{2,1,0:T(8,128)(2,1)S(1)}, u32[]{:S(2)}, u32[]{:S(2)}) %all-to-all-start.1) | async-done | bytes 1376288 | tf_op jit(solution)/shard_map/all_to_all | solution.py:274
  62.1 0.0 copy-done
  62.1 0.0 copy-done.1
  62.1 0.0 copy-done.2
  62.1 0.0 copy-done.3
  62.2 3.6 %forward.1 = (bf16[1024,256]{1,0:T(8,128)(2,1)S(1)}, f32[1024,256]{1,0:T(8,128)S(1)}, f32[1024,256]{1,0:T(8,128)S(1)}, f32[1024,256]{1,0:T(8,128)S(1)}, f32[1024...) custom-call(s32[2]{0:T(128)S(1)} %pad_add_fusion.at_ref, ...), custom_call_target="tpu_custom_call" | custom-call | flops 52428800 | bytes 3145728 | tf_op jit(solution)/shard_map/forward/pallas_call | solution.py:285
  65.7 16.6 %all_to_all.35.all_ref = f32[16,4,256]{2,1,0:T(4,128)S(1)} all-to-all(f32[16,4,256]{2,1,0:T(4,128)S(1)} %get-tuple-element.20), channel_id=1, replica_groups=mesh['z'=16,'j'=8,'doc'=4] {'z'}, dimensions={0} | all-to-all | bytes 131072 | tf_op jit(solution)/shard_map/all_to_all | solution.py:303
  82.3 2.9 %backward.1 = (f32[1024,256]{1,0:T(8,128)S(1)}, bf16[32,32,128]{2,1,0:T(8,128)(2,1)S(1)}, f32[8,256]{1,0:T(8,128)S(1)}) custom-call(s32[2]{0:T(128)S(1)} %pad_add_fusion.at_ref, bf16[8,336,256]{2,1,0:T(8,128)(2,1)S(1)} %all-to-all-done.1.buf_ref, f32[16,4,256]{2,1,0:T(4,128)S(1)} %all_to_all.35.all_ref, f32[24,256]{1,0:T(8,128)S(1)} %get-tuple-element.21.seg_ref, ...), custom_call_target="tpu_custom_call" | custom-call | flops 52428800 | bytes 3145728 | tf_op jit(solution)/shard_map/backward/pallas_call | solution.py:285
  85.3 0.1 reshape.85
  85.4 0.1 maximum_maximum_fusion
  85.5 16.8 %all_to_all.36 = bf16[32,33,128]{2,1,0:T(8,128)(2,1)S(1)} all-to-all(bf16[32,33,128]{2,1,0:T(8,128)(2,1)S(1)} %maximum_maximum_fusion), channel_id=1, replica_groups=mesh['z'=16,'j'=8,'doc'=4] {'j','doc'}, dimensions={0} | all-to-all | bytes 540672 | tf_op jit(solution)/shard_map/all_to_all | solution.py:323
  102.3 0.1 fusion.1
  102.4 0.1 broadcast_in_dim.36
  102.6 0.7 pad_maximum_fusion.2
  103.2 3.5 %all-to-all-start.4 = ((bf16[16,24,128]{2,1,0:T(8,128)(2,1)}), bf16[16,24,128]{2,1,0:T(8,128)(2,1)S(1)}, u32[]{:S(2)}, u32[]{:S(2)}) async-start(bf16[16,24,128]{2,1,0:T(8,128)(2,1)} %pad_maximum_fusion.2), calls=%async_computation.4 | async-start | bytes 196608 | tf_op jit(solution)/shard_map/all_to_all | solution.py:328
  106.8 1.3 collective-permute-start.1
  108.1 3.4 %collective-permute-done.1.head_ref = f32[3,256]{1,0:T(4,128)S(1)} collective-permute-done((f32[3,256]{1,0:T(4,128)S(1)}, f32[3,256]{1,0:T(4,128)S(1)}, u32[]{:S(2)}, u32[]{:S(2)}) %collective-permute-start.1) | collective-permute-done | bytes 3104 | tf_op jit(solution)/shard_map/ppermute | solution.py:312
  111.5 1.0 taps.1
  112.5 5.9 %all-to-all-done.4 = bf16[16,24,128]{2,1,0:T(8,128)(2,1)S(1)} async-done(((bf16[16,24,128]{2,1,0:T(8,128)(2,1)}), bf16[16,24,128]{2,1,0:T(8,128)(2,1)S(1)}, u32[]{:S(2)}, u32[]{:S(2)}) %all-to-all-start.4) | async-done | bytes 98336 | tf_op jit(solution)/shard_map/all_to_all | solution.py:328
  118.6 6.7 %all_to_all.37 = f32[4,20,128]{2,1,0:T(8,128)S(1)} all-to-all(f32[4,20,128]{2,1,0:T(8,128)S(1)} %broadcast_in_dim.39), channel_id=1, replica_groups=mesh['z'=16,'j'=8,'doc'=4] {'doc'}, dimensions={0} | all-to-all | bytes 81920 | tf_op jit(solution)/shard_map/all_to_all | solution.py:332
  125.3 0.1 reshape.88
  125.4 0.1 reshape.89
  125.5 0.8 pad_maximum_fusion.1
  126.4 7.4 %all-to-all-start.6 = ((bf16[8,144,256]{2,1,0:T(8,128)(2,1)}), bf16[8,144,256]{2,1,0:T(8,128)(2,1)S(1)}, u32[]{:S(2)}, u32[]{:S(2)}) async-start(bf16[8,144,256]{2,1,0:T(8,128)(2,1)} %pad_maximum_fusion.1), calls=%async_computation.6 | async-start | bytes 1179648 | tf_op jit(solution)/shard_map/all_to_all | solution.py:336
  133.8 0.6 copy_bitcast_fusion
  134.4 9.5 %all-to-all-done.6.got_ref = bf16[8,144,256]{2,1,0:T(8,128)(2,1)S(1)} async-done(((bf16[8,144,256]{2,1,0:T(8,128)(2,1)}), bf16[8,144,256]{2,1,0:T(8,128)(2,1)S(1)}, u32[]{:S(2)}, u32[]{:S(2)}) %all-to-all-start.6) | async-done | bytes 589856 | tf_op jit(solution)/shard_map/all_to_all | solution.py:336
  144.0 0.9 unpack.1
  (25 shorter events, 0.3 us)
Async XLA Ops:
  0.6 22.6 %copy-start.4 = (bf16[1,128,2048]{2,1,0:T(8,128)(2,1)S(1)}, bf16[1,128,2048]{2,1,0:T(8,128)(2,1)}, u32[]{:S(2)}) copy-start(bf16[1,128,2048]{2,1,0:T(8,128)(2,1)} %param.9) | copy-start | bytes 1572868
  2.1 28.9 %all-to-all-start = ((bf16[16,32,256]{2,1,0:T(8,128)(2,1)}), bf16[16,32,256]{2,1,0:T(8,128)(2,1)S(1)}, u32[]{:S(2)}, u32[]{:S(2)}) async-start(bf16[16,32,256]{2,1,0:T(8,128)(2,1)} %broadcast_in_dim.16), calls=%async_computation | async-start | bytes 524288 | tf_op jit(solution)/shard_map/all_to_all | solution.py:269
  18.7 5.3 %collective-permute-start = (bf16[3,2048]{1,0:T(4,128)(2,1)S(1)}, bf16[3,2048]{1,0:T(4,128)(2,1)S(1)}, u32[]{:S(2)}, u32[]{:S(2)}) collective-permute-start(bf16[3,2048]{1,0:T(4,128)(2,1)S(1)} %slice_bitcast_fusion.1), channel_id=1, source_target_pairs={{0,32},{32,64},{64,96},{96,128},{128,160},{160,192},{192,224},{224... | collective-permute-start | bytes 36872 | tf_op jit(solution)/shard_map/ppermute | solution.py:270
  32.2 29.9 %copy-start = (f32[4,2048]{1,0:T(4,128)S(1)}, f32[4,2048]{1,0:T(4,128)}, u32[]{:S(2)}) copy-start(f32[4,2048]{1,0:T(4,128)} %taps_ref.3) | copy-start | bytes 98308
  32.2 29.9 %copy-start.1 = (f32[2048]{0:T(1024)S(1)}, f32[2048]{0:T(1024)}, u32[]{:S(2)}) copy-start(f32[2048]{0:T(1024)} %param.15) | copy-start | bytes 24580
  32.2 29.9 %copy-start.2 = (f32[2,2048]{1,0:T(2,128)S(1)}, f32[2,2048]{1,0:T(2,128)}, u32[]{:S(2)}) copy-start(f32[2,2048]{1,0:T(2,128)} %bias_ref.1) | copy-start | bytes 49156
  32.2 29.9 %copy-start.3 = (f32[2048]{0:T(1024)S(1)}, f32[2048]{0:T(1024)}, u32[]{:S(2)}) copy-start(f32[2048]{0:T(1024)} %param.14) | copy-start | bytes 24580
  32.2 29.9 %all-to-all-start.1 = ((bf16[8,336,256]{2,1,0:T(8,128)(2,1)}), bf16[8,336,256]{2,1,0:T(8,128)(2,1)S(1)}, u32[]{:S(2)}, u32[]{:S(2)}) async-start(bf16[8,336,256]{2,1,0:T(8,128)(2,1)} %pad_maximum_fusion), calls=%async_computation.1 | async-start | bytes 2752512 | tf_op jit(solution)/shard_map/all_to_all | solution.py:274
  103.2 15.3 %all-to-all-start.4 = ((bf16[16,24,128]{2,1,0:T(8,128)(2,1)}), bf16[16,24,128]{2,1,0:T(8,128)(2,1)S(1)}, u32[]{:S(2)}, u32[]{:S(2)}) async-start(bf16[16,24,128]{2,1,0:T(8,128)(2,1)} %pad_maximum_fusion.2), calls=%async_computation.4 | async-start | bytes 196608 | tf_op jit(solution)/shard_map/all_to_all | solution.py:328
  106.8 4.7 %collective-permute-start.1 = (f32[3,256]{1,0:T(4,128)S(1)}, f32[3,256]{1,0:T(4,128)S(1)}, u32[]{:S(2)}, u32[]{:S(2)}) collective-permute-start(f32[3,256]{1,0:T(4,128)S(1)} %bitcast.58), channel_id=1, source_target_pairs={{32,0},{64,32},{96,64},{128,96},{160,128},{192,160},{224,192},{256... | collective-permute-start | bytes 9224 | tf_op jit(solution)/shard_map/ppermute | solution.py:312
  126.4 17.6 %all-to-all-start.6 = ((bf16[8,144,256]{2,1,0:T(8,128)(2,1)}), bf16[8,144,256]{2,1,0:T(8,128)(2,1)S(1)}, u32[]{:S(2)}, u32[]{:S(2)}) async-start(bf16[8,144,256]{2,1,0:T(8,128)(2,1)} %pad_maximum_fusion.1), calls=%async_computation.6 | async-start | bytes 1179648 | tf_op jit(solution)/shard_map/all_to_all | solution.py:336

commit v4 on v3

--- a/solution.py
+++ b/solution.py
@@ -235,8 +235,11 @@
     put(tail_ref, 0, final * SPAN)
 
 
-def unpack_kernel(steps, got_ref, ig_ref, rows_ref):
+def unpack_kernel(steps, got_ref, tiles_ref, ig_ref, recur_ref, input_ref, rows_ref):
     block = got_ref.shape[2]
+    for half in range(2):
+        recur_ref[:, half * 128 : (half + 1) * 128] = tiles_ref[half, :16, :]
+        input_ref[:, half * 128 : (half + 1) * 128] = tiles_ref[2 + half, :16, :]
     for b in range(SEGS):
         ig_ref[0, :, b * block : (b + 1) * block] = got_ref[b, :steps, :]
         pair = got_ref[b, steps : steps + 2 * SEGS, :].astype(F32)
@@ -271,6 +274,7 @@
     halo = jnp.pad(halo, ((0, 13), (0, 0)))
     tokens = (block_input[0], state_cotangent[0], halo)
     xs, ds, halo = (v.reshape(-1, SEGS, block).transpose(1, 0, 2) for v in tokens)
+    at, weights = lax.optimization_barrier((at, weights))
     buf = lax.all_to_all(jnp.concatenate([xs, ds, weights, halo], axis=1), "j", 0, 0)
 
     total = SEGS * steps
@@ -310,14 +314,6 @@
     )
     head = gc[: 3 * SEGS].reshape(3, SEGS, block)[:, 0]
     head = lax.ppermute(head, "z", [(k + 1, k) for k in range(shards - 1)])
-    (ig,) = call(
-        functools.partial(taps_kernel, steps),
-        "taps",
-        (shape((SEGS, steps, block), BF16),),
-        (at, gc, head, conv_taps),
-        [pltpu.VMEM((ROWS + 3 * SEGS, block), F32)],
-    )
-
     quarter = block // docs
     packed = jnp.concatenate(split(rows.reshape(SEGS * docs, 1, quarter)), axis=2)
     got = lax.all_to_all(jnp.concatenate([wg, packed], axis=1), ("j", "doc"), 0, 0)
@@ -326,23 +322,30 @@
     csum = jnp.sum(joined(got[:, :, 32, :quarter], got[:, :, 32, quarter:]), axis=1)
     csum = jnp.broadcast_to(csum.reshape(1, 4, 128), (shards, 4, 128))
     got = lax.all_to_all(jnp.concatenate((wsum.astype(BF16),) + split(csum), axis=1), "z", 0, 0)
+    (ig,) = call(
+        functools.partial(taps_kernel, steps),
+        "taps",
+        (shape((SEGS, steps, block), BF16),),
+        (at, gc, head, conv_taps),
+        [pltpu.VMEM((ROWS + 3 * SEGS, block), F32)],
+    )
     wsum = jnp.sum(got[:, :16].astype(F32), axis=0)
     csum = jnp.sum(joined(got[:, 16:20], got[:, 20:]), axis=0)
     send, ig = lax.optimization_barrier((jnp.concatenate([wsum, csum], axis=0), ig))
-    got = lax.all_to_all(jnp.broadcast_to(send[None], (docs, 20, 128)), "doc", 0, 0)
-    wgrads = got[:, :16].reshape(2, 2, 16, 128).transpose(0, 2, 1, 3).reshape(2, 16, block)
-    csum = got[:, 16:].reshape(docs, SEGS, quarter).transpose(1, 0, 2).reshape(SEGS, block)
+    tiles = lax.all_to_all(jnp.broadcast_to(send[None], (docs, 20, 128)), "doc", 0, 0)
+    csum = tiles[:, 16:].reshape(docs, SEGS, quarter).transpose(1, 0, 2).reshape(SEGS, block)
     csum = jnp.broadcast_to(jnp.concatenate(split(csum), axis=0)[None], (SEGS, 2 * SEGS, block))
     got = lax.all_to_all(jnp.concatenate([ig, csum], axis=1), "j", 0, 0)
-    input_grad, channel_grads = pl.pallas_call(
+    return pl.pallas_call(
         functools.partial(unpack_kernel, steps),
-        out_shape=(shape((1, steps, width), BF16), shape((SEGS, width), F32)),
-        in_specs=[vmem],
-        out_specs=(vmem,) * 2,
+        out_shape=(
+            shape((1, steps, width), BF16), shape((share, block), F32), shape((share, block), F32), shape((SEGS, width), F32)
+        ),
+        in_specs=[vmem] * 2,
+        out_specs=(vmem,) * 4,
         compiler_params=limit,
         name="unpack",
-    )(got)
-    return input_grad, wgrads[0], wgrads[1], channel_grads
+    )(got, tiles)
 
 
 def solution(mesh):

time: 146 us -> 143 us (0.979)
  blocking collectives: 40.1 us -> 86.7 us
  waiting for transfers between devices: 44.5 us -> 16.3 us
  starting transfers between devices: 42.5 us -> 23.8 us
  other arithmetic: 3.88 us -> 1.98 us
    all_to_all x0 -> x2, blocking collectives: none -> 46.7 us  [the longest x1 30 us: per_device(): lax.all_to_all(jnp.concatenate([xs, ds, weights, halo], axis=1), 'j', 0, 0)]
    all_to_all x2 -> x0, waiting for transfers between devices: 28.1 us -> none  [the longest x1 18.5 us: per_device(): lax.all_to_all(jnp.concatenate([xs, ds, weights, halo], axis=1), 'j', 0, 0)]
    all_to_all x2 -> x0, starting transfers between devices: 18.7 us -> none  [the longest x1 11.3 us: per_device(): lax.all_to_all(jnp.concatenate([xs, ds, weights, halo], axis=1), 'j', 0, 0)]
  transfers between devices with their start and end apart: 6 -> 4, of which waited for: 5 -> 3; matrix products, arithmetic and copies ran while one was open for 2% -> 2% of each run, Pallas kernels for 1% -> 1%
where the time goes in v4:
time: 143 us; the launch traced here: 142 us
  blocking collectives  86.7 us (61%)
  starting transfers between devices  23.8 us (17%)
  waiting for transfers between devices  16.3 us (11%)
  Pallas kernels  8.38 us (6%)
  local copies, waits for them, and re-layouts  3.93 us (3%)
  other arithmetic  1.98 us (1%)
    all_to_all x1, blocking collectives, per_device(): lax.all_to_all(jnp.concatenate([xs, ds, weights, halo], axis=1), 'j', 0, 0)  30 us
    all_to_all x1, blocking collectives, per_device(): lax.all_to_all(jnp.concatenate([wg, packed], axis=1), ('j', 'doc'), 0, 0)  16.7 us
    all_to_all x1, blocking collectives, per_device(): got = lax.all_to_all(jnp.concatenate([ig, csum], axis=1), 'j', 0, 0)  16.7 us
    all_to_all x1, blocking collectives, per_device(): everyone = lax.all_to_all(summary, 'z', 0, 0)  16.6 us
    all_to_all x1, starting transfers between devices, per_device(): weights = lax.all_to_all(weights, 'z', 0, 0).reshape(SEGS, 4 * share, block)  15.7 us
    pallas_call x3, Pallas kernels, call(): pl.pallas_call(kernel, out_shape=out_shape, in_specs=[smem] + [vmem] * (l...  7.49 us
    all_to_all x1, waiting for transfers between devices, per_device(): weights = lax.all_to_all(weights, 'z', 0, 0).reshape(SEGS, 4 * share, block)  6.92 us
    all_to_all x1, blocking collectives, per_device(): lax.all_to_all(jnp.broadcast_to(send[None], (docs, 20, 128)), 'doc', 0, 0)  6.75 us
  transfers between devices with their start and end apart: 4, of which 3 were waited for; matrix products, arithmetic and copies ran while one was open for 2% of the time, Pallas kernels for 1%

profile of v4, /device:TPU:1, one launch (start us, length us, event | category | flops | bytes accessed | tf_op | source)
XLA Modules:
  0.0 142.0 jit_solution(4278900018803471093)
XLA Ops:
  0.6 0.0 copy-start.4
  0.6 0.8 pad_maximum_fusion.3
  1.4 0.7 broadcast_in_dim.16
  2.1 15.7 %all-to-all-start = ((bf16[16,32,256]{2,1,0:T(8,128)(2,1)}), bf16[16,32,256]{2,1,0:T(8,128)(2,1)S(1)}, u32[]{:S(2)}, u32[]{:S(2)}) async-start(bf16[16,32,256]{2,1,0:T(8,128)(2,1)} %broadcast_in_dim.16), calls=%async_computation | async-start | bytes 524288 | tf_op jit(solution)/shard_map/all_to_all | solution.py:272
  17.9 0.8 slice_bitcast_fusion.1
  18.7 3.3 %collective-permute-start = (bf16[3,2048]{1,0:T(4,128)(2,1)S(1)}, bf16[3,2048]{1,0:T(4,128)(2,1)S(1)}, u32[]{:S(2)}, u32[]{:S(2)}) collective-permute-start(bf16[3,2048]{1,0:T(4,128)(2,1)S(1)} %slice_bitcast_fusion.1), channel_id=1, source_target_pairs={{0,32},{32,64},{64,96},{96,128},{128,160},{160,192},{192,224},{224... | collective-permute-start | bytes 36872 | tf_op jit(solution)/shard_map/ppermute | solution.py:273
  22.0 0.1 pad_add_fusion.at_ref
  22.0 1.3 copy.43
  23.3 0.0 copy-done.4
  23.4 0.3 copy.45
  23.6 0.2 copy.46
  23.9 0.2 copy.44
  24.1 0.0 collective-permute-done
  24.1 6.9 %all-to-all-done = bf16[16,32,256]{2,1,0:T(8,128)(2,1)S(1)} async-done(((bf16[16,32,256]{2,1,0:T(8,128)(2,1)}), bf16[16,32,256]{2,1,0:T(8,128)(2,1)S(1)}, u32[]{:S(2)}, u32[]{:S(2)}) %all-to-all-start) | async-done | bytes 262176 | tf_op jit(solution)/shard_map/all_to_all | solution.py:272
  31.0 0.1 pad_maximum_fusion
  31.1 0.0 copy-start
  31.1 0.0 copy-start.1
  31.2 0.0 copy-start.2
  31.2 0.0 copy-start.3
  31.2 30.0 %all_to_all.35.buf_ref = bf16[8,336,256]{2,1,0:T(8,128)(2,1)S(1)} all-to-all(bf16[8,336,256]{2,1,0:T(8,128)(2,1)S(1)} %pad_maximum_fusion), channel_id=1, replica_groups=mesh['z'=16,'j'=8,'doc'=4] {'j'}, dimensions={0} | all-to-all | bytes 2752512 | tf_op jit(solution)/shard_map/all_to_all | solution.py:278
  61.2 0.0 copy-done
  61.2 0.0 copy-done.1
  61.2 0.0 copy-done.2
  61.2 0.0 copy-done.3
  61.2 3.5 %forward.1 = (bf16[1024,256]{1,0:T(8,128)(2,1)S(1)}, f32[1024,256]{1,0:T(8,128)S(1)}, f32[1024,256]{1,0:T(8,128)S(1)}, f32[1024,256]{1,0:T(8,128)S(1)}, f32[1024...) custom-call(s32[2]{0:T(128)S(1)} %pad_add_fusion.at_ref, ...), custom_call_target="tpu_custom_call" | custom-call | flops 52428800 | bytes 3145728 | tf_op jit(solution)/shard_map/forward/pallas_call | solution.py:289
  64.7 16.6 %all_to_all.36.all_ref = f32[16,4,256]{2,1,0:T(4,128)S(1)} all-to-all(f32[16,4,256]{2,1,0:T(4,128)S(1)} %get-tuple-element.22), channel_id=1, replica_groups=mesh['z'=16,'j'=8,'doc'=4] {'z'}, dimensions={0} | all-to-all | bytes 131072 | tf_op jit(solution)/shard_map/all_to_all | solution.py:307
  81.3 2.9 %backward.1 = (f32[1024,256]{1,0:T(8,128)S(1)}, bf16[32,32,128]{2,1,0:T(8,128)(2,1)S(1)}, f32[8,256]{1,0:T(8,128)S(1)}) custom-call(s32[2]{0:T(128)S(1)} %pad_add_fusion.at_ref, bf16[8,336,256]{2,1,0:T(8,128)(2,1)S(1)} %all_to_all.35.buf_ref, f32[16,4,256]{2,1,0:T(4,128)S(1)} %all_to_all.36.all_ref, f32[24,256]{1,0:T(8,128)S(1)} %get-tuple-element.23.seg_ref, ...), custom_call_target="tpu_custom_call" | custom-call | flops 52428800 | bytes 3145728 | tf_op jit(solution)/shard_map/backward/pallas_call | solution.py:289
  84.3 0.1 reshape.77
  84.4 0.1 maximum_maximum_fusion
  84.5 16.7 %all_to_all.37 = bf16[32,33,128]{2,1,0:T(8,128)(2,1)S(1)} all-to-all(bf16[32,33,128]{2,1,0:T(8,128)(2,1)S(1)} %maximum_maximum_fusion), channel_id=1, replica_groups=mesh['z'=16,'j'=8,'doc'=4] {'j','doc'}, dimensions={0} | all-to-all | bytes 540672 | tf_op jit(solution)/shard_map/all_to_all | solution.py:319
  101.2 0.1 fusion.1
  101.3 0.1 broadcast_in_dim.36
  101.4 0.7 pad_maximum_fusion.2
  102.1 3.5 %all-to-all-start.4 = ((bf16[16,24,128]{2,1,0:T(8,128)(2,1)}), bf16[16,24,128]{2,1,0:T(8,128)(2,1)S(1)}, u32[]{:S(2)}, u32[]{:S(2)}) async-start(bf16[16,24,128]{2,1,0:T(8,128)(2,1)} %pad_maximum_fusion.2), calls=%async_computation.4 | async-start | bytes 196608 | tf_op jit(solution)/shard_map/all_to_all | solution.py:324
  105.7 1.3 collective-permute-start.1
  107.0 3.4 %collective-permute-done.1.head_ref = f32[3,256]{1,0:T(4,128)S(1)} collective-permute-done((f32[3,256]{1,0:T(4,128)S(1)}, f32[3,256]{1,0:T(4,128)S(1)}, u32[]{:S(2)}, u32[]{:S(2)}) %collective-permute-start.1) | collective-permute-done | bytes 3104 | tf_op jit(solution)/shard_map/ppermute | solution.py:316
  110.4 1.0 taps.1
  111.4 5.9 %all-to-all-done.4 = bf16[16,24,128]{2,1,0:T(8,128)(2,1)S(1)} async-done(((bf16[16,24,128]{2,1,0:T(8,128)(2,1)}), bf16[16,24,128]{2,1,0:T(8,128)(2,1)S(1)}, u32[]{:S(2)}, u32[]{:S(2)}) %all-to-all-start.4) | async-done | bytes 98336 | tf_op jit(solution)/shard_map/all_to_all | solution.py:324
  117.4 6.7 %all_to_all.38.tiles_ref = f32[4,20,128]{2,1,0:T(8,128)S(1)} all-to-all(f32[4,20,128]{2,1,0:T(8,128)S(1)} %broadcast_in_dim.39), channel_id=1, replica_groups=mesh['z'=16,'j'=8,'doc'=4] {'doc'}, dimensions={0} | all-to-all | bytes 81920 | tf_op jit(solution)/shard_map/all_to_all | solution.py:335
  124.2 0.1 reshape.80
  124.3 0.1 reshape.81
  124.4 16.7 %all_to_all.39.got_ref = bf16[8,144,256]{2,1,0:T(8,128)(2,1)S(1)} all-to-all(bf16[8,144,256]{2,1,0:T(8,128)(2,1)S(1)} %pad_maximum_fusion.1), channel_id=1, replica_groups=mesh['z'=16,'j'=8,'doc'=4] {'j'}, dimensions={0} | all-to-all | bytes 1179648 | tf_op jit(solution)/shard_map/all_to_all | solution.py:338
  141.1 0.9 unpack.1
  (22 shorter events, 0.3 us)
Async XLA Ops:
  0.6 22.7 %copy-start.4 = (bf16[1,128,2048]{2,1,0:T(8,128)(2,1)S(1)}, bf16[1,128,2048]{2,1,0:T(8,128)(2,1)}, u32[]{:S(2)}) copy-start(bf16[1,128,2048]{2,1,0:T(8,128)(2,1)} %param.9) | copy-start | bytes 1572868
  2.1 28.9 %all-to-all-start = ((bf16[16,32,256]{2,1,0:T(8,128)(2,1)}), bf16[16,32,256]{2,1,0:T(8,128)(2,1)S(1)}, u32[]{:S(2)}, u32[]{:S(2)}) async-start(bf16[16,32,256]{2,1,0:T(8,128)(2,1)} %broadcast_in_dim.16), calls=%async_computation | async-start | bytes 524288 | tf_op jit(solution)/shard_map/all_to_all | solution.py:272
  18.7 5.4 %collective-permute-start = (bf16[3,2048]{1,0:T(4,128)(2,1)S(1)}, bf16[3,2048]{1,0:T(4,128)(2,1)S(1)}, u32[]{:S(2)}, u32[]{:S(2)}) collective-permute-start(bf16[3,2048]{1,0:T(4,128)(2,1)S(1)} %slice_bitcast_fusion.1), channel_id=1, source_target_pairs={{0,32},{32,64},{64,96},{96,128},{128,160},{160,192},{192,224},{224... | collective-permute-start | bytes 36872 | tf_op jit(solution)/shard_map/ppermute | solution.py:273
  31.1 30.1 %copy-start = (f32[4,2048]{1,0:T(4,128)S(1)}, f32[4,2048]{1,0:T(4,128)}, u32[]{:S(2)}) copy-start(f32[4,2048]{1,0:T(4,128)} %taps_ref.3) | copy-start | bytes 98308
  31.1 30.0 %copy-start.1 = (f32[2048]{0:T(1024)S(1)}, f32[2048]{0:T(1024)}, u32[]{:S(2)}) copy-start(f32[2048]{0:T(1024)} %param.15) | copy-start | bytes 24580
  31.2 30.0 %copy-start.2 = (f32[2,2048]{1,0:T(2,128)S(1)}, f32[2,2048]{1,0:T(2,128)}, u32[]{:S(2)}) copy-start(f32[2,2048]{1,0:T(2,128)} %bias_ref.1) | copy-start | bytes 49156
  31.2 30.0 %copy-start.3 = (f32[2048]{0:T(1024)S(1)}, f32[2048]{0:T(1024)}, u32[]{:S(2)}) copy-start(f32[2048]{0:T(1024)} %param.14) | copy-start | bytes 24580
  102.1 15.3 %all-to-all-start.4 = ((bf16[16,24,128]{2,1,0:T(8,128)(2,1)}), bf16[16,24,128]{2,1,0:T(8,128)(2,1)S(1)}, u32[]{:S(2)}, u32[]{:S(2)}) async-start(bf16[16,24,128]{2,1,0:T(8,128)(2,1)} %pad_maximum_fusion.2), calls=%async_computation.4 | async-start | bytes 196608 | tf_op jit(solution)/shard_map/all_to_all | solution.py:324
  105.7 4.7 %collective-permute-start.1 = (f32[3,256]{1,0:T(4,128)S(1)}, f32[3,256]{1,0:T(4,128)S(1)}, u32[]{:S(2)}, u32[]{:S(2)}) collective-permute-start(f32[3,256]{1,0:T(4,128)S(1)} %bitcast.46), channel_id=1, source_target_pairs={{32,0},{64,32},{96,64},{128,96},{160,128},{192,160},{224,192},{256... | collective-permute-start | bytes 9224 | tf_op jit(solution)/shard_map/ppermute | solution.py:316

commit v5 on v4

--- a/solution.py
+++ b/solution.py
@@ -43,14 +43,12 @@
 
 def one_minus_square(a, decay):
     x = 2.0 * decay
-    series = x * (1.0 - x * (1 / 2) * (1.0 - x * (1 / 3) * (1.0 - x * (1 / 4))))
-    return jnp.where(x < 0.0625, series, 1.0 - a * a)
+    series = x * (1.0 - x * (1 / 2) * (1.0 - x * (1 / 3)))
+    return jnp.where(x < 0.0078125, series, 1.0 - a * a)
 
 
 def sigmoid(x):
-    below = 1.0 + jnp.exp(-jnp.maximum(x, -80.0))
-    guess = pl.reciprocal(below, approx=True)
-    return guess * (2.0 - below * guess)
+    return pl.reciprocal(1.0 + jnp.exp(-x), approx=True)
 
 
 def block_params(at_ref, bias_ref, taps_ref, cbias_ref, decay_ref, block):
@@ -60,7 +58,7 @@
 
 
 def forward_kernel(
-    steps, at_ref, buf_ref, bias_ref, taps_ref, cbias_ref, decay_ref,
+    steps, at_ref, buf_ref, halo_ref, bias_ref, taps_ref, cbias_ref, decay_ref,
     conv_ref, r_ref, i_ref, a_ref, m_ref, xpad_ref, seg_ref, sum_ref, w_ref,
 ):
     block = w_ref.shape[0]
@@ -69,7 +67,7 @@
     bias, taps, cbias, rate = block_params(at_ref, bias_ref, taps_ref, cbias_ref, decay_ref, block)
     rate8 = 8.0 * rate
     last = by_step(buf_ref, shuffle, steps - SPAN)[ROWS - 3 * SEGS :]
-    halo = jnp.where(at_ref[0] > 0, buf_ref[SEGS - 1, 2 * steps + 64 : 2 * steps + 80, :].astype(F32), 0.0)
+    halo = jnp.where(at_ref[0] > 0, halo_ref[...], 0.0)
     for k in range(3):
         rows = last[k * SEGS : (k + 1) * SEGS]
         xpad_ref[k * SEGS : (k + 1) * SEGS, :] = jnp.concatenate(
@@ -119,7 +117,7 @@
         end = prod[s : s + 1] * end + state[s : s + 1]
         back = SEGS - 1 - s
         begin = start[back : back + 1] + prod[back : back + 1] * begin
-    summary = jnp.concatenate([whole, end, begin, begin], axis=0)
+    summary = jnp.concatenate([whole, end, begin], axis=1)
     for k in range(sum_ref.shape[0]):
         sum_ref[k] = summary
 
@@ -138,10 +136,10 @@
     carry_in = jnp.zeros((1, block), F32)
     for k in range(shards):
         part = all_ref[k]
-        entering = jnp.where(k < mine, part[0:1] * entering + part[1:2], entering)
+        entering = jnp.where(k < mine, part[:, :block] * entering + part[:, block : 2 * block], entering)
         back = shards - 1 - k
         part = all_ref[back]
-        carry_in = jnp.where(back > mine, part[0:1] * carry_in + part[2:3], carry_in)
+        carry_in = jnp.where(back > mine, part[:, :block] * carry_in + part[:, 2 * block :], carry_in)
     heads, tails = [entering], [carry_in]
     for s in range(SEGS - 1):
         heads.append(seg_ref[s : s + 1] * heads[-1] + seg_ref[SEGS + s : SEGS + s + 1])
@@ -271,11 +269,12 @@
     weights = jnp.broadcast_to(weights[None], (shards, 2 * share, block))
     weights = lax.all_to_all(weights, "z", 0, 0).reshape(SEGS, 4 * share, block)
     halo = lax.ppermute(block_input[0, steps - 3 :], "z", [(k, k + 1) for k in range(shards - 1)])
-    halo = jnp.pad(halo, ((0, 13), (0, 0)))
+    halo = jnp.pad(halo, ((0, 5), (0, 0)))
     tokens = (block_input[0], state_cotangent[0], halo)
     xs, ds, halo = (v.reshape(-1, SEGS, block).transpose(1, 0, 2) for v in tokens)
     at, weights = lax.optimization_barrier((at, weights))
     buf = lax.all_to_all(jnp.concatenate([xs, ds, weights, halo], axis=1), "j", 0, 0)
+    halo = buf[SEGS - 1, 2 * steps + 4 * share :].astype(F32)
 
     total = SEGS * steps
     smem = pl.BlockSpec(memory_space=pltpu.SMEM)
@@ -301,8 +300,8 @@
         functools.partial(forward_kernel, steps),
         "forward",
         (half, full, full, full, full, pltpu.VMEM((total + 3 * SEGS, block), F32), shape((3 * SEGS, block), F32))
-        + (shape((shards, 4, block), F32), shape((block, 2 * block), BF16)),
-        (at, buf, *params),
+        + (shape((shards, 1, 3 * block), F32), shape((block, 2 * block), BF16)),
+        (at, buf, halo, *params),
     )
     everyone = lax.all_to_all(summary, "z", 0, 0)
     gc, wg, rows = call(

time: 143 us -> 142 us (level)
  no operation moved by 1% of the time
where the time goes in v5:
time: 142 us; the launch traced here: 141 us
  blocking collectives  86.2 us (61%)
  starting transfers between devices  23.8 us (17%)
  waiting for transfers between devices  16.3 us (11%)
  Pallas kernels  8.06 us (6%)
  local copies, waits for them, and re-layouts  3.93 us (3%)
  other arithmetic  1.98 us (1%)
    all_to_all x1, blocking collectives, per_device(): lax.all_to_all(jnp.concatenate([xs, ds, weights, halo], axis=1), 'j', 0, 0)  29.8 us
    all_to_all x1, blocking collectives, per_device(): got = lax.all_to_all(jnp.concatenate([ig, csum], axis=1), 'j', 0, 0)  16.7 us
    all_to_all x1, blocking collectives, per_device(): everyone = lax.all_to_all(summary, 'z', 0, 0)  16.6 us
    all_to_all x1, blocking collectives, per_device(): lax.all_to_all(jnp.concatenate([wg, packed], axis=1), ('j', 'doc'), 0, 0)  16.4 us
    all_to_all x1, starting transfers between devices, per_device(): weights = lax.all_to_all(weights, 'z', 0, 0).reshape(SEGS, 4 * share, block)  15.7 us
    pallas_call x3, Pallas kernels, call(): pl.pallas_call(kernel, out_shape=out_shape, in_specs=[smem] + [vmem] * (l...  7.17 us
    all_to_all x1, waiting for transfers between devices, per_device(): weights = lax.all_to_all(weights, 'z', 0, 0).reshape(SEGS, 4 * share, block)  6.93 us
    all_to_all x1, blocking collectives, per_device(): lax.all_to_all(jnp.broadcast_to(send[None], (docs, 20, 128)), 'doc', 0, 0)  6.75 us
  transfers between devices with their start and end apart: 4, of which 3 were waited for; matrix products, arithmetic and copies ran while one was open for 2% of the time, Pallas kernels for 1%

profile of v5, /device:TPU:1, one launch (start us, length us, event | category | flops | bytes accessed | tf_op | source)
XLA Modules:
  0.0 141.2 jit_solution(14937205473400207400)
XLA Ops:
  0.6 0.0 copy-start.4
  0.6 0.8 pad_maximum_fusion.3
  1.4 0.7 broadcast_in_dim.16
  2.1 15.7 %all-to-all-start = ((bf16[16,32,256]{2,1,0:T(8,128)(2,1)}), bf16[16,32,256]{2,1,0:T(8,128)(2,1)S(1)}, u32[]{:S(2)}, u32[]{:S(2)}) async-start(bf16[16,32,256]{2,1,0:T(8,128)(2,1)} %broadcast_in_dim.16), calls=%async_computation | async-start | bytes 524288 | tf_op jit(solution)/shard_map/all_to_all | solution.py:270
  17.9 0.8 slice_bitcast_fusion.1
  18.7 3.3 %collective-permute-start = (bf16[3,2048]{1,0:T(4,128)(2,1)S(1)}, bf16[3,2048]{1,0:T(4,128)(2,1)S(1)}, u32[]{:S(2)}, u32[]{:S(2)}) collective-permute-start(bf16[3,2048]{1,0:T(4,128)(2,1)S(1)} %slice_bitcast_fusion.1), channel_id=1, source_target_pairs={{0,32},{32,64},{64,96},{96,128},{128,160},{160,192},{192,224},{224... | collective-permute-start | bytes 36872 | tf_op jit(solution)/shard_map/ppermute | solution.py:271
  22.0 0.1 pad_add_fusion.at_ref
  22.0 1.3 copy.40
  23.3 0.0 copy-done.4
  23.4 0.3 copy.42
  23.6 0.2 copy.43
  23.9 0.2 copy.41
  24.1 0.0 collective-permute-done
  24.1 6.9 %all-to-all-done = bf16[16,32,256]{2,1,0:T(8,128)(2,1)S(1)} async-done(((bf16[16,32,256]{2,1,0:T(8,128)(2,1)}), bf16[16,32,256]{2,1,0:T(8,128)(2,1)S(1)}, u32[]{:S(2)}, u32[]{:S(2)}) %all-to-all-start) | async-done | bytes 262176 | tf_op jit(solution)/shard_map/all_to_all | solution.py:270
  31.0 0.1 pad_maximum_fusion
  31.1 0.0 copy-start
  31.1 0.0 copy-start.1
  31.1 0.0 copy-start.2
  31.2 0.0 copy-start.3
  31.2 29.8 %all_to_all.35.buf_ref = bf16[8,328,256]{2,1,0:T(8,128)(2,1)S(1)} all-to-all(bf16[8,328,256]{2,1,0:T(8,128)(2,1)S(1)} %pad_maximum_fusion), channel_id=1, replica_groups=mesh['z'=16,'j'=8,'doc'=4] {'j'}, dimensions={0} | all-to-all | bytes 2686976 | tf_op jit(solution)/shard_map/all_to_all | solution.py:276
  61.0 0.0 copy-done
  61.0 0.0 copy-done.1
  61.0 0.0 copy-done.2
  61.0 0.0 copy-done.3
  61.0 3.2 %forward.1 = (bf16[1024,256]{1,0:T(8,128)(2,1)S(1)}, f32[1024,256]{1,0:T(8,128)S(1)}, f32[1024,256]{1,0:T(8,128)S(1)}, f32[1024,256]{1,0:T(8,128)S(1)}, f32[1024...) custom-call(s32[2]{0:T(128)S(1)} %pad_add_fusion.at_ref, ...), custom_call_target="tpu_custom_call" | custom-call | flops 52428800 | bytes 3145728 | tf_op jit(solution)/shard_map/forward/pallas_call | solution.py:288
  64.2 16.6 %all_to_all.36.all_ref = f32[16,1,768]{2,1,0:T(1,128)S(1)} all-to-all(f32[16,1,768]{2,1,0:T(1,128)S(1)} %get-tuple-element.22), channel_id=1, replica_groups=mesh['z'=16,'j'=8,'doc'=4] {'z'}, dimensions={0} | all-to-all | bytes 98304 | tf_op jit(solution)/shard_map/all_to_all | solution.py:306
  80.8 3.0 %backward.1 = (f32[1024,256]{1,0:T(8,128)S(1)}, bf16[32,32,128]{2,1,0:T(8,128)(2,1)S(1)}, f32[8,256]{1,0:T(8,128)S(1)}) custom-call(s32[2]{0:T(128)S(1)} %pad_add_fusion.at_ref, bf16[8,328,256]{2,1,0:T(8,128)(2,1)S(1)} %all_to_all.35.buf_ref, f32[16,1,768]{2,1,0:T(1,128)S(1)} %all_to_all.36.all_ref, f32[24,256]{1,0:T(8,128)S(1)} %get-tuple-element.23.seg_ref, ...), custom_call_target="tpu_custom_call" | custom-call | flops 52428800 | bytes 3145728 | tf_op jit(solution)/shard_map/backward/pallas_call | solution.py:288
  83.7 0.1 reshape.79
  83.9 0.1 maximum_maximum_fusion
  84.0 16.4 %all_to_all.37 = bf16[32,33,128]{2,1,0:T(8,128)(2,1)S(1)} all-to-all(bf16[32,33,128]{2,1,0:T(8,128)(2,1)S(1)} %maximum_maximum_fusion), channel_id=1, replica_groups=mesh['z'=16,'j'=8,'doc'=4] {'j','doc'}, dimensions={0} | all-to-all | bytes 540672 | tf_op jit(solution)/shard_map/all_to_all | solution.py:318
  100.4 0.1 fusion.1
  100.6 0.1 broadcast_in_dim.36
  100.7 0.7 pad_maximum_fusion.2
  101.3 3.5 %all-to-all-start.4 = ((bf16[16,24,128]{2,1,0:T(8,128)(2,1)}), bf16[16,24,128]{2,1,0:T(8,128)(2,1)S(1)}, u32[]{:S(2)}, u32[]{:S(2)}) async-start(bf16[16,24,128]{2,1,0:T(8,128)(2,1)} %pad_maximum_fusion.2), calls=%async_computation.4 | async-start | bytes 196608 | tf_op jit(solution)/shard_map/all_to_all | solution.py:323
  104.9 1.3 collective-permute-start.1
  106.2 3.4 %collective-permute-done.1.head_ref = f32[3,256]{1,0:T(4,128)S(1)} collective-permute-done((f32[3,256]{1,0:T(4,128)S(1)}, f32[3,256]{1,0:T(4,128)S(1)}, u32[]{:S(2)}, u32[]{:S(2)}) %collective-permute-start.1) | collective-permute-done | bytes 3104 | tf_op jit(solution)/shard_map/ppermute | solution.py:315
  109.6 1.0 taps.1
  110.6 5.9 %all-to-all-done.4 = bf16[16,24,128]{2,1,0:T(8,128)(2,1)S(1)} async-done(((bf16[16,24,128]{2,1,0:T(8,128)(2,1)}), bf16[16,24,128]{2,1,0:T(8,128)(2,1)S(1)}, u32[]{:S(2)}, u32[]{:S(2)}) %all-to-all-start.4) | async-done | bytes 98336 | tf_op jit(solution)/shard_map/all_to_all | solution.py:323
  116.7 6.7 %all_to_all.38.tiles_ref = f32[4,20,128]{2,1,0:T(8,128)S(1)} all-to-all(f32[4,20,128]{2,1,0:T(8,128)S(1)} %broadcast_in_dim.39), channel_id=1, replica_groups=mesh['z'=16,'j'=8,'doc'=4] {'doc'}, dimensions={0} | all-to-all | bytes 81920 | tf_op jit(solution)/shard_map/all_to_all | solution.py:334
  123.4 0.1 reshape.82
  123.5 0.1 reshape.83
  123.7 16.7 %all_to_all.39.got_ref = bf16[8,144,256]{2,1,0:T(8,128)(2,1)S(1)} all-to-all(bf16[8,144,256]{2,1,0:T(8,128)(2,1)S(1)} %pad_maximum_fusion.1), channel_id=1, replica_groups=mesh['z'=16,'j'=8,'doc'=4] {'j'}, dimensions={0} | all-to-all | bytes 1179648 | tf_op jit(solution)/shard_map/all_to_all | solution.py:337
  140.3 0.9 unpack.1
  (22 shorter events, 0.3 us)
Async XLA Ops:
  0.6 22.7 %copy-start.4 = (bf16[1,128,2048]{2,1,0:T(8,128)(2,1)S(1)}, bf16[1,128,2048]{2,1,0:T(8,128)(2,1)}, u32[]{:S(2)}) copy-start(bf16[1,128,2048]{2,1,0:T(8,128)(2,1)} %param.9) | copy-start | bytes 1572868
  2.1 28.9 %all-to-all-start = ((bf16[16,32,256]{2,1,0:T(8,128)(2,1)}), bf16[16,32,256]{2,1,0:T(8,128)(2,1)S(1)}, u32[]{:S(2)}, u32[]{:S(2)}) async-start(bf16[16,32,256]{2,1,0:T(8,128)(2,1)} %broadcast_in_dim.16), calls=%async_computation | async-start | bytes 524288 | tf_op jit(solution)/shard_map/all_to_all | solution.py:270
  18.7 5.4 %collective-permute-start = (bf16[3,2048]{1,0:T(4,128)(2,1)S(1)}, bf16[3,2048]{1,0:T(4,128)(2,1)S(1)}, u32[]{:S(2)}, u32[]{:S(2)}) collective-permute-start(bf16[3,2048]{1,0:T(4,128)(2,1)S(1)} %slice_bitcast_fusion.1), channel_id=1, source_target_pairs={{0,32},{32,64},{64,96},{96,128},{128,160},{160,192},{192,224},{224... | collective-permute-start | bytes 36872 | tf_op jit(solution)/shard_map/ppermute | solution.py:271
  31.1 29.9 %copy-start = (f32[4,2048]{1,0:T(4,128)S(1)}, f32[4,2048]{1,0:T(4,128)}, u32[]{:S(2)}) copy-start(f32[4,2048]{1,0:T(4,128)} %taps_ref.3) | copy-start | bytes 98308
  31.1 29.9 %copy-start.1 = (f32[2048]{0:T(1024)S(1)}, f32[2048]{0:T(1024)}, u32[]{:S(2)}) copy-start(f32[2048]{0:T(1024)} %param.15) | copy-start | bytes 24580
  31.1 29.9 %copy-start.2 = (f32[2,2048]{1,0:T(2,128)S(1)}, f32[2,2048]{1,0:T(2,128)}, u32[]{:S(2)}) copy-start(f32[2,2048]{1,0:T(2,128)} %bias_ref.1) | copy-start | bytes 49156
  31.2 29.9 %copy-start.3 = (f32[2048]{0:T(1024)S(1)}, f32[2048]{0:T(1024)}, u32[]{:S(2)}) copy-start(f32[2048]{0:T(1024)} %param.14) | copy-start | bytes 24580
  101.3 15.3 %all-to-all-start.4 = ((bf16[16,24,128]{2,1,0:T(8,128)(2,1)}), bf16[16,24,128]{2,1,0:T(8,128)(2,1)S(1)}, u32[]{:S(2)}, u32[]{:S(2)}) async-start(bf16[16,24,128]{2,1,0:T(8,128)(2,1)} %pad_maximum_fusion.2), calls=%async_computation.4 | async-start | bytes 196608 | tf_op jit(solution)/shard_map/all_to_all | solution.py:323
  104.9 4.7 %collective-permute-start.1 = (f32[3,256]{1,0:T(4,128)S(1)}, f32[3,256]{1,0:T(4,128)S(1)}, u32[]{:S(2)}, u32[]{:S(2)}) collective-permute-start(f32[3,256]{1,0:T(4,128)S(1)} %bitcast.46), channel_id=1, source_target_pairs={{32,0},{64,32},{96,64},{128,96},{160,128},{192,160},{224,192},{256... | collective-permute-start | bytes 9224 | tf_op jit(solution)/shard_map/ppermute | solution.py:315

commit v6 on v5

--- a/solution.py
+++ b/solution.py
@@ -10,7 +10,7 @@
 
 QFLOOR = 0.001
 SEGS = 8
-SPAN = 16
+SPAN = 32
 ROWS = SEGS * SPAN
 UNROLL = (True, True, True, True)
 F32 = jnp.float32

time: 142 us -> 141 us (level)
  no operation moved by 1% of the time
where the time goes in v6:
time: 141 us
  blocking collectives  86.2 us (61%)
  starting transfers between devices  23.8 us (17%)
  waiting for transfers between devices  16.3 us (12%)
  Pallas kernels  7.51 us (5%)
  local copies, waits for them, and re-layouts  3.93 us (3%)
  other arithmetic  1.98 us (1%)
    all_to_all x1, blocking collectives, per_device(): lax.all_to_all(jnp.concatenate([xs, ds, weights, halo], axis=1), 'j', 0, 0)  29.8 us
    all_to_all x1, blocking collectives, per_device(): got = lax.all_to_all(jnp.concatenate([ig, csum], axis=1), 'j', 0, 0)  16.7 us
    all_to_all x1, blocking collectives, per_device(): everyone = lax.all_to_all(summary, 'z', 0, 0)  16.5 us
    all_to_all x1, blocking collectives, per_device(): lax.all_to_all(jnp.concatenate([wg, packed], axis=1), ('j', 'doc'), 0, 0)  16.4 us
    all_to_all x1, starting transfers between devices, per_device(): weights = lax.all_to_all(weights, 'z', 0, 0).reshape(SEGS, 4 * share, block)  15.7 us
    all_to_all x1, waiting for transfers between devices, per_device(): weights = lax.all_to_all(weights, 'z', 0, 0).reshape(SEGS, 4 * share, block)  6.93 us
    all_to_all x1, blocking collectives, per_device(): lax.all_to_all(jnp.broadcast_to(send[None], (docs, 20, 128)), 'doc', 0, 0)  6.75 us
    pallas_call x3, Pallas kernels, call(): pl.pallas_call(kernel, out_shape=out_shape, in_specs=[smem] + [vmem] * (l...  6.62 us
  transfers between devices with their start and end apart: 4, of which 3 were waited for; matrix products, arithmetic and copies ran while one was open for 2% of the time, Pallas kernels for 1%

profile of v6, /device:TPU:1, one launch (start us, length us, event | category | flops | bytes accessed | tf_op | source)
XLA Modules:
  0.0 140.6 jit_solution(4552833307813880582)
XLA Ops:
  0.6 0.0 copy-start.4
  0.6 0.8 pad_maximum_fusion.3
  1.4 0.7 broadcast_in_dim.16
  2.1 15.7 %all-to-all-start = ((bf16[16,32,256]{2,1,0:T(8,128)(2,1)}), bf16[16,32,256]{2,1,0:T(8,128)(2,1)S(1)}, u32[]{:S(2)}, u32[]{:S(2)}) async-start(bf16[16,32,256]{2,1,0:T(8,128)(2,1)} %broadcast_in_dim.16), calls=%async_computation | async-start | bytes 524288 | tf_op jit(solution)/shard_map/all_to_all | solution.py:270
  17.9 0.8 slice_bitcast_fusion.1
  18.7 3.3 %collective-permute-start = (bf16[3,2048]{1,0:T(4,128)(2,1)S(1)}, bf16[3,2048]{1,0:T(4,128)(2,1)S(1)}, u32[]{:S(2)}, u32[]{:S(2)}) collective-permute-start(bf16[3,2048]{1,0:T(4,128)(2,1)S(1)} %slice_bitcast_fusion.1), channel_id=1, source_target_pairs={{0,32},{32,64},{64,96},{96,128},{128,160},{160,192},{192,224},{224... | collective-permute-start | bytes 36872 | tf_op jit(solution)/shard_map/ppermute | solution.py:271
  22.0 0.1 pad_add_fusion.at_ref
  22.0 1.3 copy.40
  23.3 0.0 copy-done.4
  23.4 0.3 copy.42
  23.6 0.2 copy.43
  23.9 0.2 copy.41
  24.1 0.0 collective-permute-done
  24.1 6.9 %all-to-all-done = bf16[16,32,256]{2,1,0:T(8,128)(2,1)S(1)} async-done(((bf16[16,32,256]{2,1,0:T(8,128)(2,1)}), bf16[16,32,256]{2,1,0:T(8,128)(2,1)S(1)}, u32[]{:S(2)}, u32[]{:S(2)}) %all-to-all-start) | async-done | bytes 262176 | tf_op jit(solution)/shard_map/all_to_all | solution.py:270
  31.0 0.1 pad_maximum_fusion
  31.1 0.0 copy-start
  31.1 0.0 copy-start.1
  31.1 0.0 copy-start.2
  31.2 0.0 copy-start.3
  31.2 29.8 %all_to_all.35.buf_ref = bf16[8,328,256]{2,1,0:T(8,128)(2,1)S(1)} all-to-all(bf16[8,328,256]{2,1,0:T(8,128)(2,1)S(1)} %pad_maximum_fusion), channel_id=1, replica_groups=mesh['z'=16,'j'=8,'doc'=4] {'j'}, dimensions={0} | all-to-all | bytes 2686976 | tf_op jit(solution)/shard_map/all_to_all | solution.py:276
  61.0 0.0 copy-done
  61.0 0.0 copy-done.1
  61.0 0.0 copy-done.2
  61.0 0.0 copy-done.3
  61.0 2.7 %forward.1 = (bf16[1024,256]{1,0:T(8,128)(2,1)S(1)}, f32[1024,256]{1,0:T(8,128)S(1)}, f32[1024,256]{1,0:T(8,128)S(1)}, f32[1024,256]{1,0:T(8,128)S(1)}, f32[1024...) custom-call(s32[2]{0:T(128)S(1)} %pad_add_fusion.at_ref, ...), custom_call_target="tpu_custom_call" | custom-call | flops 52428800 | bytes 3145728 | tf_op jit(solution)/shard_map/forward/pallas_call | solution.py:288
  63.7 16.5 %all_to_all.36.all_ref = f32[16,1,768]{2,1,0:T(1,128)S(1)} all-to-all(f32[16,1,768]{2,1,0:T(1,128)S(1)} %get-tuple-element.22), channel_id=1, replica_groups=mesh['z'=16,'j'=8,'doc'=4] {'z'}, dimensions={0} | all-to-all | bytes 98304 | tf_op jit(solution)/shard_map/all_to_all | solution.py:306
  80.3 2.8 %backward.1 = (f32[1024,256]{1,0:T(8,128)S(1)}, bf16[32,32,128]{2,1,0:T(8,128)(2,1)S(1)}, f32[8,256]{1,0:T(8,128)S(1)}) custom-call(s32[2]{0:T(128)S(1)} %pad_add_fusion.at_ref, bf16[8,328,256]{2,1,0:T(8,128)(2,1)S(1)} %all_to_all.35.buf_ref, f32[16,1,768]{2,1,0:T(1,128)S(1)} %all_to_all.36.all_ref, f32[24,256]{1,0:T(8,128)S(1)} %get-tuple-element.23.seg_ref, ...), custom_call_target="tpu_custom_call" | custom-call | flops 52428800 | bytes 3145728 | tf_op jit(solution)/shard_map/backward/pallas_call | solution.py:288
  83.1 0.1 reshape.79
  83.3 0.1 maximum_maximum_fusion
  83.4 16.4 %all_to_all.37 = bf16[32,33,128]{2,1,0:T(8,128)(2,1)S(1)} all-to-all(bf16[32,33,128]{2,1,0:T(8,128)(2,1)S(1)} %maximum_maximum_fusion), channel_id=1, replica_groups=mesh['z'=16,'j'=8,'doc'=4] {'j','doc'}, dimensions={0} | all-to-all | bytes 540672 | tf_op jit(solution)/shard_map/all_to_all | solution.py:318
  99.8 0.1 fusion.1
  99.9 0.1 broadcast_in_dim.36
  100.1 0.7 pad_maximum_fusion.2
  100.7 3.5 %all-to-all-start.4 = ((bf16[16,24,128]{2,1,0:T(8,128)(2,1)}), bf16[16,24,128]{2,1,0:T(8,128)(2,1)S(1)}, u32[]{:S(2)}, u32[]{:S(2)}) async-start(bf16[16,24,128]{2,1,0:T(8,128)(2,1)} %pad_maximum_fusion.2), calls=%async_computation.4 | async-start | bytes 196608 | tf_op jit(solution)/shard_map/all_to_all | solution.py:323
  104.3 1.3 collective-permute-start.1
  105.6 3.4 %collective-permute-done.1.head_ref = f32[3,256]{1,0:T(4,128)S(1)} collective-permute-done((f32[3,256]{1,0:T(4,128)S(1)}, f32[3,256]{1,0:T(4,128)S(1)}, u32[]{:S(2)}, u32[]{:S(2)}) %collective-permute-start.1) | collective-permute-done | bytes 3104 | tf_op jit(solution)/shard_map/ppermute | solution.py:315
  109.0 1.1 taps.1
  110.1 5.9 %all-to-all-done.4 = bf16[16,24,128]{2,1,0:T(8,128)(2,1)S(1)} async-done(((bf16[16,24,128]{2,1,0:T(8,128)(2,1)}), bf16[16,24,128]{2,1,0:T(8,128)(2,1)S(1)}, u32[]{:S(2)}, u32[]{:S(2)}) %all-to-all-start.4) | async-done | bytes 98336 | tf_op jit(solution)/shard_map/all_to_all | solution.py:323
  116.1 6.7 %all_to_all.38.tiles_ref = f32[4,20,128]{2,1,0:T(8,128)S(1)} all-to-all(f32[4,20,128]{2,1,0:T(8,128)S(1)} %broadcast_in_dim.39), channel_id=1, replica_groups=mesh['z'=16,'j'=8,'doc'=4] {'doc'}, dimensions={0} | all-to-all | bytes 81920 | tf_op jit(solution)/shard_map/all_to_all | solution.py:334
  122.8 0.1 reshape.82
  122.9 0.1 reshape.83
  123.1 16.7 %all_to_all.39.got_ref = bf16[8,144,256]{2,1,0:T(8,128)(2,1)S(1)} all-to-all(bf16[8,144,256]{2,1,0:T(8,128)(2,1)S(1)} %pad_maximum_fusion.1), channel_id=1, replica_groups=mesh['z'=16,'j'=8,'doc'=4] {'j'}, dimensions={0} | all-to-all | bytes 1179648 | tf_op jit(solution)/shard_map/all_to_all | solution.py:337
  139.7 0.9 unpack.1
  (22 shorter events, 0.3 us)
Async XLA Ops:
  0.6 22.7 %copy-start.4 = (bf16[1,128,2048]{2,1,0:T(8,128)(2,1)S(1)}, bf16[1,128,2048]{2,1,0:T(8,128)(2,1)}, u32[]{:S(2)}) copy-start(bf16[1,128,2048]{2,1,0:T(8,128)(2,1)} %param.9) | copy-start | bytes 1572868
  2.1 28.9 %all-to-all-start = ((bf16[16,32,256]{2,1,0:T(8,128)(2,1)}), bf16[16,32,256]{2,1,0:T(8,128)(2,1)S(1)}, u32[]{:S(2)}, u32[]{:S(2)}) async-start(bf16[16,32,256]{2,1,0:T(8,128)(2,1)} %broadcast_in_dim.16), calls=%async_computation | async-start | bytes 524288 | tf_op jit(solution)/shard_map/all_to_all | solution.py:270
  18.7 5.4 %collective-permute-start = (bf16[3,2048]{1,0:T(4,128)(2,1)S(1)}, bf16[3,2048]{1,0:T(4,128)(2,1)S(1)}, u32[]{:S(2)}, u32[]{:S(2)}) collective-permute-start(bf16[3,2048]{1,0:T(4,128)(2,1)S(1)} %slice_bitcast_fusion.1), channel_id=1, source_target_pairs={{0,32},{32,64},{64,96},{96,128},{128,160},{160,192},{192,224},{224... | collective-permute-start | bytes 36872 | tf_op jit(solution)/shard_map/ppermute | solution.py:271
  31.1 29.9 %copy-start = (f32[4,2048]{1,0:T(4,128)S(1)}, f32[4,2048]{1,0:T(4,128)}, u32[]{:S(2)}) copy-start(f32[4,2048]{1,0:T(4,128)} %taps_ref.3) | copy-start | bytes 98308
  31.1 29.9 %copy-start.1 = (f32[2048]{0:T(1024)S(1)}, f32[2048]{0:T(1024)}, u32[]{:S(2)}) copy-start(f32[2048]{0:T(1024)} %param.15) | copy-start | bytes 24580
  31.1 29.9 %copy-start.2 = (f32[2,2048]{1,0:T(2,128)S(1)}, f32[2,2048]{1,0:T(2,128)}, u32[]{:S(2)}) copy-start(f32[2,2048]{1,0:T(2,128)} %bias_ref.1) | copy-start | bytes 49156
  31.2 29.9 %copy-start.3 = (f32[2048]{0:T(1024)S(1)}, f32[2048]{0:T(1024)}, u32[]{:S(2)}) copy-start(f32[2048]{0:T(1024)} %param.14) | copy-start | bytes 24580
  100.7 15.3 %all-to-all-start.4 = ((bf16[16,24,128]{2,1,0:T(8,128)(2,1)}), bf16[16,24,128]{2,1,0:T(8,128)(2,1)S(1)}, u32[]{:S(2)}, u32[]{:S(2)}) async-start(bf16[16,24,128]{2,1,0:T(8,128)(2,1)} %pad_maximum_fusion.2), calls=%async_computation.4 | async-start | bytes 196608 | tf_op jit(solution)/shard_map/all_to_all | solution.py:323
  104.3 4.7 %collective-permute-start.1 = (f32[3,256]{1,0:T(4,128)S(1)}, f32[3,256]{1,0:T(4,128)S(1)}, u32[]{:S(2)}, u32[]{:S(2)}) collective-permute-start(f32[3,256]{1,0:T(4,128)S(1)} %bitcast.46), channel_id=1, source_target_pairs={{32,0},{64,32},{96,64},{128,96},{160,128},{192,160},{224,192},{256... | collective-permute-start | bytes 9224 | tf_op jit(solution)/shard_map/ppermute | solution.py:315

commit v7 on v6

--- a/solution.py
+++ b/solution.py
@@ -320,7 +320,6 @@
     wsum = jnp.sum(got[:, :, :32].astype(F32), axis=1).reshape(shards, 16, 128)
     csum = jnp.sum(joined(got[:, :, 32, :quarter], got[:, :, 32, quarter:]), axis=1)
     csum = jnp.broadcast_to(csum.reshape(1, 4, 128), (shards, 4, 128))
-    got = lax.all_to_all(jnp.concatenate((wsum.astype(BF16),) + split(csum), axis=1), "z", 0, 0)
     (ig,) = call(
         functools.partial(taps_kernel, steps),
         "taps",
@@ -328,9 +327,11 @@
         (at, gc, head, conv_taps),
         [pltpu.VMEM((ROWS + 3 * SEGS, block), F32)],
     )
+    send, ig = lax.optimization_barrier((jnp.concatenate((wsum.astype(BF16),) + split(csum), axis=1), ig))
+    got = lax.all_to_all(send, "z", 0, 0)
     wsum = jnp.sum(got[:, :16].astype(F32), axis=0)
     csum = jnp.sum(joined(got[:, 16:20], got[:, 20:]), axis=0)
-    send, ig = lax.optimization_barrier((jnp.concatenate([wsum, csum], axis=0), ig))
+    send = jnp.concatenate([wsum, csum], axis=0)
     tiles = lax.all_to_all(jnp.broadcast_to(send[None], (docs, 20, 128)), "doc", 0, 0)
     csum = tiles[:, 16:].reshape(docs, SEGS, quarter).transpose(1, 0, 2).reshape(SEGS, block)
     csum = jnp.broadcast_to(jnp.concatenate(split(csum), axis=0)[None], (SEGS, 2 * SEGS, block))

time: 141 us -> 142 us (level)
  starting transfers between devices: 23.8 us -> 27.5 us
  waiting for transfers between devices: 16.3 us -> 14 us
    all_to_all x1, starting transfers between devices: 3.51 us -> 7.17 us  [per_device(): lax.all_to_all(jnp.concatenate([wg, packed], axis=1), ('j', 'doc'), 0, 0)]
    all_to_all x1, waiting for transfers between devices: 5.91 us -> 3.7 us  [per_device(): lax.all_to_all(jnp.concatenate([wg, packed], axis=1), ('j', 'doc'), 0, 0)]
    all_to_all x1, blocking collectives: 16.4 us -> 14.4 us  [per_device(): got = lax.all_to_all(send, 'z', 0, 0)]
where the time goes in v7:
time: 142 us; the launch traced here: 141 us
  blocking collectives  85.1 us (60%)
  starting transfers between devices  27.5 us (19%)
  waiting for transfers between devices  14 us (10%)
  Pallas kernels  7.51 us (5%)
  local copies, waits for them, and re-layouts  3.93 us (3%)
  other arithmetic  2.06 us (1%)
    all_to_all x1, blocking collectives, per_device(): lax.all_to_all(jnp.concatenate([xs, ds, weights, halo], axis=1), 'j', 0, 0)  29.8 us
    all_to_all x1, blocking collectives, per_device(): got = lax.all_to_all(jnp.concatenate([ig, csum], axis=1), 'j', 0, 0)  17.6 us
    all_to_all x1, blocking collectives, per_device(): everyone = lax.all_to_all(summary, 'z', 0, 0)  16.5 us
    all_to_all x1, starting transfers between devices, per_device(): weights = lax.all_to_all(weights, 'z', 0, 0).reshape(SEGS, 4 * share, block)  15.7 us
    all_to_all x1, blocking collectives, per_device(): got = lax.all_to_all(send, 'z', 0, 0)  14.4 us
    all_to_all x1, starting transfers between devices, per_device(): lax.all_to_all(jnp.concatenate([wg, packed], axis=1), ('j', 'doc'), 0, 0)  7.17 us
    all_to_all x1, waiting for transfers between devices, per_device(): weights = lax.all_to_all(weights, 'z', 0, 0).reshape(SEGS, 4 * share, block)  6.93 us
    all_to_all x1, blocking collectives, per_device(): lax.all_to_all(jnp.broadcast_to(send[None], (docs, 20, 128)), 'doc', 0, 0)  6.75 us
  transfers between devices with their start and end apart: 4, of which 3 were waited for; matrix products, arithmetic and copies ran while one was open for 2% of the time, Pallas kernels for 1%

profile of v7, /device:TPU:1, one launch (start us, length us, event | category | flops | bytes accessed | tf_op | source)
XLA Modules:
  0.0 140.9 jit_solution(16279377706922446073)
XLA Ops:
  0.6 0.0 copy-start.4
  0.6 0.8 pad_maximum_fusion.3
  1.4 0.7 broadcast_in_dim.16
  2.1 15.7 %all-to-all-start = ((bf16[16,32,256]{2,1,0:T(8,128)(2,1)}), bf16[16,32,256]{2,1,0:T(8,128)(2,1)S(1)}, u32[]{:S(2)}, u32[]{:S(2)}) async-start(bf16[16,32,256]{2,1,0:T(8,128)(2,1)} %broadcast_in_dim.16), calls=%async_computation | async-start | bytes 524288 | tf_op jit(solution)/shard_map/all_to_all | solution.py:270
  17.9 0.8 slice_bitcast_fusion.1
  18.7 3.3 %collective-permute-start = (bf16[3,2048]{1,0:T(4,128)(2,1)S(1)}, bf16[3,2048]{1,0:T(4,128)(2,1)S(1)}, u32[]{:S(2)}, u32[]{:S(2)}) collective-permute-start(bf16[3,2048]{1,0:T(4,128)(2,1)S(1)} %slice_bitcast_fusion.1), channel_id=1, source_target_pairs={{0,32},{32,64},{64,96},{96,128},{128,160},{160,192},{192,224},{224... | collective-permute-start | bytes 36872 | tf_op jit(solution)/shard_map/ppermute | solution.py:271
  22.0 0.1 pad_add_fusion.at_ref
  22.0 1.3 copy.40
  23.3 0.0 copy-done.4
  23.4 0.3 copy.42
  23.6 0.2 copy.43
  23.9 0.2 copy.41
  24.1 0.0 collective-permute-done
  24.1 6.9 %all-to-all-done = bf16[16,32,256]{2,1,0:T(8,128)(2,1)S(1)} async-done(((bf16[16,32,256]{2,1,0:T(8,128)(2,1)}), bf16[16,32,256]{2,1,0:T(8,128)(2,1)S(1)}, u32[]{:S(2)}, u32[]{:S(2)}) %all-to-all-start) | async-done | bytes 262176 | tf_op jit(solution)/shard_map/all_to_all | solution.py:270
  31.0 0.1 pad_maximum_fusion
  31.1 0.0 copy-start
  31.1 0.0 copy-start.1
  31.1 0.0 copy-start.2
  31.2 0.0 copy-start.3
  31.2 29.8 %all_to_all.35.buf_ref = bf16[8,328,256]{2,1,0:T(8,128)(2,1)S(1)} all-to-all(bf16[8,328,256]{2,1,0:T(8,128)(2,1)S(1)} %pad_maximum_fusion), channel_id=1, replica_groups=mesh['z'=16,'j'=8,'doc'=4] {'j'}, dimensions={0} | all-to-all | bytes 2686976 | tf_op jit(solution)/shard_map/all_to_all | solution.py:276
  61.0 0.0 copy-done
  61.0 0.0 copy-done.1
  61.0 0.0 copy-done.2
  61.0 0.0 copy-done.3
  61.0 2.7 %forward.1 = (bf16[1024,256]{1,0:T(8,128)(2,1)S(1)}, f32[1024,256]{1,0:T(8,128)S(1)}, f32[1024,256]{1,0:T(8,128)S(1)}, f32[1024,256]{1,0:T(8,128)S(1)}, f32[1024...) custom-call(s32[2]{0:T(128)S(1)} %pad_add_fusion.at_ref, ...), custom_call_target="tpu_custom_call" | custom-call | flops 52428800 | bytes 3145728 | tf_op jit(solution)/shard_map/forward/pallas_call | solution.py:288
  63.7 16.5 %all_to_all.36.all_ref = f32[16,1,768]{2,1,0:T(1,128)S(1)} all-to-all(f32[16,1,768]{2,1,0:T(1,128)S(1)} %get-tuple-element.22), channel_id=1, replica_groups=mesh['z'=16,'j'=8,'doc'=4] {'z'}, dimensions={0} | all-to-all | bytes 98304 | tf_op jit(solution)/shard_map/all_to_all | solution.py:306
  80.3 2.8 %backward.1 = (f32[1024,256]{1,0:T(8,128)S(1)}, bf16[32,32,128]{2,1,0:T(8,128)(2,1)S(1)}, f32[8,256]{1,0:T(8,128)S(1)}) custom-call(s32[2]{0:T(128)S(1)} %pad_add_fusion.at_ref, bf16[8,328,256]{2,1,0:T(8,128)(2,1)S(1)} %all_to_all.35.buf_ref, f32[16,1,768]{2,1,0:T(1,128)S(1)} %all_to_all.36.all_ref, f32[24,256]{1,0:T(8,128)S(1)} %get-tuple-element.23.seg_ref, ...), custom_call_target="tpu_custom_call" | custom-call | flops 52428800 | bytes 3145728 | tf_op jit(solution)/shard_map/backward/pallas_call | solution.py:288
  83.1 0.1 reshape.79
  83.3 0.8 maximum_maximum_fusion
  84.1 7.2 %all-to-all-start.3 = ((bf16[32,33,128]{2,1,0:T(8,128)(2,1)}), bf16[32,33,128]{2,1,0:T(8,128)(2,1)S(1)}, u32[]{:S(2)}, u32[]{:S(2)}) async-start(bf16[32,33,128]{2,1,0:T(8,128)(2,1)} %maximum_maximum_fusion), calls=%async_computation.3 | async-start | bytes 655360 | tf_op jit(solution)/shard_map/all_to_all | solution.py:318
  91.3 1.3 collective-permute-start.1
  92.6 3.3 %collective-permute-done.1.head_ref = f32[3,256]{1,0:T(4,128)S(1)} collective-permute-done((f32[3,256]{1,0:T(4,128)S(1)}, f32[3,256]{1,0:T(4,128)S(1)}, u32[]{:S(2)}, u32[]{:S(2)}) %collective-permute-start.1) | collective-permute-done | bytes 3104 | tf_op jit(solution)/shard_map/ppermute | solution.py:315
  95.9 1.1 taps.1
  97.0 3.7 %all-to-all-done.3 = bf16[32,33,128]{2,1,0:T(8,128)(2,1)S(1)} async-done(((bf16[32,33,128]{2,1,0:T(8,128)(2,1)}), bf16[32,33,128]{2,1,0:T(8,128)(2,1)S(1)}, u32[]{:S(2)}, u32[]{:S(2)}) %all-to-all-start.3) | async-done | bytes 270368 | tf_op jit(solution)/shard_map/all_to_all | solution.py:318
  100.7 0.1 fusion.1
  100.9 0.1 broadcast_in_dim.36
  101.0 14.4 %all_to_all.37 = bf16[16,24,128]{2,1,0:T(8,128)(2,1)S(1)} all-to-all(bf16[16,24,128]{2,1,0:T(8,128)(2,1)S(1)} %pad_maximum_fusion.2), channel_id=1, replica_groups=mesh['z'=16,'j'=8,'doc'=4] {'z'}, dimensions={0} | all-to-all | bytes 196608 | tf_op jit(solution)/shard_map/all_to_all | solution.py:331
  115.5 6.7 %all_to_all.38.tiles_ref = f32[4,20,128]{2,1,0:T(8,128)S(1)} all-to-all(f32[4,20,128]{2,1,0:T(8,128)S(1)} %broadcast_in_dim.39), channel_id=1, replica_groups=mesh['z'=16,'j'=8,'doc'=4] {'doc'}, dimensions={0} | all-to-all | bytes 81920 | tf_op jit(solution)/shard_map/all_to_all | solution.py:335
  122.2 0.1 reshape.82
  122.3 0.1 reshape.83
  122.5 17.6 %all_to_all.39.got_ref = bf16[8,144,256]{2,1,0:T(8,128)(2,1)S(1)} all-to-all(bf16[8,144,256]{2,1,0:T(8,128)(2,1)S(1)} %pad_maximum_fusion.1), channel_id=1, replica_groups=mesh['z'=16,'j'=8,'doc'=4] {'j'}, dimensions={0} | all-to-all | bytes 1179648 | tf_op jit(solution)/shard_map/all_to_all | solution.py:338
  140.0 0.9 unpack.1
  (23 shorter events, 0.3 us)
Async XLA Ops:
  0.6 22.7 %copy-start.4 = (bf16[1,128,2048]{2,1,0:T(8,128)(2,1)S(1)}, bf16[1,128,2048]{2,1,0:T(8,128)(2,1)}, u32[]{:S(2)}) copy-start(bf16[1,128,2048]{2,1,0:T(8,128)(2,1)} %param.9) | copy-start | bytes 1572868
  2.1 28.9 %all-to-all-start = ((bf16[16,32,256]{2,1,0:T(8,128)(2,1)}), bf16[16,32,256]{2,1,0:T(8,128)(2,1)S(1)}, u32[]{:S(2)}, u32[]{:S(2)}) async-start(bf16[16,32,256]{2,1,0:T(8,128)(2,1)} %broadcast_in_dim.16), calls=%async_computation | async-start | bytes 524288 | tf_op jit(solution)/shard_map/all_to_all | solution.py:270
  18.7 5.4 %collective-permute-start = (bf16[3,2048]{1,0:T(4,128)(2,1)S(1)}, bf16[3,2048]{1,0:T(4,128)(2,1)S(1)}, u32[]{:S(2)}, u32[]{:S(2)}) collective-permute-start(bf16[3,2048]{1,0:T(4,128)(2,1)S(1)} %slice_bitcast_fusion.1), channel_id=1, source_target_pairs={{0,32},{32,64},{64,96},{96,128},{128,160},{160,192},{192,224},{224... | collective-permute-start | bytes 36872 | tf_op jit(solution)/shard_map/ppermute | solution.py:271
  31.1 29.9 %copy-start = (f32[4,2048]{1,0:T(4,128)S(1)}, f32[4,2048]{1,0:T(4,128)}, u32[]{:S(2)}) copy-start(f32[4,2048]{1,0:T(4,128)} %taps_ref.3) | copy-start | bytes 98308
  31.1 29.9 %copy-start.1 = (f32[2048]{0:T(1024)S(1)}, f32[2048]{0:T(1024)}, u32[]{:S(2)}) copy-start(f32[2048]{0:T(1024)} %param.15) | copy-start | bytes 24580
  31.1 29.9 %copy-start.2 = (f32[2,2048]{1,0:T(2,128)S(1)}, f32[2,2048]{1,0:T(2,128)}, u32[]{:S(2)}) copy-start(f32[2,2048]{1,0:T(2,128)} %bias_ref.1) | copy-start | bytes 49156
  31.2 29.9 %copy-start.3 = (f32[2048]{0:T(1024)S(1)}, f32[2048]{0:T(1024)}, u32[]{:S(2)}) copy-start(f32[2048]{0:T(1024)} %param.14) | copy-start | bytes 24580
  84.1 16.6 %all-to-all-start.3 = ((bf16[32,33,128]{2,1,0:T(8,128)(2,1)}), bf16[32,33,128]{2,1,0:T(8,128)(2,1)S(1)}, u32[]{:S(2)}, u32[]{:S(2)}) async-start(bf16[32,33,128]{2,1,0:T(8,128)(2,1)} %maximum_maximum_fusion), calls=%async_computation.3 | async-start | bytes 655360 | tf_op jit(solution)/shard_map/all_to_all | solution.py:318
  91.3 4.6 %collective-permute-start.1 = (f32[3,256]{1,0:T(4,128)S(1)}, f32[3,256]{1,0:T(4,128)S(1)}, u32[]{:S(2)}, u32[]{:S(2)}) collective-permute-start(f32[3,256]{1,0:T(4,128)S(1)} %bitcast.46), channel_id=1, source_target_pairs={{32,0},{64,32},{96,64},{128,96},{160,128},{192,160},{224,192},{256... | collective-permute-start | bytes 9224 | tf_op jit(solution)/shard_map/ppermute | solution.py:315

commit v8 on v6

--- a/solution.py
+++ b/solution.py
@@ -233,17 +233,15 @@
     put(tail_ref, 0, final * SPAN)
 
 
-def unpack_kernel(steps, got_ref, tiles_ref, ig_ref, recur_ref, input_ref, rows_ref):
+def unpack_kernel(steps, got_ref, tiles_ref, all_ref, ig_ref, recur_ref, input_ref, rows_ref):
     block = got_ref.shape[2]
     for half in range(2):
         recur_ref[:, half * 128 : (half + 1) * 128] = tiles_ref[half, :16, :]
         input_ref[:, half * 128 : (half + 1) * 128] = tiles_ref[2 + half, :16, :]
     for b in range(SEGS):
         ig_ref[0, :, b * block : (b + 1) * block] = got_ref[b, :steps, :]
-        pair = got_ref[b, steps : steps + 2 * SEGS, :].astype(F32)
-        row = pair[:SEGS] + pair[SEGS:]
         for k in range(SEGS):
-            rows_ref[b : b + 1, k * block : (k + 1) * block] = row[k : k + 1]
+            rows_ref[b : b + 1, k * block : (k + 1) * block] = all_ref[b, k : k + 1, :]
 
 
 def split(v):
@@ -333,18 +331,19 @@
     send, ig = lax.optimization_barrier((jnp.concatenate([wsum, csum], axis=0), ig))
     tiles = lax.all_to_all(jnp.broadcast_to(send[None], (docs, 20, 128)), "doc", 0, 0)
     csum = tiles[:, 16:].reshape(docs, SEGS, quarter).transpose(1, 0, 2).reshape(SEGS, block)
-    csum = jnp.broadcast_to(jnp.concatenate(split(csum), axis=0)[None], (SEGS, 2 * SEGS, block))
+    csum = jnp.broadcast_to(csum.astype(BF16)[None], (SEGS, SEGS, block))
     got = lax.all_to_all(jnp.concatenate([ig, csum], axis=1), "j", 0, 0)
+    rows = got[:, steps:].astype(F32)
     return pl.pallas_call(
         functools.partial(unpack_kernel, steps),
         out_shape=(
             shape((1, steps, width), BF16), shape((share, block), F32), shape((share, block), F32), shape((SEGS, width), F32)
         ),
-        in_specs=[vmem] * 2,
+        in_specs=[vmem] * 3,
         out_specs=(vmem,) * 4,
         compiler_params=limit,
         name="unpack",
-    )(got, tiles)
+    )(got, tiles, rows)
 
 
 def solution(mesh):

time: 141 us -> 141 us (level)
  no operation moved by 1% of the time
where the time goes in v8:
time: 141 us; the launch traced here: 140 us
  blocking collectives  86 us (61%)
  starting transfers between devices  23.8 us (17%)
  waiting for transfers between devices  16.3 us (12%)
  Pallas kernels  7.53 us (5%)
  local copies, waits for them, and re-layouts  3.93 us (3%)
  other arithmetic  1.97 us (1%)
    all_to_all x1, blocking collectives, per_device(): lax.all_to_all(jnp.concatenate([xs, ds, weights, halo], axis=1), 'j', 0, 0)  29.8 us
    all_to_all x1, blocking collectives, per_device(): everyone = lax.all_to_all(summary, 'z', 0, 0)  16.5 us
    all_to_all x1, blocking collectives, per_device(): got = lax.all_to_all(jnp.concatenate([ig, csum], axis=1), 'j', 0, 0)  16.5 us
    all_to_all x1, blocking collectives, per_device(): lax.all_to_all(jnp.concatenate([wg, packed], axis=1), ('j', 'doc'), 0, 0)  16.4 us
    all_to_all x1, starting transfers between devices, per_device(): weights = lax.all_to_all(weights, 'z', 0, 0).reshape(SEGS, 4 * share, block)  15.7 us
    all_to_all x1, waiting for transfers between devices, per_device(): weights = lax.all_to_all(weights, 'z', 0, 0).reshape(SEGS, 4 * share, block)  6.93 us
    all_to_all x1, blocking collectives, per_device(): lax.all_to_all(jnp.broadcast_to(send[None], (docs, 20, 128)), 'doc', 0, 0)  6.75 us
    pallas_call x3, Pallas kernels, call(): pl.pallas_call(kernel, out_shape=out_shape, in_specs=[smem] + [vmem] * (l...  6.62 us
  transfers between devices with their start and end apart: 4, of which 3 were waited for; matrix products, arithmetic and copies ran while one was open for 2% of the time, Pallas kernels for 1%

profile of v8, /device:TPU:1, one launch (start us, length us, event | category | flops | bytes accessed | tf_op | source)
XLA Modules:
  0.0 140.5 jit_solution(364520024137418423)
XLA Ops:
  0.6 0.0 copy-start.4
  0.6 0.8 pad_maximum_fusion.3
  1.4 0.7 broadcast_in_dim.16
  2.1 15.7 %all-to-all-start = ((bf16[16,32,256]{2,1,0:T(8,128)(2,1)}), bf16[16,32,256]{2,1,0:T(8,128)(2,1)S(1)}, u32[]{:S(2)}, u32[]{:S(2)}) async-start(bf16[16,32,256]{2,1,0:T(8,128)(2,1)} %broadcast_in_dim.16), calls=%async_computation | async-start | bytes 524288 | tf_op jit(solution)/shard_map/all_to_all | solution.py:268
  17.9 0.8 slice_bitcast_fusion.1
  18.7 3.3 %collective-permute-start = (bf16[3,2048]{1,0:T(4,128)(2,1)S(1)}, bf16[3,2048]{1,0:T(4,128)(2,1)S(1)}, u32[]{:S(2)}, u32[]{:S(2)}) collective-permute-start(bf16[3,2048]{1,0:T(4,128)(2,1)S(1)} %slice_bitcast_fusion.1), channel_id=1, source_target_pairs={{0,32},{32,64},{64,96},{96,128},{128,160},{160,192},{192,224},{224... | collective-permute-start | bytes 36872 | tf_op jit(solution)/shard_map/ppermute | solution.py:269
  22.0 0.1 pad_add_fusion.at_ref
  22.0 1.3 copy.41
  23.3 0.0 copy-done.4
  23.4 0.3 copy.43
  23.6 0.2 copy.44
  23.9 0.2 copy.42
  24.1 0.0 collective-permute-done
  24.1 6.9 %all-to-all-done = bf16[16,32,256]{2,1,0:T(8,128)(2,1)S(1)} async-done(((bf16[16,32,256]{2,1,0:T(8,128)(2,1)}), bf16[16,32,256]{2,1,0:T(8,128)(2,1)S(1)}, u32[]{:S(2)}, u32[]{:S(2)}) %all-to-all-start) | async-done | bytes 262176 | tf_op jit(solution)/shard_map/all_to_all | solution.py:268
  31.0 0.1 pad_maximum_fusion
  31.1 0.0 copy-start
  31.1 0.0 copy-start.1
  31.1 0.0 copy-start.2
  31.2 0.0 copy-start.3
  31.2 29.8 %all_to_all.35.buf_ref = bf16[8,328,256]{2,1,0:T(8,128)(2,1)S(1)} all-to-all(bf16[8,328,256]{2,1,0:T(8,128)(2,1)S(1)} %pad_maximum_fusion), channel_id=1, replica_groups=mesh['z'=16,'j'=8,'doc'=4] {'j'}, dimensions={0} | all-to-all | bytes 2686976 | tf_op jit(solution)/shard_map/all_to_all | solution.py:274
  61.0 0.0 copy-done
  61.0 0.0 copy-done.1
  61.0 0.0 copy-done.2
  61.0 0.0 copy-done.3
  61.0 2.7 %forward.1 = (bf16[1024,256]{1,0:T(8,128)(2,1)S(1)}, f32[1024,256]{1,0:T(8,128)S(1)}, f32[1024,256]{1,0:T(8,128)S(1)}, f32[1024,256]{1,0:T(8,128)S(1)}, f32[1024...) custom-call(s32[2]{0:T(128)S(1)} %pad_add_fusion.at_ref, ...), custom_call_target="tpu_custom_call" | custom-call | flops 52428800 | bytes 3145728 | tf_op jit(solution)/shard_map/forward/pallas_call | solution.py:286
  63.7 16.5 %all_to_all.36.all_ref = f32[16,1,768]{2,1,0:T(1,128)S(1)} all-to-all(f32[16,1,768]{2,1,0:T(1,128)S(1)} %get-tuple-element.22), channel_id=1, replica_groups=mesh['z'=16,'j'=8,'doc'=4] {'z'}, dimensions={0} | all-to-all | bytes 98304 | tf_op jit(solution)/shard_map/all_to_all | solution.py:304
  80.3 2.8 %backward.1 = (f32[1024,256]{1,0:T(8,128)S(1)}, bf16[32,32,128]{2,1,0:T(8,128)(2,1)S(1)}, f32[8,256]{1,0:T(8,128)S(1)}) custom-call(s32[2]{0:T(128)S(1)} %pad_add_fusion.at_ref, bf16[8,328,256]{2,1,0:T(8,128)(2,1)S(1)} %all_to_all.35.buf_ref, f32[16,1,768]{2,1,0:T(1,128)S(1)} %all_to_all.36.all_ref, f32[24,256]{1,0:T(8,128)S(1)} %get-tuple-element.23.seg_ref, ...), custom_call_target="tpu_custom_call" | custom-call | flops 52428800 | bytes 3145728 | tf_op jit(solution)/shard_map/backward/pallas_call | solution.py:286
  83.1 0.1 reshape.81
  83.3 0.1 maximum_maximum_fusion
  83.4 16.4 %all_to_all.37 = bf16[32,33,128]{2,1,0:T(8,128)(2,1)S(1)} all-to-all(bf16[32,33,128]{2,1,0:T(8,128)(2,1)S(1)} %maximum_maximum_fusion), channel_id=1, replica_groups=mesh['z'=16,'j'=8,'doc'=4] {'j','doc'}, dimensions={0} | all-to-all | bytes 540672 | tf_op jit(solution)/shard_map/all_to_all | solution.py:316
  99.8 0.1 fusion.1
  99.9 0.1 broadcast_in_dim.36
  100.1 0.7 pad_maximum_fusion.2
  100.7 3.5 %all-to-all-start.4 = ((bf16[16,24,128]{2,1,0:T(8,128)(2,1)}), bf16[16,24,128]{2,1,0:T(8,128)(2,1)S(1)}, u32[]{:S(2)}, u32[]{:S(2)}) async-start(bf16[16,24,128]{2,1,0:T(8,128)(2,1)} %pad_maximum_fusion.2), calls=%async_computation.4 | async-start | bytes 196608 | tf_op jit(solution)/shard_map/all_to_all | solution.py:321
  104.3 1.3 collective-permute-start.1
  105.6 3.4 %collective-permute-done.1.head_ref = f32[3,256]{1,0:T(4,128)S(1)} collective-permute-done((f32[3,256]{1,0:T(4,128)S(1)}, f32[3,256]{1,0:T(4,128)S(1)}, u32[]{:S(2)}, u32[]{:S(2)}) %collective-permute-start.1) | collective-permute-done | bytes 3104 | tf_op jit(solution)/shard_map/ppermute | solution.py:313
  109.0 1.1 taps.1
  110.1 5.9 %all-to-all-done.4 = bf16[16,24,128]{2,1,0:T(8,128)(2,1)S(1)} async-done(((bf16[16,24,128]{2,1,0:T(8,128)(2,1)}), bf16[16,24,128]{2,1,0:T(8,128)(2,1)S(1)}, u32[]{:S(2)}, u32[]{:S(2)}) %all-to-all-start.4) | async-done | bytes 98336 | tf_op jit(solution)/shard_map/all_to_all | solution.py:321
  116.1 6.7 %all_to_all.38.tiles_ref = f32[4,20,128]{2,1,0:T(8,128)S(1)} all-to-all(f32[4,20,128]{2,1,0:T(8,128)S(1)} %broadcast_in_dim.39), channel_id=1, replica_groups=mesh['z'=16,'j'=8,'doc'=4] {'doc'}, dimensions={0} | all-to-all | bytes 81920 | tf_op jit(solution)/shard_map/all_to_all | solution.py:332
  122.8 0.1 convert_element_type.88
  122.9 0.1 convert_element_type.90
  123.0 16.5 %all_to_all.39.got_ref = bf16[8,136,256]{2,1,0:T(8,128)(2,1)S(1)} all-to-all(bf16[8,136,256]{2,1,0:T(8,128)(2,1)S(1)} %pad_maximum_fusion.1), channel_id=1, replica_groups=mesh['z'=16,'j'=8,'doc'=4] {'j'}, dimensions={0} | all-to-all | bytes 1114112 | tf_op jit(solution)/shard_map/all_to_all | solution.py:335
  139.6 0.9 unpack.1
  (21 shorter events, 0.2 us)
Async XLA Ops:
  0.6 22.7 %copy-start.4 = (bf16[1,128,2048]{2,1,0:T(8,128)(2,1)S(1)}, bf16[1,128,2048]{2,1,0:T(8,128)(2,1)}, u32[]{:S(2)}) copy-start(bf16[1,128,2048]{2,1,0:T(8,128)(2,1)} %param.9) | copy-start | bytes 1572868
  2.1 28.9 %all-to-all-start = ((bf16[16,32,256]{2,1,0:T(8,128)(2,1)}), bf16[16,32,256]{2,1,0:T(8,128)(2,1)S(1)}, u32[]{:S(2)}, u32[]{:S(2)}) async-start(bf16[16,32,256]{2,1,0:T(8,128)(2,1)} %broadcast_in_dim.16), calls=%async_computation | async-start | bytes 524288 | tf_op jit(solution)/shard_map/all_to_all | solution.py:268
  18.7 5.4 %collective-permute-start = (bf16[3,2048]{1,0:T(4,128)(2,1)S(1)}, bf16[3,2048]{1,0:T(4,128)(2,1)S(1)}, u32[]{:S(2)}, u32[]{:S(2)}) collective-permute-start(bf16[3,2048]{1,0:T(4,128)(2,1)S(1)} %slice_bitcast_fusion.1), channel_id=1, source_target_pairs={{0,32},{32,64},{64,96},{96,128},{128,160},{160,192},{192,224},{224... | collective-permute-start | bytes 36872 | tf_op jit(solution)/shard_map/ppermute | solution.py:269
  31.1 29.9 %copy-start = (f32[4,2048]{1,0:T(4,128)S(1)}, f32[4,2048]{1,0:T(4,128)}, u32[]{:S(2)}) copy-start(f32[4,2048]{1,0:T(4,128)} %taps_ref.3) | copy-start | bytes 98308
  31.1 29.9 %copy-start.1 = (f32[2048]{0:T(1024)S(1)}, f32[2048]{0:T(1024)}, u32[]{:S(2)}) copy-start(f32[2048]{0:T(1024)} %param.15) | copy-start | bytes 24580
  31.1 29.9 %copy-start.2 = (f32[2,2048]{1,0:T(2,128)S(1)}, f32[2,2048]{1,0:T(2,128)}, u32[]{:S(2)}) copy-start(f32[2,2048]{1,0:T(2,128)} %bias_ref.1) | copy-start | bytes 49156
  31.2 29.9 %copy-start.3 = (f32[2048]{0:T(1024)S(1)}, f32[2048]{0:T(1024)}, u32[]{:S(2)}) copy-start(f32[2048]{0:T(1024)} %param.14) | copy-start | bytes 24580
  100.7 15.3 %all-to-all-start.4 = ((bf16[16,24,128]{2,1,0:T(8,128)(2,1)}), bf16[16,24,128]{2,1,0:T(8,128)(2,1)S(1)}, u32[]{:S(2)}, u32[]{:S(2)}) async-start(bf16[16,24,128]{2,1,0:T(8,128)(2,1)} %pad_maximum_fusion.2), calls=%async_computation.4 | async-start | bytes 196608 | tf_op jit(solution)/shard_map/all_to_all | solution.py:321
  104.3 4.7 %collective-permute-start.1 = (f32[3,256]{1,0:T(4,128)S(1)}, f32[3,256]{1,0:T(4,128)S(1)}, u32[]{:S(2)}, u32[]{:S(2)}) collective-permute-start(f32[3,256]{1,0:T(4,128)S(1)} %bitcast.44), channel_id=1, source_target_pairs={{32,0},{64,32},{96,64},{128,96},{160,128},{192,160},{224,192},{256... | collective-permute-start | bytes 9224 | tf_op jit(solution)/shard_map/ppermute | solution.py:313

commit v9 on v8

--- a/solution.py
+++ b/solution.py
@@ -236,8 +236,8 @@
 def unpack_kernel(steps, got_ref, tiles_ref, all_ref, ig_ref, recur_ref, input_ref, rows_ref):
     block = got_ref.shape[2]
     for half in range(2):
-        recur_ref[:, half * 128 : (half + 1) * 128] = tiles_ref[half, :16, :]
-        input_ref[:, half * 128 : (half + 1) * 128] = tiles_ref[2 + half, :16, :]
+        recur_ref[:, half * 128 : (half + 1) * 128] = tiles_ref[half, :16, :].astype(F32)
+        input_ref[:, half * 128 : (half + 1) * 128] = tiles_ref[2 + half, :16, :].astype(F32)
     for b in range(SEGS):
         ig_ref[0, :, b * block : (b + 1) * block] = got_ref[b, :steps, :]
         for k in range(SEGS):
@@ -328,7 +328,7 @@
     )
     wsum = jnp.sum(got[:, :16].astype(F32), axis=0)
     csum = jnp.sum(joined(got[:, 16:20], got[:, 20:]), axis=0)
-    send, ig = lax.optimization_barrier((jnp.concatenate([wsum, csum], axis=0), ig))
+    send, ig = lax.optimization_barrier((jnp.concatenate([wsum, csum], axis=0).astype(BF16), ig))
     tiles = lax.all_to_all(jnp.broadcast_to(send[None], (docs, 20, 128)), "doc", 0, 0)
     csum = tiles[:, 16:].reshape(docs, SEGS, quarter).transpose(1, 0, 2).reshape(SEGS, block)
     csum = jnp.broadcast_to(csum.astype(BF16)[None], (SEGS, SEGS, block))

time: 141 us -> 141 us (level)
  no operation moved by 1% of the time
where the time goes in v9:
time: 141 us; the launch traced here: 140 us
  blocking collectives  85.9 us (61%)
  starting transfers between devices  23.8 us (17%)
  waiting for transfers between devices  16.3 us (12%)
  Pallas kernels  7.53 us (5%)
  local copies, waits for them, and re-layouts  3.93 us (3%)
  other arithmetic  1.97 us (1%)
    all_to_all x1, blocking collectives, per_device(): lax.all_to_all(jnp.concatenate([xs, ds, weights, halo], axis=1), 'j', 0, 0)  29.8 us
    all_to_all x1, blocking collectives, per_device(): everyone = lax.all_to_all(summary, 'z', 0, 0)  16.5 us
    all_to_all x1, blocking collectives, per_device(): got = lax.all_to_all(jnp.concatenate([ig, csum], axis=1), 'j', 0, 0)  16.5 us
    all_to_all x1, blocking collectives, per_device(): lax.all_to_all(jnp.concatenate([wg, packed], axis=1), ('j', 'doc'), 0, 0)  16.4 us
    all_to_all x1, starting transfers between devices, per_device(): weights = lax.all_to_all(weights, 'z', 0, 0).reshape(SEGS, 4 * share, block)  15.7 us
    all_to_all x1, waiting for transfers between devices, per_device(): weights = lax.all_to_all(weights, 'z', 0, 0).reshape(SEGS, 4 * share, block)  6.93 us
    pallas_call x3, Pallas kernels, call(): pl.pallas_call(kernel, out_shape=out_shape, in_specs=[smem] + [vmem] * (l...  6.62 us
    all_to_all x1, blocking collectives, per_device(): lax.all_to_all(jnp.broadcast_to(send[None], (docs, 20, 128)), 'doc', 0, 0)  6.61 us
  transfers between devices with their start and end apart: 4, of which 3 were waited for; matrix products, arithmetic and copies ran while one was open for 2% of the time, Pallas kernels for 1%

profile of v9, /device:TPU:1, one launch (start us, length us, event | category | flops | bytes accessed | tf_op | source)
XLA Modules:
  0.0 140.3 jit_solution(17595992537019912756)
XLA Ops:
  0.6 0.0 copy-start.4
  0.6 0.8 pad_maximum_fusion.3
  1.4 0.7 broadcast_in_dim.34
  2.1 15.7 %all-to-all-start = ((bf16[16,32,256]{2,1,0:T(8,128)(2,1)}), bf16[16,32,256]{2,1,0:T(8,128)(2,1)S(1)}, u32[]{:S(2)}, u32[]{:S(2)}) async-start(bf16[16,32,256]{2,1,0:T(8,128)(2,1)} %broadcast_in_dim.34), calls=%async_computation | async-start | bytes 524288 | tf_op jit(solution)/shard_map/all_to_all | solution.py:268
  17.9 0.8 slice_bitcast_fusion.1
  18.7 3.3 %collective-permute-start = (bf16[3,2048]{1,0:T(4,128)(2,1)S(1)}, bf16[3,2048]{1,0:T(4,128)(2,1)S(1)}, u32[]{:S(2)}, u32[]{:S(2)}) collective-permute-start(bf16[3,2048]{1,0:T(4,128)(2,1)S(1)} %slice_bitcast_fusion.1), channel_id=1, source_target_pairs={{0,32},{32,64},{64,96},{96,128},{128,160},{160,192},{192,224},{224... | collective-permute-start | bytes 36872 | tf_op jit(solution)/shard_map/ppermute | solution.py:269
  22.0 0.1 pad_add_fusion.at_ref
  22.0 1.3 copy.41
  23.3 0.0 copy-done.4
  23.4 0.3 copy.43
  23.6 0.2 copy.44
  23.9 0.2 copy.42
  24.1 0.0 collective-permute-done
  24.1 6.9 %all-to-all-done = bf16[16,32,256]{2,1,0:T(8,128)(2,1)S(1)} async-done(((bf16[16,32,256]{2,1,0:T(8,128)(2,1)}), bf16[16,32,256]{2,1,0:T(8,128)(2,1)S(1)}, u32[]{:S(2)}, u32[]{:S(2)}) %all-to-all-start) | async-done | bytes 262176 | tf_op jit(solution)/shard_map/all_to_all | solution.py:268
  31.0 0.1 pad_maximum_fusion
  31.1 0.0 copy-start
  31.1 0.0 copy-start.1
  31.1 0.0 copy-start.2
  31.2 0.0 copy-start.3
  31.2 29.8 %all_to_all.35.buf_ref = bf16[8,328,256]{2,1,0:T(8,128)(2,1)S(1)} all-to-all(bf16[8,328,256]{2,1,0:T(8,128)(2,1)S(1)} %pad_maximum_fusion), channel_id=1, replica_groups=mesh['z'=16,'j'=8,'doc'=4] {'j'}, dimensions={0} | all-to-all | bytes 2686976 | tf_op jit(solution)/shard_map/all_to_all | solution.py:274
  61.0 0.0 copy-done
  61.0 0.0 copy-done.1
  61.0 0.0 copy-done.2
  61.0 0.0 copy-done.3
  61.0 2.7 %forward.1 = (bf16[1024,256]{1,0:T(8,128)(2,1)S(1)}, f32[1024,256]{1,0:T(8,128)S(1)}, f32[1024,256]{1,0:T(8,128)S(1)}, f32[1024,256]{1,0:T(8,128)S(1)}, f32[1024...) custom-call(s32[2]{0:T(128)S(1)} %pad_add_fusion.at_ref, ...), custom_call_target="tpu_custom_call" | custom-call | flops 52428800 | bytes 3145728 | tf_op jit(solution)/shard_map/forward/pallas_call | solution.py:286
  63.7 16.5 %all_to_all.36.all_ref = f32[16,1,768]{2,1,0:T(1,128)S(1)} all-to-all(f32[16,1,768]{2,1,0:T(1,128)S(1)} %get-tuple-element.22), channel_id=1, replica_groups=mesh['z'=16,'j'=8,'doc'=4] {'z'}, dimensions={0} | all-to-all | bytes 98304 | tf_op jit(solution)/shard_map/all_to_all | solution.py:304
  80.3 2.8 %backward.1 = (f32[1024,256]{1,0:T(8,128)S(1)}, bf16[32,32,128]{2,1,0:T(8,128)(2,1)S(1)}, f32[8,256]{1,0:T(8,128)S(1)}) custom-call(s32[2]{0:T(128)S(1)} %pad_add_fusion.at_ref, bf16[8,328,256]{2,1,0:T(8,128)(2,1)S(1)} %all_to_all.35.buf_ref, f32[16,1,768]{2,1,0:T(1,128)S(1)} %all_to_all.36.all_ref, f32[24,256]{1,0:T(8,128)S(1)} %get-tuple-element.23.seg_ref, ...), custom_call_target="tpu_custom_call" | custom-call | flops 52428800 | bytes 3145728 | tf_op jit(solution)/shard_map/backward/pallas_call | solution.py:286
  83.1 0.1 reshape.76
  83.3 0.1 maximum_maximum_fusion
  83.4 16.4 %all_to_all.37 = bf16[32,33,128]{2,1,0:T(8,128)(2,1)S(1)} all-to-all(bf16[32,33,128]{2,1,0:T(8,128)(2,1)S(1)} %maximum_maximum_fusion), channel_id=1, replica_groups=mesh['z'=16,'j'=8,'doc'=4] {'j','doc'}, dimensions={0} | all-to-all | bytes 540672 | tf_op jit(solution)/shard_map/all_to_all | solution.py:316
  99.8 0.1 fusion.1
  99.9 0.1 broadcast_in_dim.37
  100.1 0.7 pad_maximum_fusion.2
  100.7 3.5 %all-to-all-start.4 = ((bf16[16,24,128]{2,1,0:T(8,128)(2,1)}), bf16[16,24,128]{2,1,0:T(8,128)(2,1)S(1)}, u32[]{:S(2)}, u32[]{:S(2)}) async-start(bf16[16,24,128]{2,1,0:T(8,128)(2,1)} %pad_maximum_fusion.2), calls=%async_computation.4 | async-start | bytes 196608 | tf_op jit(solution)/shard_map/all_to_all | solution.py:321
  104.3 1.3 collective-permute-start.1
  105.6 3.4 %collective-permute-done.1.head_ref = f32[3,256]{1,0:T(4,128)S(1)} collective-permute-done((f32[3,256]{1,0:T(4,128)S(1)}, f32[3,256]{1,0:T(4,128)S(1)}, u32[]{:S(2)}, u32[]{:S(2)}) %collective-permute-start.1) | collective-permute-done | bytes 3104 | tf_op jit(solution)/shard_map/ppermute | solution.py:313
  109.0 1.1 taps.1
  110.1 5.9 %all-to-all-done.4 = bf16[16,24,128]{2,1,0:T(8,128)(2,1)S(1)} async-done(((bf16[16,24,128]{2,1,0:T(8,128)(2,1)}), bf16[16,24,128]{2,1,0:T(8,128)(2,1)S(1)}, u32[]{:S(2)}, u32[]{:S(2)}) %all-to-all-start.4) | async-done | bytes 98336 | tf_op jit(solution)/shard_map/all_to_all | solution.py:321
  116.1 6.6 %all_to_all.38.tiles_ref = bf16[4,20,128]{2,1,0:T(8,128)(2,1)S(1)} all-to-all(bf16[4,20,128]{2,1,0:T(8,128)(2,1)S(1)} %broadcast_in_dim.40), channel_id=1, replica_groups=mesh['z'=16,'j'=8,'doc'=4] {'doc'}, dimensions={0} | all-to-all | bytes 40960 | tf_op jit(solution)/shard_map/all_to_all | solution.py:332
  122.7 0.1 reshape.79
  122.8 0.1 broadcast_in_dim.41
  122.9 16.5 %all_to_all.39.got_ref = bf16[8,136,256]{2,1,0:T(8,128)(2,1)S(1)} all-to-all(bf16[8,136,256]{2,1,0:T(8,128)(2,1)S(1)} %pad_maximum_fusion.1), channel_id=1, replica_groups=mesh['z'=16,'j'=8,'doc'=4] {'j'}, dimensions={0} | all-to-all | bytes 1114112 | tf_op jit(solution)/shard_map/all_to_all | solution.py:335
  139.4 0.9 unpack.1
  (21 shorter events, 0.3 us)
Async XLA Ops:
  0.6 22.7 %copy-start.4 = (bf16[1,128,2048]{2,1,0:T(8,128)(2,1)S(1)}, bf16[1,128,2048]{2,1,0:T(8,128)(2,1)}, u32[]{:S(2)}) copy-start(bf16[1,128,2048]{2,1,0:T(8,128)(2,1)} %param.9) | copy-start | bytes 1572868
  2.1 28.9 %all-to-all-start = ((bf16[16,32,256]{2,1,0:T(8,128)(2,1)}), bf16[16,32,256]{2,1,0:T(8,128)(2,1)S(1)}, u32[]{:S(2)}, u32[]{:S(2)}) async-start(bf16[16,32,256]{2,1,0:T(8,128)(2,1)} %broadcast_in_dim.34), calls=%async_computation | async-start | bytes 524288 | tf_op jit(solution)/shard_map/all_to_all | solution.py:268
  18.7 5.4 %collective-permute-start = (bf16[3,2048]{1,0:T(4,128)(2,1)S(1)}, bf16[3,2048]{1,0:T(4,128)(2,1)S(1)}, u32[]{:S(2)}, u32[]{:S(2)}) collective-permute-start(bf16[3,2048]{1,0:T(4,128)(2,1)S(1)} %slice_bitcast_fusion.1), channel_id=1, source_target_pairs={{0,32},{32,64},{64,96},{96,128},{128,160},{160,192},{192,224},{224... | collective-permute-start | bytes 36872 | tf_op jit(solution)/shard_map/ppermute | solution.py:269
  31.1 29.9 %copy-start = (f32[4,2048]{1,0:T(4,128)S(1)}, f32[4,2048]{1,0:T(4,128)}, u32[]{:S(2)}) copy-start(f32[4,2048]{1,0:T(4,128)} %taps_ref.3) | copy-start | bytes 98308
  31.1 29.9 %copy-start.1 = (f32[2048]{0:T(1024)S(1)}, f32[2048]{0:T(1024)}, u32[]{:S(2)}) copy-start(f32[2048]{0:T(1024)} %param.15) | copy-start | bytes 24580
  31.1 29.9 %copy-start.2 = (f32[2,2048]{1,0:T(2,128)S(1)}, f32[2,2048]{1,0:T(2,128)}, u32[]{:S(2)}) copy-start(f32[2,2048]{1,0:T(2,128)} %bias_ref.1) | copy-start | bytes 49156
  31.2 29.9 %copy-start.3 = (f32[2048]{0:T(1024)S(1)}, f32[2048]{0:T(1024)}, u32[]{:S(2)}) copy-start(f32[2048]{0:T(1024)} %param.14) | copy-start | bytes 24580
  100.7 15.3 %all-to-all-start.4 = ((bf16[16,24,128]{2,1,0:T(8,128)(2,1)}), bf16[16,24,128]{2,1,0:T(8,128)(2,1)S(1)}, u32[]{:S(2)}, u32[]{:S(2)}) async-start(bf16[16,24,128]{2,1,0:T(8,128)(2,1)} %pad_maximum_fusion.2), calls=%async_computation.4 | async-start | bytes 196608 | tf_op jit(solution)/shard_map/all_to_all | solution.py:321
  104.3 4.7 %collective-permute-start.1 = (f32[3,256]{1,0:T(4,128)S(1)}, f32[3,256]{1,0:T(4,128)S(1)}, u32[]{:S(2)}, u32[]{:S(2)}) collective-permute-start(f32[3,256]{1,0:T(4,128)S(1)} %bitcast.44), channel_id=1, source_target_pairs={{32,0},{64,32},{96,64},{128,96},{160,128},{192,160},{224,192},{256... | collective-permute-start | bytes 9224 | tf_op jit(solution)/shard_map/ppermute | solution.py:313
